TPU v7x, 128 devices: a whole 4x4x4 slice. The times are simulated.
128 devices in a mesh: pool: 4 (over x), section: 4 (over y_hi, core), tp: 8 (over z, y_lo).
Axes of the slice: x: 4, y: 4 (y_hi: 2, y_lo: 2; y = y_hi * 2 + y_lo), z: 4, core: 2. Of those that a mesh axis runs over, the one named last changes fastest.
Arguments:
- frames: bfloat16 [4, 4, 256, 1280], P('pool', 'section'), may hold values from -6 to 6
- ln_gain: bfloat16 [1280], replicated, may hold values from 0.25 to 1.75
- ln_bias: bfloat16 [1280], replicated, may hold values from -4 to 4
- enc_up: bfloat16 [1280, 5120], P(None, 'tp'), may hold values from -0.15625 to 0.15625
- up_bias: bfloat16 [5120], P('tp'), may hold values from -4 to 4
- enc_down: bfloat16 [5120, 1280], P('tp'), may hold values from -0.15625 to 0.15625
- down_bias: bfloat16 [1280], replicated, may hold values from -4 to 4
- adapt_in: bfloat16 [5120, 5120], P(None, ('section', 'tp')), may hold values from -0.078125 to 0.078125
- adapt_out: bfloat16 [5120, 5120], P(('section', 'tp')), may hold values from -0.078125 to 0.078125
- lengths: int32 [4, 4, 8], replicated, may hold values from 1 to 16, 64 in all within a row
- routes: int32 [4, 4, 8, 1], replicated, may hold values from 0 to 3; in each aligned block of 8 rows (0 to 7, 8 to 15, ..., all dimensions but the last counted through in order) at most 2 rows name the same one
- attn_gain: bfloat16 [4, 5120], P('section'), may hold values from 0.25 to 1.75
- q_weight: bfloat16 [4, 5120, 4096], P('section', None, 'tp'), may hold values from -1 to 1
- k_weight: bfloat16 [4, 5120, 1024], P('section', None, 'tp'), may hold values from -4 to 4
- v_weight: bfloat16 [4, 5120, 1024], P('section', None, 'tp'), may hold values from -0.078125 to 0.078125
- o_weight: bfloat16 [4, 4096, 5120], P('section', 'tp'), may hold values from -0.09375 to 0.09375
Outputs:
- decoded: float32 [4, 4, 128, 5120], P('pool', 'section', 'tp')
Inputs may be any that keep to these rules, and one draw needn't show every extreme that they name: Each encoder group's lengths sum to 64; the longest window of every group has exactly 16 tokens. `routes`: each encoder group's 8 windows name every prefill group exactly 2 times.
All inputs are finite; a program needn't handle non-finite values.
Results may differ from a plain program's by a relative error of at most 0.034.
Values may be sent and summed in bfloat16 or wider, within the bound.
No kernel may reach another device: no remote copies, remote signals or barrier semaphores. Data moves between devices by JAX's collectives and lax.ppermute only.
A program may use at most 128 MiB of HBM per device.

v0:
```python
import jax
import jax.numpy as jnp
from jax import lax
from jax.experimental import pallas as pl
from jax.experimental.pallas import tpu as pltpu
from jax.sharding import PartitionSpec as P

HD = 128
LANES = 128
WIN_MAX = 16
CAPW = 2
STACK = 4
EPSILON = 1e-05
BF = jnp.bfloat16
F32 = jnp.float32


def slot_tables(route_row, length_row, dest_count, capacity):
    windows = route_row.shape[0]
    window_ids = jnp.arange(windows, dtype=jnp.int32)
    starts = jnp.cumsum(length_row, dtype=jnp.int32) - length_row
    earlier = (route_row[None, :] == route_row[:, None]) & (
        window_ids[None, :] < window_ids[:, None]
    )
    window_rank = jnp.sum(earlier.astype(jnp.int32), axis=1, dtype=jnp.int32)
    dest_ids = jnp.arange(dest_count, dtype=jnp.int32)
    rank_ids = jnp.arange(capacity, dtype=jnp.int32)
    chosen = (route_row[None, None, :] == dest_ids[:, None, None]) & (
        window_rank[None, None, :] == rank_ids[None, :, None]
    )
    chosen = chosen.astype(jnp.int32)
    return (
        jnp.sum(chosen * starts, axis=2, dtype=jnp.int32),
        jnp.sum(chosen * length_row, axis=2, dtype=jnp.int32),
    )


def dot(a, b):
    return jnp.dot(a, b, preferred_element_type=F32)

def exact_gelu(x):
    return 0.5 * x * (1.0 + lax.erf(x * (0.5**0.5)))


def vmem():
    return pl.BlockSpec(memory_space=pltpu.VMEM)


def anywhere():
    return pl.BlockSpec(memory_space=pl.ANY)


def smem():
    return pl.BlockSpec(memory_space=pltpu.SMEM)


def encoder_kernel(
    frames_ref, gain_ref, bias_ref, up_ref, up_bias_ref, down_ref, out_ref, up_v, down_v, rows, sems
):
    copies = [
        pltpu.make_async_copy(up_ref, up_v, sems.at[0]),
        pltpu.make_async_copy(down_ref, down_v, sems.at[1]),
    ]
    for copy in copies:
        copy.start()
    values = frames_ref[...].astype(F32)
    centered = values - jnp.mean(values, axis=-1, keepdims=True)
    variance = jnp.mean(centered * centered, axis=-1, keepdims=True)
    normed = (
        centered * lax.rsqrt(variance + EPSILON) * gain_ref[...].astype(F32)
        + bias_ref[...].astype(F32)
    ).astype(BF)
    copies[0].wait()
    raised = dot(normed, up_v[...]) + up_bias_ref[...].astype(F32)
    active = exact_gelu(raised).astype(BF)
    copies[1].wait()
    lowered = dot(active, down_v[...])
    group, count = out_ref.shape[0], out_ref.shape[1]
    for c in range(rows.shape[0]):
        cols = slice(c * LANES, (c + 1) * LANES)
        rows[c] = lowered[:, cols]
        for j in range(group):
            out_ref[j, :, cols] = rows[c, pl.ds(j, count, stride=group), :].astype(BF)


def encoder(frames, gain, bias, up, up_bias, down):
    count, width = frames.shape
    hidden = up.shape[1]
    return pl.pallas_call(
        encoder_kernel,
        out_shape=jax.ShapeDtypeStruct((STACK, count // STACK, width), BF),
        in_specs=[vmem(), vmem(), vmem(), anywhere(), vmem(), anywhere()],
        out_specs=vmem(),
        scratch_shapes=[
            pltpu.VMEM((width, hidden), BF),
            pltpu.VMEM((hidden, width), BF),
            pltpu.VMEM((width // LANES, count, LANES), F32),
            pltpu.SemaphoreType.DMA((2,)),
        ],
        compiler_params=pltpu.CompilerParams(vmem_limit_bytes=32 << 20),
        cost_estimate=pl.CostEstimate(
            flops=4 * count * width * hidden,
            bytes_accessed=4 * width * hidden,
            transcendentals=count * hidden,
        ),
        name="encoder_units",
    )(frames, gain.reshape(1, -1), bias.reshape(1, -1), up, up_bias.reshape(1, -1), down)


def adapter_kernel(x_ref, in0, in1, out0, out1, part_ref, win, wout, sems):
    in_copies = [
        pltpu.make_async_copy(ref, win.at[i], sems.at[i]) for i, ref in enumerate((in0, in1))
    ]
    out_copies = [
        pltpu.make_async_copy(ref, wout.at[i], sems.at[2 + i])
        for i, ref in enumerate((out0, out1))
    ]
    for copy in in_copies + out_copies:
        copy.start()
    blocks, _, depth = x_ref.shape
    lifted = []
    for i in range(2):
        in_copies[i].wait()
        total = sum(
            dot(x_ref[b], win[i, b * depth : (b + 1) * depth, :]) for b in range(blocks)
        )
        lifted.append(exact_gelu(total).astype(BF))
    for copy in out_copies:
        copy.wait()
    for b in range(blocks):
        cols = slice(b * depth, (b + 1) * depth)
        part_ref[b] = sum(dot(lifted[i], wout[i, :, cols]) for i in range(2)).astype(BF)


def adapter(blocks, in_pair, out_pair):
    width, units = in_pair[0].shape
    rows = blocks.shape[1]
    return pl.pallas_call(
        adapter_kernel,
        out_shape=jax.ShapeDtypeStruct(blocks.shape, BF),
        in_specs=[vmem()] + [anywhere()] * 4,
        out_specs=vmem(),
        scratch_shapes=[
            pltpu.VMEM((2, width, units), BF),
            pltpu.VMEM((2, units, width), BF),
            pltpu.SemaphoreType.DMA((4,)),
        ],
        compiler_params=pltpu.CompilerParams(vmem_limit_bytes=40 << 20),
        cost_estimate=pl.CostEstimate(
            flops=8 * rows * width * units,
            bytes_accessed=8 * width * units,
            transcendentals=2 * rows * units,
        ),
        name="adapter_units",
    )(blocks, *in_pair, *out_pair)


def layer_kernel(
    which, x_ref, gain_ref, mask_ref, q0, k0, v0, o0, q1, k1, v1, o1, out_ref, wq, wk, wv, wo, sems
):
    blocks, rows, depth = x_ref.shape

    def copies(q_ref, k_ref, v_ref, o_ref):
        made = []
        for b in range(blocks):
            part = pl.ds(b * depth, depth)
            made.append(
                [
                    pltpu.make_async_copy(q_ref.at[part, :], wq.at[b], sems.at[0, b]),
                    pltpu.make_async_copy(k_ref.at[part, :], wk.at[b], sems.at[1, b]),
                    pltpu.make_async_copy(v_ref.at[part, :], wv.at[b], sems.at[2, b]),
                    pltpu.make_async_copy(o_ref.at[:, part], wo.at[b], sems.at[3, b]),
                ]
            )
        return made

    def begin(refs):
        made = copies(*refs)
        for group in made:
            for copy in group[:3]:
                copy.start()
        for group in made:
            group[3].start()

    @pl.when(which[0] == 0)
    def _():
        begin((q0, k0, v0, o0))

    @pl.when(which[0] != 0)
    def _():
        begin((q1, k1, v1, o1))

    waits = copies(q0, k0, v0, o0)
    squares = sum(
        jnp.sum(jnp.square(x_ref[b].astype(F32)), axis=-1, keepdims=True) for b in range(blocks)
    )
    scale = lax.rsqrt(squares / (blocks * depth) + EPSILON)
    queries, keys, values = 0.0, 0.0, 0.0
    for b in range(blocks):
        gain = gain_ref[:, b * depth : (b + 1) * depth].astype(F32)
        normed = (x_ref[b].astype(F32) * scale * gain).astype(BF)
        for copy in waits[b][:3]:
            copy.wait()
        queries += dot(normed, wq[b])
        keys += dot(normed, wk[b])
        values += dot(normed, wv[b])
    heads = queries.shape[1] // HD
    queries = queries.astype(BF)
    stacked = jnp.concatenate([queries[:, h * HD : (h + 1) * HD] for h in range(heads)], axis=0)
    scores = lax.dot_general(
        stacked, keys.astype(BF), (((1,), (1,)), ((), ())), preferred_element_type=F32
    ) * HD ** (-0.5)
    mask = jnp.concatenate([mask_ref[...]] * heads, axis=0)
    scores = jnp.where(mask > 0.5, scores, -1e30)
    exponent = jnp.exp(scores - jnp.max(scores, axis=-1, keepdims=True))
    probs = (exponent / jnp.sum(exponent, axis=-1, keepdims=True)).astype(BF)
    context = dot(probs, values.astype(BF)).astype(BF)
    context = jnp.concatenate([context[h * rows : (h + 1) * rows] for h in range(heads)], axis=1)
    for b in range(blocks):
        waits[b][3].wait()
        out_ref[b] = dot(context, wo[b]).astype(BF)


def decoder_layer(which, blocks, gain, mask, own, other):
    count, rows, depth = blocks.shape
    q_cols, kv_cols = own[0].shape[1], own[1].shape[1]
    weights = count * depth * (2 * q_cols + 2 * kv_cols)
    return pl.pallas_call(
        layer_kernel,
        out_shape=jax.ShapeDtypeStruct(blocks.shape, BF),
        in_specs=[smem(), vmem(), vmem(), vmem()] + [anywhere()] * 8,
        out_specs=vmem(),
        scratch_shapes=[
            pltpu.VMEM((count, depth, q_cols), BF),
            pltpu.VMEM((count, depth, kv_cols), BF),
            pltpu.VMEM((count, depth, kv_cols), BF),
            pltpu.VMEM((count, q_cols, depth), BF),
            pltpu.SemaphoreType.DMA((4, count)),
        ],
        compiler_params=pltpu.CompilerParams(vmem_limit_bytes=40 << 20),
        cost_estimate=pl.CostEstimate(
            flops=2 * rows * weights, bytes_accessed=2 * weights, transcendentals=rows * rows * 4
        ),
        name="decoder_layer",
    )(which, blocks, gain.reshape(1, -1), mask, *own, *other)


def per_device(
    frames,
    ln_gain,
    ln_bias,
    enc_up,
    up_bias,
    enc_down,
    down_bias,
    adapt_in,
    adapt_out,
    lengths,
    routes,
    attn_gain,
    q_weight,
    k_weight,
    v_weight,
    o_weight,
):
    pool_count = lax.axis_size("pool")
    tp_count = lax.axis_size("tp")
    section_count = lax.axis_size("section")
    z_count = tp_count // 2
    pool_index = lax.axis_index("pool")
    section_index = lax.axis_index("section")
    tp_index = lax.axis_index("tp")
    z_index, y_low = tp_index // 2, tp_index % 2
    core, high = section_index % 2, section_index // 2
    z_groups = [[2 * z + y for z in range(z_count)] for y in range(2)]

    def chip_swap(value):
        return lax.ppermute(value, "section", [(i, i ^ 1) for i in range(section_count)])

    def y_move(value, moves):
        pairs = []
        for high_from, high_to, y_flip in moves:
            for c in range(2):
                for t in range(tp_count):
                    pairs.append(
                        (
                            (2 * high_from + c) * tp_count + t,
                            (2 * high_to + c) * tp_count + (t ^ y_flip),
                        )
                    )
        return lax.ppermute(value, ("section", "tp"), pairs)

    def z_all_to_all(value):
        return lax.all_to_all(
            value, "tp", split_axis=0, concat_axis=0, tiled=True, axis_index_groups=z_groups
        )

    def z_sum(partial):
        return jnp.sum(z_all_to_all(partial).astype(F32), axis=0)

    def z_gather(shard):
        return z_all_to_all(jnp.broadcast_to(shard[None], (z_count,) + shard.shape))

    def at_first(value):
        return jnp.where(y_low == 0, value, jnp.zeros_like(value))

    both = ((0, 0, 1), (1, 1, 1))

    own_layer = (q_weight[0], k_weight[0], v_weight[0], o_weight[0])
    other_layer = tuple(chip_swap(weight) for weight in own_layer)
    own_gain, other_gain = attn_gain[0], chip_swap(attn_gain[0])
    in_pair = (adapt_in, chip_swap(adapt_in))
    out_pair = (adapt_out, chip_swap(adapt_out))

    width = frames.shape[3]
    tokens = frames.shape[2] // STACK
    partial_down = encoder(frames[0, 0], ln_gain, ln_bias, enc_up, up_bias, enc_down)
    own_frames = lax.dynamic_index_in_dim(
        frames[0, 0].reshape(tokens, STACK, width), z_index, 1, keepdims=False
    )
    extra = at_first(own_frames.astype(F32) + down_bias.astype(F32)[None])
    share = (z_sum(partial_down) + extra).astype(BF)
    here = share.astype(F32) + y_move(share, both).astype(F32)
    there = y_move(share, ((0, 1, 0), (1, 0, 0))).astype(F32) + y_move(
        share, ((0, 1, 1), (1, 0, 1))
    ).astype(F32)
    encoded = jnp.where(high == 0, jnp.stack([here, there]), jnp.stack([there, here]))
    encoded = encoded.astype(BF).reshape(2 * tokens, width)

    share = z_sum(adapter(z_gather(encoded), in_pair, out_pair)).astype(BF)
    moved = (
        y_move(share, both),
        y_move(share, ((1, 0, 0),)),
        y_move(share, ((1, 0, 1),)),
    )
    hidden = (share.astype(F32) + sum(part.astype(F32) for part in moved)).astype(BF)

    ends = jnp.cumsum(lengths[pool_index], axis=1, dtype=jnp.int32)
    token_ids = jnp.arange(tokens, dtype=jnp.int32)
    windows = jnp.sum(
        (ends[:, None, :] <= token_ids[None, :, None]).astype(jnp.int32), axis=2, dtype=jnp.int32
    )
    tags = windows + jnp.arange(section_count, dtype=jnp.int32)[:, None] * lengths.shape[2]
    tags = lax.dynamic_slice_in_dim(tags.reshape(2, 2, tokens), core, 1, 1).reshape(-1)
    row_ids = jnp.arange(2 * tokens, dtype=jnp.int32)
    allowed = (tags[:, None] == tags[None, :]) & (row_ids[None, :] <= row_ids[:, None])
    mask = allowed.astype(F32)

    tables = jax.vmap(
        jax.vmap(lambda route_row, length_row: slot_tables(route_row, length_row, pool_count, CAPW))
    )
    starts, spans = tables(routes[..., 0], lengths)
    offsets = jnp.arange(WIN_MAX, dtype=jnp.int32)

    def of_pair(table):
        pair = lax.dynamic_index_in_dim(table, pool_index, 0, keepdims=False)
        pair = pair.reshape((2, 2) + pair.shape[1:])
        pair = lax.dynamic_index_in_dim(pair, core, 1, keepdims=False)
        return jnp.transpose(pair, (0, 2, 1))

    row_valid = offsets < of_pair(spans)[..., None]
    row_index = of_pair(starts)[..., None] + offsets
    row_index = row_index + (jnp.arange(2, dtype=jnp.int32) * tokens)[:, None, None, None]
    row_index = jnp.where(row_valid, row_index, 0)

    for turn in range(4):
        which = (core != turn % 2).astype(jnp.int32)
        gain = jnp.where(which == 0, own_gain, other_gain)
        partial = decoder_layer(
            which.reshape(1), z_gather(hidden), gain, mask, own_layer, other_layer
        )
        share = (z_sum(partial) + at_first(hidden.astype(F32))).astype(BF)
        if turn == 1:
            moved = (y_move(share, ((0, 1, 0),)), y_move(share, ((0, 1, 1),)))
            hidden = sum(part.astype(F32) for part in moved).astype(BF)
        elif turn < 3:
            hidden = (share.astype(F32) + y_move(share, both).astype(F32)).astype(BF)

    picked = jnp.take(share, row_index.reshape(-1), axis=0)
    picked = jnp.where(row_valid.reshape(-1, 1), picked, jnp.zeros_like(picked))
    picked = picked.reshape(2, CAPW, pool_count, WIN_MAX, width)
    stay = lax.dynamic_index_in_dim(picked, y_low, 1, keepdims=False)
    leave = lax.dynamic_index_in_dim(picked, 1 - y_low, 1, keepdims=False)
    moved = (
        y_move(stay[0], ((1, 0, 0),)),
        y_move(leave[0], ((1, 0, 1),)),
        y_move(leave[1], ((1, 1, 1),)),
        jnp.where(high == 1, stay[1], jnp.zeros_like(stay[1])),
    )
    final = sum(part.astype(F32) for part in moved).astype(BF)
    landed = []
    for step in range(pool_count):
        pairs = []
        for x in range(pool_count):
            for z in range(z_count):
                for y in range(2):
                    pairs.append(
                        (
                            x * tp_count + 2 * z + y,
                            ((z + step) % pool_count) * tp_count + 2 * x + y,
                        )
                    )
        piece = lax.dynamic_index_in_dim(
            final, (z_index + step) % pool_count, 0, keepdims=False
        )
        landed.append(lax.ppermute(piece, ("pool", "tp"), pairs))
    landed = jnp.stack(landed)
    blocks = [
        lax.dynamic_index_in_dim(landed, (pool_index - z) % pool_count, 0, keepdims=False)
        for z in range(z_count)
    ]
    decoded = jnp.concatenate(blocks, axis=1).astype(F32)
    return decoded[None, None]


def solution(mesh):
    in_specs = (
        P("pool", "section", None, None),
        P(),
        P(),
        P(None, "tp"),
        P("tp"),
        P("tp", None),
        P(),
        P(None, ("section", "tp")),
        P(("section", "tp"), None),
        P(),
        P(),
        P("section", None),
        P("section", None, "tp"),
        P("section", None, "tp"),
        P("section", None, "tp"),
        P("section", "tp", None),
    )
    out_specs = P("pool", "section", "tp", None)
    return jax.shard_map(
        per_device, mesh=mesh, in_specs=in_specs, out_specs=out_specs, check_vma=False
    )
```

profile of v0, /device:TPU:30, one launch (start us, length us, event | category | flops | bytes accessed | tf_op | source)
XLA Modules:
  0.0 362.7 jit_solution(15342869480545586248)
XLA Ops:
  9.4 5.5 %all-to-all-start = ((bf16[4,64,1280]{2,1,0:T(8,128)(2,1)}), bf16[4,64,1280]{2,1,0:T(8,128)(2,1)S(1)}, u32[]{:S(2)}, u32[]{:S(2)}) async-start(bf16[4,64,1280]{2,1,0:T(8,128)(2,1)} %encoder_units.1), calls=%async_computation | async-start | bytes 1310720 | tf_op jit(solution)/shard_map/all_to_all | solution.py:294
  15.9 9.9 %all-to-all-done = bf16[4,64,1280]{2,1,0:T(8,128)(2,1)S(1)} async-done(((bf16[4,64,1280]{2,1,0:T(8,128)(2,1)}), bf16[4,64,1280]{2,1,0:T(8,128)(2,1)S(1)}, u32[]{:S(2)}, u32[]{:S(2)}) %all-to-all-start) | async-done | bytes 655392 | tf_op jit(solution)/shard_map/all_to_all | solution.py:294
  27.7 5.2 %collective-permute-done = bf16[64,1280]{1,0:T(8,128)(2,1)S(1)} collective-permute-done((bf16[64,1280]{1,0:T(8,128)(2,1)S(1)}, bf16[64,1280]{1,0:T(8,128)(2,1)S(1)}, u32[]{:S(2)}, u32[]{:S(2)}) %collective-permute-start) | collective-permute-done | bytes 163872 | tf_op jit(solution)/shard_map/ppermute | solution.py:291
  34.9 4.5 %collective-permute-done.2 = bf16[64,1280]{1,0:T(8,128)(2,1)S(1)} collective-permute-done((bf16[64,1280]{1,0:T(8,128)(2,1)S(1)}, bf16[64,1280]{1,0:T(8,128)(2,1)S(1)}, u32[]{:S(2)}, u32[]{:S(2)}) %collective-permute-start.2) | collective-permute-done | bytes 163872 | tf_op jit(solution)/shard_map/ppermute | solution.py:291
  40.7 4.3 %all-to-all-start.1 = ((bf16[4,128,1280]{2,1,0:T(8,128)(2,1)}), bf16[4,128,1280]{2,1,0:T(8,128)(2,1)}, u32[]{:S(2)}, u32[]{:S(2)}) async-start(bf16[4,128,1280]{2,1,0:T(8,128)(2,1)} %broadcast_in_dim.38), calls=%async_computation.1 | async-start | bytes 2621440 | tf_op jit(solution)/shard_map/all_to_all | solution.py:294
  48.0 4.0 %copy.24.in1 = bf16[5120,160]{1,0:T(8,128)(2,1)} copy(bf16[5120,160]{0,1:T(8,128)(2,1)} %collective-permute-done.3) | data formatting | bytes 3276800 | tf_op jit(solution)/shard_map/ppermute | solution.py:278
  52.0 8.4 %all-to-all-done.1.x_ref = bf16[4,128,1280]{2,1,0:T(8,128)(2,1)} async-done(((bf16[4,128,1280]{2,1,0:T(8,128)(2,1)}), bf16[4,128,1280]{2,1,0:T(8,128)(2,1)}, u32[]{:S(2)}, u32[]{:S(2)}) %all-to-all-start.1) | async-done | bytes 1310752 | tf_op jit(solution)/shard_map/all_to_all | solution.py:294
  62.1 4.5 %adapter_units.1 = bf16[4,128,1280]{2,1,0:T(8,128)(2,1)S(1)} custom-call(bf16[4,128,1280]{2,1,0:T(8,128)(2,1)} %all-to-all-done.1.x_ref, bf16[5120,160]{1,0:T(8,128)(2,1)S(1)} %copy.23.in0, bf16[5120,160]{1,0:T(8,128)(2,1)S(1)} %copy-done.5, bf16[160,5120]{1,0:T(8,128)(2,1)} %out0.1, bf16[160,5120]{1,0:T(8,128)(2,1)} %collective-permute-done.4.out1), custom_call_target="tpu_custom_call" | custom-call | flops 838860800 | bytes 6553600 | tf_op jit(solution)/shard_map/adapter_units/pallas_call | solution.py:138
  66.6 17.4 %all_to_all.55 = bf16[4,128,1280]{2,1,0:T(8,128)(2,1)} all-to-all(bf16[4,128,1280]{2,1,0:T(8,128)(2,1)S(1)} %adapter_units.1), channel_id=1, replica_groups={{0,2,4,6},{1,3,5,7},{8,10,12,14},{9,11,13,15},{16,18,20,22},{17,19,21,2..., dimensions={0} | all-to-all | bytes 2621440 | tf_op jit(solution)/shard_map/all_to_all | solution.py:294
  89.3 7.0 %collective-permute-start.6 = (bf16[128,1280]{1,0:T(8,128)(2,1)S(1)}, bf16[128,1280]{1,0:T(8,128)(2,1)}, u32[]{:S(2)}, u32[]{:S(2)}) collective-permute-start(bf16[128,1280]{1,0:T(8,128)(2,1)S(1)} %reduce_sum.99), channel_id=1, source_target_pairs={{16,0},{17,1},{18,2},{19,3},{20,4},{21,5},{22,6},{23,7},{24,8},{25... | collective-permute-start | bytes 983048 | tf_op jit(solution)/shard_map/ppermute | solution.py:291
  100.9 6.4 %collective-permute-done.7 = bf16[128,1280]{1,0:T(8,128)(2,1)} collective-permute-done((bf16[128,1280]{1,0:T(8,128)(2,1)S(1)}, bf16[128,1280]{1,0:T(8,128)(2,1)}, u32[]{:S(2)}, u32[]{:S(2)}) %collective-permute-start.7) | collective-permute-done | bytes 327712 | tf_op jit(solution)/shard_map/ppermute | solution.py:291
  109.8 4.4 %all-to-all-start.3 = ((bf16[4,128,1280]{2,1,0:T(8,128)(2,1)}), bf16[4,128,1280]{2,1,0:T(8,128)(2,1)}, u32[]{:S(2)}, u32[]{:S(2)}) async-start(bf16[4,128,1280]{2,1,0:T(8,128)(2,1)} %broadcast_in_dim.39), calls=%async_computation.3 | async-start | bytes 2621440 | tf_op jit(solution)/shard_map/all_to_all | solution.py:294
  115.0 18.2 %all-to-all-done.3.x_ref = bf16[4,128,1280]{2,1,0:T(8,128)(2,1)} async-done(((bf16[4,128,1280]{2,1,0:T(8,128)(2,1)}), bf16[4,128,1280]{2,1,0:T(8,128)(2,1)}, u32[]{:S(2)}, u32[]{:S(2)}) %all-to-all-start.3) | async-done | bytes 1310752 | tf_op jit(solution)/shard_map/all_to_all | solution.py:294
  135.7 7.5 %decoder_layer.4 = bf16[4,128,1280]{2,1,0:T(8,128)(2,1)S(1)} custom-call(s32[1]{0:T(128)} %bitcast.8.which, bf16[4,128,1280]{2,1,0:T(8,128)(2,1)} %all-to-all-done.3.x_ref, bf16[1,5120]{1,0:T(2,128)(2,1)S(1)} %reshape.288.gain_ref, f32[128,128]{1,0:T(8,128)S(1)} %fusion.9.mask_ref, bf16[5120,512]{1,0:T(8,128)(2,1)S(1)} %bitcast.70, ...), custom_call_target="tpu_custom_call" | custom-call | flops 1677721600 | bytes 13107200 | tf_op jit(solution)/shard_map/decoder_layer/pallas_call | solution.py:228
  143.2 20.6 %all_to_all.56 = bf16[4,128,1280]{2,1,0:T(8,128)(2,1)S(1)} all-to-all(bf16[4,128,1280]{2,1,0:T(8,128)(2,1)S(1)} %decoder_layer.4), channel_id=1, replica_groups={{0,2,4,6},{1,3,5,7},{8,10,12,14},{9,11,13,15},{16,18,20,22},{17,19,21,2..., dimensions={0} | all-to-all | bytes 2621440 | tf_op jit(solution)/shard_map/all_to_all | solution.py:294
  165.1 7.2 %collective-permute-done.13 = bf16[128,1280]{1,0:T(8,128)(2,1)S(1)} collective-permute-done((bf16[128,1280]{1,0:T(8,128)(2,1)S(1)}, bf16[128,1280]{1,0:T(8,128)(2,1)S(1)}, u32[]{:S(2)}, u32[]{:S(2)}) %collective-permute-start.13) | collective-permute-done | bytes 327712 | tf_op jit(solution)/shard_map/ppermute | solution.py:291
  173.6 4.3 %all-to-all-start.5 = ((bf16[4,128,1280]{2,1,0:T(8,128)(2,1)}), bf16[4,128,1280]{2,1,0:T(8,128)(2,1)}, u32[]{:S(2)}, u32[]{:S(2)}) async-start(bf16[4,128,1280]{2,1,0:T(8,128)(2,1)} %broadcast_in_dim.40), calls=%async_computation.5 | async-start | bytes 2621440 | tf_op jit(solution)/shard_map/all_to_all | solution.py:294
  177.9 16.1 %all-to-all-done.5.x_ref = bf16[4,128,1280]{2,1,0:T(8,128)(2,1)} async-done(((bf16[4,128,1280]{2,1,0:T(8,128)(2,1)}), bf16[4,128,1280]{2,1,0:T(8,128)(2,1)}, u32[]{:S(2)}, u32[]{:S(2)}) %all-to-all-start.5) | async-done | bytes 1310752 | tf_op jit(solution)/shard_map/all_to_all | solution.py:294
  196.5 7.6 %decoder_layer.5 = bf16[4,128,1280]{2,1,0:T(8,128)(2,1)S(1)} custom-call(s32[1]{0:T(128)} %bitcast.7.which, bf16[4,128,1280]{2,1,0:T(8,128)(2,1)} %all-to-all-done.5.x_ref, bf16[1,5120]{1,0:T(2,128)(2,1)S(1)} %reshape.289.gain_ref, f32[128,128]{1,0:T(8,128)S(1)} %fusion.9.mask_ref, bf16[5120,512]{1,0:T(8,128)(2,1)S(1)} %bitcast.71, ...), custom_call_target="tpu_custom_call" | custom-call | flops 1677721600 | bytes 13107200 | tf_op jit(solution)/shard_map/decoder_layer/pallas_call | solution.py:228
  204.0 17.3 %all_to_all.57 = bf16[4,128,1280]{2,1,0:T(8,128)(2,1)S(1)} all-to-all(bf16[4,128,1280]{2,1,0:T(8,128)(2,1)S(1)} %decoder_layer.5), channel_id=1, replica_groups={{0,2,4,6},{1,3,5,7},{8,10,12,14},{9,11,13,15},{16,18,20,22},{17,19,21,2..., dimensions={0} | all-to-all | bytes 2621440 | tf_op jit(solution)/shard_map/all_to_all | solution.py:294
  224.2 8.0 %collective-permute-done.14 = bf16[128,1280]{1,0:T(8,128)(2,1)S(1)} collective-permute-done((bf16[128,1280]{1,0:T(8,128)(2,1)S(1)}, bf16[128,1280]{1,0:T(8,128)(2,1)S(1)}, u32[]{:S(2)}, u32[]{:S(2)}) %collective-permute-start.14) | collective-permute-done | bytes 327712 | tf_op jit(solution)/shard_map/ppermute | solution.py:291
  232.2 5.1 %collective-permute-done.15 = bf16[128,1280]{1,0:T(8,128)(2,1)S(1)} collective-permute-done((bf16[128,1280]{1,0:T(8,128)(2,1)S(1)}, bf16[128,1280]{1,0:T(8,128)(2,1)S(1)}, u32[]{:S(2)}, u32[]{:S(2)}) %collective-permute-start.15) | collective-permute-done | bytes 327712 | tf_op jit(solution)/shard_map/ppermute | solution.py:291
  237.4 18.9 %all_to_all.58.x_ref = bf16[4,128,1280]{2,1,0:T(8,128)(2,1)S(1)} all-to-all(bf16[4,128,1280]{2,1,0:T(8,128)(2,1)S(1)} %broadcast_in_dim.41), channel_id=1, replica_groups={{0,2,4,6},{1,3,5,7},{8,10,12,14},{9,11,13,15},{16,18,20,22},{17,19,21,2..., dimensions={0} | all-to-all | bytes 2621440 | tf_op jit(solution)/shard_map/all_to_all | solution.py:294
  256.3 6.2 %decoder_layer.6 = bf16[4,128,1280]{2,1,0:T(8,128)(2,1)S(1)} custom-call(s32[1]{0:T(128)} %bitcast.8.which, bf16[4,128,1280]{2,1,0:T(8,128)(2,1)S(1)} %all_to_all.58.x_ref, bf16[1,5120]{1,0:T(2,128)(2,1)S(1)} %reshape.288.gain_ref, f32[128,128]{1,0:T(8,128)S(1)} %fusion.9.mask_ref, bf16[5120,512]{1,0:T(8,128)(2,1)S(1)} %bitcast.72, ...), custom_call_target="tpu_custom_call" | custom-call | flops 1677721600 | bytes 13107200 | tf_op jit(solution)/shard_map/decoder_layer/pallas_call | solution.py:228
  262.6 17.9 %all_to_all.59 = bf16[4,128,1280]{2,1,0:T(8,128)(2,1)S(1)} all-to-all(bf16[4,128,1280]{2,1,0:T(8,128)(2,1)S(1)} %decoder_layer.6), channel_id=1, replica_groups={{0,2,4,6},{1,3,5,7},{8,10,12,14},{9,11,13,15},{16,18,20,22},{17,19,21,2..., dimensions={0} | all-to-all | bytes 2621440 | tf_op jit(solution)/shard_map/all_to_all | solution.py:294
  282.6 5.5 %collective-permute-done.16 = bf16[128,1280]{1,0:T(8,128)(2,1)} collective-permute-done((bf16[128,1280]{1,0:T(8,128)(2,1)S(1)}, bf16[128,1280]{1,0:T(8,128)(2,1)}, u32[]{:S(2)}, u32[]{:S(2)}) %collective-permute-start.16) | collective-permute-done | bytes 327712 | tf_op jit(solution)/shard_map/ppermute | solution.py:291
  290.3 4.4 %all-to-all-start.9 = ((bf16[4,128,1280]{2,1,0:T(8,128)(2,1)}), bf16[4,128,1280]{2,1,0:T(8,128)(2,1)}, u32[]{:S(2)}, u32[]{:S(2)}) async-start(bf16[4,128,1280]{2,1,0:T(8,128)(2,1)} %broadcast_in_dim.42), calls=%async_computation.9 | async-start | bytes 2621440 | tf_op jit(solution)/shard_map/all_to_all | solution.py:294
  296.5 11.5 %all-to-all-done.9.x_ref = bf16[4,128,1280]{2,1,0:T(8,128)(2,1)} async-done(((bf16[4,128,1280]{2,1,0:T(8,128)(2,1)}), bf16[4,128,1280]{2,1,0:T(8,128)(2,1)}, u32[]{:S(2)}, u32[]{:S(2)}) %all-to-all-start.9) | async-done | bytes 1310752 | tf_op jit(solution)/shard_map/all_to_all | solution.py:294
  310.4 7.6 %decoder_layer.7 = bf16[4,128,1280]{2,1,0:T(8,128)(2,1)S(1)} custom-call(s32[1]{0:T(128)} %bitcast.7.which, bf16[4,128,1280]{2,1,0:T(8,128)(2,1)} %all-to-all-done.9.x_ref, bf16[1,5120]{1,0:T(2,128)(2,1)S(1)} %reshape.289.gain_ref, f32[128,128]{1,0:T(8,128)S(1)} %fusion.9.mask_ref, bf16[5120,512]{1,0:T(8,128)(2,1)S(1)} %bitcast.73, ...), custom_call_target="tpu_custom_call" | custom-call | flops 1677721600 | bytes 13107200 | tf_op jit(solution)/shard_map/decoder_layer/pallas_call | solution.py:228
  322.9 12.0 %all-to-all-done.10 = bf16[4,128,1280]{2,1,0:T(8,128)(2,1)S(1)} async-done(((bf16[4,128,1280]{2,1,0:T(8,128)(2,1)}), bf16[4,128,1280]{2,1,0:T(8,128)(2,1)S(1)}, u32[]{:S(2)}, u32[]{:S(2)}) %all-to-all-start.10) | async-done | bytes 1310752 | tf_op jit(solution)/shard_map/all_to_all | solution.py:294
  343.3 4.4 %collective-permute-done.19 = bf16[4,16,1280]{2,1,0:T(8,128)(2,1)S(1)} collective-permute-done((bf16[4,16,1280]{2,1,0:T(8,128)(2,1)S(1)}, bf16[4,16,1280]{2,1,0:T(8,128)(2,1)S(1)}, u32[]{:S(2)}, u32[]{:S(2)}) %collective-permute-start.19) | collective-permute-done | bytes 163872 | tf_op jit(solution)/shard_map/ppermute | solution.py:291
  350.8 4.7 %collective-permute-start.21 = (bf16[16,1280]{1,0:T(8,128)(2,1)S(1)}, bf16[16,1280]{1,0:T(8,128)(2,1)S(1)}, u32[]{:S(2)}, u32[]{:S(2)}) collective-permute-start(bf16[16,1280]{1,0:T(8,128)(2,1)S(1)} %get-tuple-element.17), channel_id=1, source_target_pairs={{0,32},{1,33},{2,64},{3,65},{4,96},{5,97},{6,0},{7,1},{32,34},{33,... | collective-permute-start | bytes 122888 | tf_op jit(solution)/shard_map/ppermute | solution.py:406
  (138 shorter events, 75.9 us)
Async XLA Ops:
  9.4 16.3 %all-to-all-start = ((bf16[4,64,1280]{2,1,0:T(8,128)(2,1)}), bf16[4,64,1280]{2,1,0:T(8,128)(2,1)S(1)}, u32[]{:S(2)}, u32[]{:S(2)}) async-start(bf16[4,64,1280]{2,1,0:T(8,128)(2,1)} %encoder_units.1), calls=%async_computation | async-start | bytes 1310720 | tf_op jit(solution)/shard_map/all_to_all | solution.py:294
  14.9 118.3 %collective-permute-start.12 = (bf16[512,5120]{1,0:T(8,128)(2,1)}, bf16[512,5120]{1,0:T(8,128)(2,1)}, u32[]{:S(2)}, u32[]{:S(2)}) collective-permute-start(bf16[512,5120]{1,0:T(8,128)(2,1)} %bitcast.85), channel_id=1, source_target_pairs={{0,8},{8,0},{16,24},{24,16},{1,9},{9,1},{17,25},{25,17},{2,10},{10... | collective-permute-start | bytes 15728648 | tf_op jit(solution)/shard_map/ppermute | solution.py:278
  14.9 118.3 %collective-permute-start.9 = (bf16[5120,512]{1,0:T(8,128)(2,1)}, bf16[5120,512]{1,0:T(8,128)(2,1)}, u32[]{:S(2)}, u32[]{:S(2)}) collective-permute-start(bf16[5120,512]{1,0:T(8,128)(2,1)} %bitcast.69), channel_id=1, source_target_pairs={{0,8},{8,0},{16,24},{24,16},{1,9},{9,1},{17,25},{25,17},{2,10},{10... | collective-permute-start | bytes 15728648 | tf_op jit(solution)/shard_map/ppermute | solution.py:278
  25.9 7.0 %collective-permute-start = (bf16[64,1280]{1,0:T(8,128)(2,1)S(1)}, bf16[64,1280]{1,0:T(8,128)(2,1)S(1)}, u32[]{:S(2)}, u32[]{:S(2)}) collective-permute-start(bf16[64,1280]{1,0:T(8,128)(2,1)S(1)} %fusion.3), channel_id=1, source_target_pairs={{0,1},{1,0},{2,3},{3,2},{4,5},{5,4},{6,7},{7,6},{8,9},{9,8},{10,11... | collective-permute-start | bytes 491528 | tf_op jit(solution)/shard_map/ppermute | solution.py:291
  26.7 21.3 %collective-permute-start.3 = (bf16[5120,160]{0,1:T(8,128)(2,1)}, bf16[5120,160]{0,1:T(8,128)(2,1)}, u32[]{:S(2)}, u32[]{:S(2)}) collective-permute-start(bf16[5120,160]{0,1:T(8,128)(2,1)} %param.23), channel_id=1, source_target_pairs={{0,8},{8,0},{16,24},{24,16},{1,9},{9,1},{17,25},{25,17},{2,10},{10... | collective-permute-start | bytes 4915208 | tf_op jit(solution)/shard_map/ppermute | solution.py:278
  26.7 8.2 %collective-permute-start.1 = (bf16[64,1280]{1,0:T(8,128)(2,1)S(1)}, bf16[64,1280]{1,0:T(8,128)(2,1)S(1)}, u32[]{:S(2)}, u32[]{:S(2)}) collective-permute-start(bf16[64,1280]{1,0:T(8,128)(2,1)S(1)} %fusion.3), channel_id=1, source_target_pairs={{0,16},{1,17},{2,18},{3,19},{4,20},{5,21},{6,22},{7,23},{8,24},{9,... | collective-permute-start | bytes 491528 | tf_op jit(solution)/shard_map/ppermute | solution.py:291
  32.9 6.5 %collective-permute-start.2 = (bf16[64,1280]{1,0:T(8,128)(2,1)S(1)}, bf16[64,1280]{1,0:T(8,128)(2,1)S(1)}, u32[]{:S(2)}, u32[]{:S(2)}) collective-permute-start(bf16[64,1280]{1,0:T(8,128)(2,1)S(1)} %fusion.3), channel_id=1, source_target_pairs={{0,17},{1,16},{2,19},{3,18},{4,21},{5,20},{6,23},{7,22},{8,25},{9,... | collective-permute-start | bytes 491528 | tf_op jit(solution)/shard_map/ppermute | solution.py:291
  34.9 25.5 %collective-permute-start.4 = (bf16[160,5120]{1,0:T(8,128)(2,1)}, bf16[160,5120]{1,0:T(8,128)(2,1)}, u32[]{:S(2)}, u32[]{:S(2)}) collective-permute-start(bf16[160,5120]{1,0:T(8,128)(2,1)} %out0.1), channel_id=1, source_target_pairs={{0,8},{8,0},{16,24},{24,16},{1,9},{9,1},{17,25},{25,17},{2,10},{10... | collective-permute-start | bytes 4915208 | tf_op jit(solution)/shard_map/ppermute | solution.py:278
  40.7 19.7 %all-to-all-start.1 = ((bf16[4,128,1280]{2,1,0:T(8,128)(2,1)}), bf16[4,128,1280]{2,1,0:T(8,128)(2,1)}, u32[]{:S(2)}, u32[]{:S(2)}) async-start(bf16[4,128,1280]{2,1,0:T(8,128)(2,1)} %broadcast_in_dim.38), calls=%async_computation.1 | async-start | bytes 2621440 | tf_op jit(solution)/shard_map/all_to_all | solution.py:294
  66.6 40.7 %copy-start.4 = (bf16[1,5120,128]{2,1,0:T(8,128)(2,1)S(1)}, bf16[1,5120,128]{2,1,0:T(8,128)(2,1)}, u32[]{:S(2)}) copy-start(bf16[1,5120,128]{2,1,0:T(8,128)(2,1)} %param.30) | copy-start | bytes 3932164
  84.1 16.9 %copy-start.3 = (bf16[1,5120,128]{2,1,0:T(8,128)(2,1)S(1)}, bf16[1,5120,128]{2,1,0:T(8,128)(2,1)}, u32[]{:S(2)}) copy-start(bf16[1,5120,128]{2,1,0:T(8,128)(2,1)} %param.29) | copy-start | bytes 3932164
  85.7 12.6 %collective-permute-start.5 = (bf16[128,1280]{1,0:T(8,128)(2,1)S(1)}, bf16[128,1280]{1,0:T(8,128)(2,1)S(1)}, u32[]{:S(2)}, u32[]{:S(2)}) collective-permute-start(bf16[128,1280]{1,0:T(8,128)(2,1)S(1)} %reduce_sum.99), channel_id=1, source_target_pairs={{0,1},{1,0},{2,3},{3,2},{4,5},{5,4},{6,7},{7,6},{8,9},{9,8},{10,11... | collective-permute-start | bytes 983048 | tf_op jit(solution)/shard_map/ppermute | solution.py:291
  89.3 11.7 %collective-permute-start.6 = (bf16[128,1280]{1,0:T(8,128)(2,1)S(1)}, bf16[128,1280]{1,0:T(8,128)(2,1)}, u32[]{:S(2)}, u32[]{:S(2)}) collective-permute-start(bf16[128,1280]{1,0:T(8,128)(2,1)S(1)} %reduce_sum.99), channel_id=1, source_target_pairs={{16,0},{17,1},{18,2},{19,3},{20,4},{21,5},{22,6},{23,7},{24,8},{25... | collective-permute-start | bytes 983048 | tf_op jit(solution)/shard_map/ppermute | solution.py:291
  96.2 11.1 %collective-permute-start.7 = (bf16[128,1280]{1,0:T(8,128)(2,1)S(1)}, bf16[128,1280]{1,0:T(8,128)(2,1)}, u32[]{:S(2)}, u32[]{:S(2)}) collective-permute-start(bf16[128,1280]{1,0:T(8,128)(2,1)S(1)} %reduce_sum.99), channel_id=1, source_target_pairs={{16,1},{17,0},{18,3},{19,2},{20,5},{21,4},{22,7},{23,6},{24,9},{25... | collective-permute-start | bytes 983048 | tf_op jit(solution)/shard_map/ppermute | solution.py:291
  98.3 16.6 %collective-permute-start.8 = (bf16[5120]{0:T(1024)(128)(2,1)S(1)}, bf16[5120]{0:T(1024)(128)(2,1)S(1)}, u32[]{:S(2)}, u32[]{:S(2)}) collective-permute-start(bf16[5120]{0:T(1024)(128)(2,1)S(1)} %reduce.1), channel_id=1, source_target_pairs={{0,8},{8,0},{16,24},{24,16},{1,9},{9,1},{17,25},{25,17},{2,10},{10... | collective-permute-start | bytes 30728 | tf_op jit(solution)/shard_map/ppermute | solution.py:278
  100.9 14.1 %collective-permute-start.10 = (bf16[5120,128]{1,0:T(8,128)(2,1)S(1)}, bf16[5120,128]{1,0:T(8,128)(2,1)}, u32[]{:S(2)}, u32[]{:S(2)}) collective-permute-start(bf16[5120,128]{1,0:T(8,128)(2,1)S(1)} %bitcast.74), channel_id=1, source_target_pairs={{0,8},{8,0},{16,24},{24,16},{1,9},{9,1},{17,25},{25,17},{2,10},{10... | collective-permute-start | bytes 3932168 | tf_op jit(solution)/shard_map/ppermute | solution.py:278
  107.3 7.7 %collective-permute-start.11 = (bf16[5120,128]{1,0:T(8,128)(2,1)S(1)}, bf16[5120,128]{1,0:T(8,128)(2,1)}, u32[]{:S(2)}, u32[]{:S(2)}) collective-permute-start(bf16[5120,128]{1,0:T(8,128)(2,1)S(1)} %bitcast.79), channel_id=1, source_target_pairs={{0,8},{8,0},{16,24},{24,16},{1,9},{9,1},{17,25},{25,17},{2,10},{10... | collective-permute-start | bytes 3932168 | tf_op jit(solution)/shard_map/ppermute | solution.py:278
  109.8 23.4 %all-to-all-start.3 = ((bf16[4,128,1280]{2,1,0:T(8,128)(2,1)}), bf16[4,128,1280]{2,1,0:T(8,128)(2,1)}, u32[]{:S(2)}, u32[]{:S(2)}) async-start(bf16[4,128,1280]{2,1,0:T(8,128)(2,1)} %broadcast_in_dim.39), calls=%async_computation.3 | async-start | bytes 2621440 | tf_op jit(solution)/shard_map/all_to_all | solution.py:294
  164.0 8.3 %collective-permute-start.13 = (bf16[128,1280]{1,0:T(8,128)(2,1)S(1)}, bf16[128,1280]{1,0:T(8,128)(2,1)S(1)}, u32[]{:S(2)}, u32[]{:S(2)}) collective-permute-start(bf16[128,1280]{1,0:T(8,128)(2,1)S(1)} %add_convert_fusion.6), channel_id=1, source_target_pairs={{0,1},{1,0},{2,3},{3,2},{4,5},{5,4},{6,7},{7,6},{8,9},{9,8},{10,11... | collective-permute-start | bytes 983048 | tf_op jit(solution)/shard_map/ppermute | solution.py:291
  173.6 20.4 %all-to-all-start.5 = ((bf16[4,128,1280]{2,1,0:T(8,128)(2,1)}), bf16[4,128,1280]{2,1,0:T(8,128)(2,1)}, u32[]{:S(2)}, u32[]{:S(2)}) async-start(bf16[4,128,1280]{2,1,0:T(8,128)(2,1)} %broadcast_in_dim.40), calls=%async_computation.5 | async-start | bytes 2621440 | tf_op jit(solution)/shard_map/all_to_all | solution.py:294
  221.6 10.6 %collective-permute-start.14 = (bf16[128,1280]{1,0:T(8,128)(2,1)S(1)}, bf16[128,1280]{1,0:T(8,128)(2,1)S(1)}, u32[]{:S(2)}, u32[]{:S(2)}) collective-permute-start(bf16[128,1280]{1,0:T(8,128)(2,1)S(1)} %add_convert_fusion.4), channel_id=1, source_target_pairs={{0,16},{1,17},{2,18},{3,19},{4,20},{5,21},{6,22},{7,23},{8,24},{9,... | collective-permute-start | bytes 983048 | tf_op jit(solution)/shard_map/ppermute | solution.py:291
  222.9 14.3 %collective-permute-start.15 = (bf16[128,1280]{1,0:T(8,128)(2,1)S(1)}, bf16[128,1280]{1,0:T(8,128)(2,1)S(1)}, u32[]{:S(2)}, u32[]{:S(2)}) collective-permute-start(bf16[128,1280]{1,0:T(8,128)(2,1)S(1)} %add_convert_fusion.4), channel_id=1, source_target_pairs={{0,17},{1,16},{2,19},{3,18},{4,21},{5,20},{6,23},{7,22},{8,25},{9,... | collective-permute-start | bytes 983048 | tf_op jit(solution)/shard_map/ppermute | solution.py:291
  280.8 7.3 %collective-permute-start.16 = (bf16[128,1280]{1,0:T(8,128)(2,1)S(1)}, bf16[128,1280]{1,0:T(8,128)(2,1)}, u32[]{:S(2)}, u32[]{:S(2)}) collective-permute-start(bf16[128,1280]{1,0:T(8,128)(2,1)S(1)} %add_convert_fusion.2), channel_id=1, source_target_pairs={{0,1},{1,0},{2,3},{3,2},{4,5},{5,4},{6,7},{7,6},{8,9},{9,8},{10,11... | collective-permute-start | bytes 983048 | tf_op jit(solution)/shard_map/ppermute | solution.py:291
  290.3 17.7 %all-to-all-start.9 = ((bf16[4,128,1280]{2,1,0:T(8,128)(2,1)}), bf16[4,128,1280]{2,1,0:T(8,128)(2,1)}, u32[]{:S(2)}, u32[]{:S(2)}) async-start(bf16[4,128,1280]{2,1,0:T(8,128)(2,1)} %broadcast_in_dim.42), calls=%async_computation.9 | async-start | bytes 2621440 | tf_op jit(solution)/shard_map/all_to_all | solution.py:294
  319.1 15.8 %all-to-all-start.10 = ((bf16[4,128,1280]{2,1,0:T(8,128)(2,1)}), bf16[4,128,1280]{2,1,0:T(8,128)(2,1)S(1)}, u32[]{:S(2)}, u32[]{:S(2)}) async-start(bf16[4,128,1280]{2,1,0:T(8,128)(2,1)} %copy-done.6), calls=%async_computation.10 | async-start | bytes 2621440 | tf_op jit(solution)/shard_map/all_to_all | solution.py:294
  336.6 5.9 %collective-permute-start.17 = (bf16[4,16,1280]{2,1,0:T(8,128)(2,1)S(1)}, bf16[4,16,1280]{2,1,0:T(8,128)(2,1)S(1)}, u32[]{:S(2)}, u32[]{:S(2)}) collective-permute-start(bf16[4,16,1280]{2,1,0:T(8,128)(2,1)S(1)} %get-tuple-element.7), channel_id=1, source_target_pairs={{16,0},{17,1},{18,2},{19,3},{20,4},{21,5},{22,6},{23,7},{24,8},{25... | collective-permute-start | bytes 491528 | tf_op jit(solution)/shard_map/ppermute | solution.py:291
  339.2 4.1 %collective-permute-start.18 = (bf16[4,16,1280]{2,1,0:T(8,128)(2,1)S(1)}, bf16[4,16,1280]{2,1,0:T(8,128)(2,1)S(1)}, u32[]{:S(2)}, u32[]{:S(2)}) collective-permute-start(bf16[4,16,1280]{2,1,0:T(8,128)(2,1)S(1)} %get-tuple-element.8), channel_id=1, source_target_pairs={{16,1},{17,0},{18,3},{19,2},{20,5},{21,4},{22,7},{23,6},{24,9},{25... | collective-permute-start | bytes 491528 | tf_op jit(solution)/shard_map/ppermute | solution.py:291
  340.5 7.2 %collective-permute-start.19 = (bf16[4,16,1280]{2,1,0:T(8,128)(2,1)S(1)}, bf16[4,16,1280]{2,1,0:T(8,128)(2,1)S(1)}, u32[]{:S(2)}, u32[]{:S(2)}) collective-permute-start(bf16[4,16,1280]{2,1,0:T(8,128)(2,1)S(1)} %get-tuple-element.9), channel_id=1, source_target_pairs={{16,17},{17,16},{18,19},{19,18},{20,21},{21,20},{22,23},{23,22},{2... | collective-permute-start | bytes 491528 | tf_op jit(solution)/shard_map/ppermute | solution.py:291
  347.8 9.7 %collective-permute-start.20 = (bf16[16,1280]{1,0:T(8,128)(2,1)S(1)}, bf16[16,1280]{1,0:T(8,128)(2,1)S(1)}, u32[]{:S(2)}, u32[]{:S(2)}) collective-permute-start(bf16[16,1280]{1,0:T(8,128)(2,1)S(1)} %get-tuple-element.14), channel_id=1, source_target_pairs={{0,0},{1,1},{2,32},{3,33},{4,64},{5,65},{6,96},{7,97},{32,2},{33,3... | collective-permute-start | bytes 122888 | tf_op jit(solution)/shard_map/ppermute | solution.py:406
  350.8 7.7 %collective-permute-start.21 = (bf16[16,1280]{1,0:T(8,128)(2,1)S(1)}, bf16[16,1280]{1,0:T(8,128)(2,1)S(1)}, u32[]{:S(2)}, u32[]{:S(2)}) collective-permute-start(bf16[16,1280]{1,0:T(8,128)(2,1)S(1)} %get-tuple-element.17), channel_id=1, source_target_pairs={{0,32},{1,33},{2,64},{3,65},{4,96},{5,97},{6,0},{7,1},{32,34},{33,... | collective-permute-start | bytes 122888 | tf_op jit(solution)/shard_map/ppermute | solution.py:406
  355.4 6.1 %collective-permute-start.22 = (bf16[16,1280]{1,0:T(8,128)(2,1)S(1)}, bf16[16,1280]{1,0:T(8,128)(2,1)S(1)}, u32[]{:S(2)}, u32[]{:S(2)}) collective-permute-start(bf16[16,1280]{1,0:T(8,128)(2,1)S(1)} %get-tuple-element.16), channel_id=1, source_target_pairs={{0,64},{1,65},{2,96},{3,97},{4,0},{5,1},{6,32},{7,33},{32,66},{33,... | collective-permute-start | bytes 122888 | tf_op jit(solution)/shard_map/ppermute | solution.py:406
  356.5 5.4 %collective-permute-start.23 = (bf16[16,1280]{1,0:T(8,128)(2,1)S(1)}, bf16[16,1280]{1,0:T(8,128)(2,1)S(1)}, u32[]{:S(2)}, u32[]{:S(2)}) collective-permute-start(bf16[16,1280]{1,0:T(8,128)(2,1)S(1)} %get-tuple-element.15), channel_id=1, source_target_pairs={{0,96},{1,97},{2,0},{3,1},{4,32},{5,33},{6,64},{7,65},{32,98},{33,... | collective-permute-start | bytes 122888 | tf_op jit(solution)/shard_map/ppermute | solution.py:406
  (14 other events, 58.5 us)
where the time goes:
time: 364 us; the launch traced here: 363 us
  waiting for transfers between devices  133 us (37%)
  blocking collectives  92.1 us (25%)
  starting transfers between devices  60.9 us (17%)
  Pallas kernels  36.7 us (10%)
  local copies, waits for them, and re-layouts  29.9 us (8%)
  other arithmetic  9.9 us (3%)
    all_to_all x5, blocking collectives, z_all_to_all(): lax.all_to_all(value, 'tp', split_axis=0, concat_axis=0, tiled=True, axis...  92.1 us
    all_to_all x6, waiting for transfers between devices, z_all_to_all(): lax.all_to_all(value, 'tp', split_axis=0, concat_axis=0, tiled=True, axis...  75.9 us
    ppermute x13, waiting for transfers between devices, y_move(): return lax.ppermute(value, ('section', 'tp'), pairs)  51.4 us
    pallas_call x4, Pallas kernels, decoder_layer(): pl.pallas_call(layer_kernel, out_shape=jax.ShapeDtypeStruct(blocks.shape,...  28.9 us
    all_to_all x6, starting transfers between devices, z_all_to_all(): lax.all_to_all(value, 'tp', split_axis=0, concat_axis=0, tiled=True, axis...  26.5 us
    ppermute x13, starting transfers between devices, y_move(): return lax.ppermute(value, ('section', 'tp'), pairs)  24.8 us
    unnamed x33, local copies, waits for them, and re-layouts  17.3 us
    ppermute x4, starting transfers between devices, per_device(): landed.append(lax.ppermute(piece, ('pool', 'tp'), pairs))  8.96 us
  transfers between devices with their start and end apart: 30, of which 21 were waited for; matrix products, arithmetic and copies ran while one was open for 5% of the time, Pallas kernels for 1%

commit v1 on v0

--- a/solution.py
+++ b/solution.py
@@ -37,6 +37,10 @@
 
 def dot(a, b):
     return jnp.dot(a, b, preferred_element_type=F32)
+
+def dot_t(a, b):
+    return lax.dot_general(a, b, (((1,), (1,)), ((), ())), preferred_element_type=F32)
+
 
 def exact_gelu(x):
     return 0.5 * x * (1.0 + lax.erf(x * (0.5**0.5)))
@@ -67,11 +71,11 @@
     centered = values - jnp.mean(values, axis=-1, keepdims=True)
     variance = jnp.mean(centered * centered, axis=-1, keepdims=True)
     normed = (
-        centered * lax.rsqrt(variance + EPSILON) * gain_ref[...].astype(F32)
-        + bias_ref[...].astype(F32)
+        centered * lax.rsqrt(variance + EPSILON) * gain_ref[...].astype(F32)[None]
+        + bias_ref[...].astype(F32)[None]
     ).astype(BF)
     copies[0].wait()
-    raised = dot(normed, up_v[...]) + up_bias_ref[...].astype(F32)
+    raised = dot(normed, up_v[...]) + up_bias_ref[...].astype(F32)[None]
     active = exact_gelu(raised).astype(BF)
     copies[1].wait()
     lowered = dot(active, down_v[...])
@@ -97,14 +101,14 @@
             pltpu.VMEM((width // LANES, count, LANES), F32),
             pltpu.SemaphoreType.DMA((2,)),
         ],
-        compiler_params=pltpu.CompilerParams(vmem_limit_bytes=32 << 20),
+        compiler_params=pltpu.CompilerParams(vmem_limit_bytes=56 << 20),
         cost_estimate=pl.CostEstimate(
             flops=4 * count * width * hidden,
             bytes_accessed=4 * width * hidden,
             transcendentals=count * hidden,
         ),
         name="encoder_units",
-    )(frames, gain.reshape(1, -1), bias.reshape(1, -1), up, up_bias.reshape(1, -1), down)
+    )(frames, gain, bias, up, up_bias, down)
 
 
 def adapter_kernel(x_ref, in0, in1, out0, out1, part_ref, win, wout, sems):
@@ -122,7 +126,7 @@
     for i in range(2):
         in_copies[i].wait()
         total = sum(
-            dot(x_ref[b], win[i, b * depth : (b + 1) * depth, :]) for b in range(blocks)
+            dot_t(x_ref[b], win[i, :, b * depth : (b + 1) * depth]) for b in range(blocks)
         )
         lifted.append(exact_gelu(total).astype(BF))
     for copy in out_copies:
@@ -133,7 +137,7 @@
 
 
 def adapter(blocks, in_pair, out_pair):
-    width, units = in_pair[0].shape
+    units, width = in_pair[0].shape
     rows = blocks.shape[1]
     return pl.pallas_call(
         adapter_kernel,
@@ -141,11 +145,11 @@
         in_specs=[vmem()] + [anywhere()] * 4,
         out_specs=vmem(),
         scratch_shapes=[
-            pltpu.VMEM((2, width, units), BF),
+            pltpu.VMEM((2, units, width), BF),
             pltpu.VMEM((2, units, width), BF),
             pltpu.SemaphoreType.DMA((4,)),
         ],
-        compiler_params=pltpu.CompilerParams(vmem_limit_bytes=40 << 20),
+        compiler_params=pltpu.CompilerParams(vmem_limit_bytes=56 << 20),
         cost_estimate=pl.CostEstimate(
             flops=8 * rows * width * units,
             bytes_accessed=8 * width * units,
@@ -156,7 +160,7 @@
 
 
 def layer_kernel(
-    which, x_ref, gain_ref, mask_ref, q0, k0, v0, o0, q1, k1, v1, o1, out_ref, wq, wk, wv, wo, sems
+    which, x_ref, gain0, gain1, mask_ref, q0, k0, v0, o0, q1, k1, v1, o1, out_ref, wq, wk, wv, wo, sems
 ):
     blocks, rows, depth = x_ref.shape
 
@@ -197,7 +201,8 @@
     scale = lax.rsqrt(squares / (blocks * depth) + EPSILON)
     queries, keys, values = 0.0, 0.0, 0.0
     for b in range(blocks):
-        gain = gain_ref[:, b * depth : (b + 1) * depth].astype(F32)
+        cols = slice(b * depth, (b + 1) * depth)
+        gain = jnp.where(which[0] == 0, gain0[:, cols], gain1[:, cols])
         normed = (x_ref[b].astype(F32) * scale * gain).astype(BF)
         for copy in waits[b][:3]:
             copy.wait()
@@ -207,9 +212,7 @@
     heads = queries.shape[1] // HD
     queries = queries.astype(BF)
     stacked = jnp.concatenate([queries[:, h * HD : (h + 1) * HD] for h in range(heads)], axis=0)
-    scores = lax.dot_general(
-        stacked, keys.astype(BF), (((1,), (1,)), ((), ())), preferred_element_type=F32
-    ) * HD ** (-0.5)
+    scores = dot_t(stacked, keys.astype(BF)) * HD ** (-0.5)
     mask = jnp.concatenate([mask_ref[...]] * heads, axis=0)
     scores = jnp.where(mask > 0.5, scores, -1e30)
     exponent = jnp.exp(scores - jnp.max(scores, axis=-1, keepdims=True))
@@ -221,14 +224,14 @@
         out_ref[b] = dot(context, wo[b]).astype(BF)
 
 
-def decoder_layer(which, blocks, gain, mask, own, other):
+def decoder_layer(which, blocks, gains, mask, own, other):
     count, rows, depth = blocks.shape
     q_cols, kv_cols = own[0].shape[1], own[1].shape[1]
     weights = count * depth * (2 * q_cols + 2 * kv_cols)
     return pl.pallas_call(
         layer_kernel,
         out_shape=jax.ShapeDtypeStruct(blocks.shape, BF),
-        in_specs=[smem(), vmem(), vmem(), vmem()] + [anywhere()] * 8,
+        in_specs=[smem(), vmem(), vmem(), vmem(), vmem()] + [anywhere()] * 8,
         out_specs=vmem(),
         scratch_shapes=[
             pltpu.VMEM((count, depth, q_cols), BF),
@@ -237,12 +240,12 @@
             pltpu.VMEM((count, q_cols, depth), BF),
             pltpu.SemaphoreType.DMA((4, count)),
         ],
-        compiler_params=pltpu.CompilerParams(vmem_limit_bytes=40 << 20),
+        compiler_params=pltpu.CompilerParams(vmem_limit_bytes=56 << 20),
         cost_estimate=pl.CostEstimate(
             flops=2 * rows * weights, bytes_accessed=2 * weights, transcendentals=rows * rows * 4
         ),
         name="decoder_layer",
-    )(which, blocks, gain.reshape(1, -1), mask, *own, *other)
+    )(which, blocks, *gains, mask, *own, *other)
 
 
 def per_device(
@@ -308,8 +311,8 @@
 
     own_layer = (q_weight[0], k_weight[0], v_weight[0], o_weight[0])
     other_layer = tuple(chip_swap(weight) for weight in own_layer)
-    own_gain, other_gain = attn_gain[0], chip_swap(attn_gain[0])
-    in_pair = (adapt_in, chip_swap(adapt_in))
+    gains = [g.astype(F32).reshape(1, -1) for g in (attn_gain[0], chip_swap(attn_gain[0]))]
+    in_pair = (adapt_in.T, chip_swap(adapt_in.T))
     out_pair = (adapt_out, chip_swap(adapt_out))
 
     width = frames.shape[3]
@@ -324,6 +327,9 @@
     there = y_move(share, ((0, 1, 0), (1, 0, 0))).astype(F32) + y_move(
         share, ((0, 1, 1), (1, 0, 1))
     ).astype(F32)
+    here, in_pair, out_pair, other_layer, gains = lax.optimization_barrier(
+        (here, in_pair, out_pair, other_layer, gains)
+    )
     encoded = jnp.where(high == 0, jnp.stack([here, there]), jnp.stack([there, here]))
     encoded = encoded.astype(BF).reshape(2 * tokens, width)
 
@@ -365,9 +371,8 @@
 
     for turn in range(4):
         which = (core != turn % 2).astype(jnp.int32)
-        gain = jnp.where(which == 0, own_gain, other_gain)
         partial = decoder_layer(
-            which.reshape(1), z_gather(hidden), gain, mask, own_layer, other_layer
+            which.reshape(1), z_gather(hidden), gains, mask, own_layer, other_layer
         )
         share = (z_sum(partial) + at_first(hidden.astype(F32))).astype(BF)
         if turn == 1:

time: 364 us -> 347 us (0.953)
  local copies, waits for them, and re-layouts: 29.9 us -> 9.55 us
  blocking collectives: 92.1 us -> 109 us
  waiting for transfers between devices: 133 us -> 120 us
  starting transfers between devices: 60.9 us -> 48.7 us
  Pallas kernels: 36.7 us -> 47.1 us
    all_to_all x5 -> x6, blocking collectives: 92.1 us -> 109 us  [z_all_to_all(): lax.all_to_all(value, 'tp', split_axis=0, concat_axis=0, tiled=True, axis...]
    all_to_all x6 -> x5, waiting for transfers between devices: 75.9 us -> 59 us  [z_all_to_all(): lax.all_to_all(value, 'tp', split_axis=0, concat_axis=0, tiled=True, axis...]
    unnamed x33 -> x22, local copies, waits for them, and re-layouts: 17.3 us -> 3.27 us
    ppermute x13, starting transfers between devices: 24.8 us -> 17.7 us  [y_move(): return lax.ppermute(value, ('section', 'tp'), pairs)]
    all_to_all x6 -> x5, starting transfers between devices: 26.5 us -> 20.1 us  [z_all_to_all(): lax.all_to_all(value, 'tp', split_axis=0, concat_axis=0, tiled=True, axis...]
    pallas_call x4, Pallas kernels: 28.9 us -> 35.3 us  [decoder_layer(): pl.pallas_call(layer_kernel, out_shape=jax.ShapeDtypeStruct(blocks.shape,...]
    ppermute x7, waiting for transfers between devices: 0.02 us -> 5.35 us  [chip_swap(): lax.ppermute(value, 'section', [(i, i ^ 1) for i in range(section_count)])]
    ppermute x1 -> x0, local copies, waits for them, and re-layouts: 4 us -> none  [chip_swap(): lax.ppermute(value, 'section', [(i, i ^ 1) for i in range(section_count)])]
  transfers between devices with their start and end apart: 30 -> 29, of which waited for: 21 -> 22; matrix products, arithmetic and copies ran while one was open for 5% -> 3% of each run, Pallas kernels for 1% -> 1%
where the time goes in v1:
time: 347 us; the launch traced here: 346 us
  waiting for transfers between devices  120 us (35%)
  blocking collectives  109 us (31%)
  starting transfers between devices  48.7 us (14%)
  Pallas kernels  47.1 us (14%)
  other arithmetic  11.1 us (3%)
  local copies, waits for them, and re-layouts  9.55 us (3%)
    all_to_all x6, blocking collectives, z_all_to_all(): lax.all_to_all(value, 'tp', split_axis=0, concat_axis=0, tiled=True, axis...  109 us
    all_to_all x5, waiting for transfers between devices, z_all_to_all(): lax.all_to_all(value, 'tp', split_axis=0, concat_axis=0, tiled=True, axis...  59 us
    ppermute x13, waiting for transfers between devices, y_move(): return lax.ppermute(value, ('section', 'tp'), pairs)  50.2 us
    pallas_call x4, Pallas kernels, decoder_layer(): pl.pallas_call(layer_kernel, out_shape=jax.ShapeDtypeStruct(blocks.shape,...  35.3 us
    all_to_all x5, starting transfers between devices, z_all_to_all(): lax.all_to_all(value, 'tp', split_axis=0, concat_axis=0, tiled=True, axis...  20.1 us
    ppermute x13, starting transfers between devices, y_move(): return lax.ppermute(value, ('section', 'tp'), pairs)  17.7 us
    ppermute x4, starting transfers between devices, per_device(): landed.append(lax.ppermute(piece, ('pool', 'tp'), pairs))  9.95 us
  transfers between devices with their start and end apart: 29, of which 22 were waited for; matrix products, arithmetic and copies ran while one was open for 3% of the time, Pallas kernels for 1%

profile of v1, /device:TPU:30, one launch (start us, length us, event | category | flops | bytes accessed | tf_op | source)
XLA Modules:
  0.0 345.9 jit_solution(1740546298932664829)
XLA Ops:
  0.5 5.1 %encoder_units.1 = bf16[4,64,1280]{2,1,0:T(8,128)(2,1)} custom-call(bf16[256,1280]{1,0:T(8,128)(2,1)} %bitcast.91, bf16[1280]{0:T(1024)(128)(2,1)} %gain_ref.1, bf16[1280]{0:T(1024)(128)(2,1)} %bias_ref.1, bf16[1280,640]{1,0:T(8,128)(2,1)} %up_ref.1, bf16[640]{0:T(1024)(128)(2,1)} %up_bias_ref.1, bf16[640,1280]{1,0:T(8,128)(2,1)} %down_ref.1), custom_call_target="tpu_custom_call" | custom-call | flops 838860800 | bytes 3276800 | tf_op jit(solution)/shard_map/encoder_units/pallas_call | solution.py:93
  5.7 5.5 %all-to-all-start = ((bf16[4,64,1280]{2,1,0:T(8,128)(2,1)}), bf16[4,64,1280]{2,1,0:T(8,128)(2,1)S(1)}, u32[]{:S(2)}, u32[]{:S(2)}) async-start(bf16[4,64,1280]{2,1,0:T(8,128)(2,1)} %encoder_units.1), calls=%async_computation | async-start | bytes 1310720 | tf_op jit(solution)/shard_map/all_to_all | solution.py:297
  14.4 7.8 %all-to-all-done = bf16[4,64,1280]{2,1,0:T(8,128)(2,1)S(1)} async-done(((bf16[4,64,1280]{2,1,0:T(8,128)(2,1)}), bf16[4,64,1280]{2,1,0:T(8,128)(2,1)S(1)}, u32[]{:S(2)}, u32[]{:S(2)}) %all-to-all-start) | async-done | bytes 655392 | tf_op jit(solution)/shard_map/all_to_all | solution.py:297
  29.9 3.9 %collective-permute-done.8 = bf16[64,1280]{1,0:T(8,128)(2,1)S(1)} collective-permute-done((bf16[64,1280]{1,0:T(8,128)(2,1)S(1)}, bf16[64,1280]{1,0:T(8,128)(2,1)S(1)}, u32[]{:S(2)}, u32[]{:S(2)}) %collective-permute-start.8) | collective-permute-done | bytes 163872 | tf_op jit(solution)/shard_map/ppermute | solution.py:294
  38.4 4.2 %collective-permute-done.5.v1 = bf16[5120,128]{1,0:T(8,128)(2,1)S(1)} collective-permute-done((bf16[5120,128]{1,0:T(8,128)(2,1)S(1)}, bf16[5120,128]{1,0:T(8,128)(2,1)S(1)}, u32[]{:S(2)}, u32[]{:S(2)}) %collective-permute-start.5) | collective-permute-done | bytes 1310752 | tf_op jit(solution)/shard_map/ppermute | solution.py:281
  42.8 21.7 %all_to_all.55.x_ref = bf16[4,128,1280]{2,1,0:T(8,128)(2,1)} all-to-all(bf16[4,128,1280]{2,1,0:T(8,128)(2,1)S(1)} %broadcast_in_dim.38), channel_id=1, replica_groups={{0,2,4,6},{1,3,5,7},{8,10,12,14},{9,11,13,15},{16,18,20,22},{17,19,21,2..., dimensions={0} | all-to-all | bytes 2621440 | tf_op jit(solution)/shard_map/all_to_all | solution.py:297
  64.4 6.7 %adapter_units.1 = bf16[4,128,1280]{2,1,0:T(8,128)(2,1)} custom-call(bf16[4,128,1280]{2,1,0:T(8,128)(2,1)} %all_to_all.55.x_ref, bf16[160,5120]{1,0:T(8,128)(2,1)} %bitcast.93, bf16[160,5120]{1,0:T(8,128)(2,1)} %collective-permute-done.1.in1, bf16[160,5120]{1,0:T(8,128)(2,1)} %out0, bf16[160,5120]{1,0:T(8,128)(2,1)} %collective-permute-done.2.out1), custom_call_target="tpu_custom_call" | custom-call | flops 838860800 | bytes 6553600 | tf_op jit(solution)/shard_map/adapter_units/pallas_call | solution.py:142
  71.2 21.2 %all_to_all.56 = bf16[4,128,1280]{2,1,0:T(8,128)(2,1)S(1)} all-to-all(bf16[4,128,1280]{2,1,0:T(8,128)(2,1)} %adapter_units.1), channel_id=1, replica_groups={{0,2,4,6},{1,3,5,7},{8,10,12,14},{9,11,13,15},{16,18,20,22},{17,19,21,2..., dimensions={0} | all-to-all | bytes 2621440 | tf_op jit(solution)/shard_map/all_to_all | solution.py:297
  92.8 4.3 %collective-permute-start.11 = (bf16[128,1280]{1,0:T(8,128)(2,1)S(1)}, bf16[128,1280]{1,0:T(8,128)(2,1)S(1)}, u32[]{:S(2)}, u32[]{:S(2)}) collective-permute-start(bf16[128,1280]{1,0:T(8,128)(2,1)S(1)} %reduce_sum.99), channel_id=1, source_target_pairs={{16,0},{17,1},{18,2},{19,3},{20,4},{21,5},{22,6},{23,7},{24,8},{25... | collective-permute-start | bytes 983048 | tf_op jit(solution)/shard_map/ppermute | solution.py:294
  98.5 4.8 %collective-permute-done.10 = bf16[128,1280]{1,0:T(8,128)(2,1)S(1)} collective-permute-done((bf16[128,1280]{1,0:T(8,128)(2,1)S(1)}, bf16[128,1280]{1,0:T(8,128)(2,1)S(1)}, u32[]{:S(2)}, u32[]{:S(2)}) %collective-permute-start.10) | collective-permute-done | bytes 327712 | tf_op jit(solution)/shard_map/ppermute | solution.py:294
  105.5 4.9 %collective-permute-done.12 = bf16[128,1280]{1,0:T(8,128)(2,1)S(1)} collective-permute-done((bf16[128,1280]{1,0:T(8,128)(2,1)S(1)}, bf16[128,1280]{1,0:T(8,128)(2,1)S(1)}, u32[]{:S(2)}, u32[]{:S(2)}) %collective-permute-start.12) | collective-permute-done | bytes 327712 | tf_op jit(solution)/shard_map/ppermute | solution.py:294
  111.7 3.9 %all-to-all-start.3 = ((bf16[4,128,1280]{2,1,0:T(8,128)(2,1)}), bf16[4,128,1280]{2,1,0:T(8,128)(2,1)S(1)}, u32[]{:S(2)}, u32[]{:S(2)}) async-start(bf16[4,128,1280]{2,1,0:T(8,128)(2,1)} %broadcast_in_dim.39), calls=%async_computation.3 | async-start | bytes 2621440 | tf_op jit(solution)/shard_map/all_to_all | solution.py:297
  116.8 15.0 %all-to-all-done.3.x_ref = bf16[4,128,1280]{2,1,0:T(8,128)(2,1)S(1)} async-done(((bf16[4,128,1280]{2,1,0:T(8,128)(2,1)}), bf16[4,128,1280]{2,1,0:T(8,128)(2,1)S(1)}, u32[]{:S(2)}, u32[]{:S(2)}) %all-to-all-start.3) | async-done | bytes 1310752 | tf_op jit(solution)/shard_map/all_to_all | solution.py:297
  132.9 8.7 %decoder_layer.4 = bf16[4,128,1280]{2,1,0:T(8,128)(2,1)} custom-call(s32[1]{0:T(128)} %bitcast.8.which, bf16[4,128,1280]{2,1,0:T(8,128)(2,1)} %copy-done.3, f32[1,5120]{1,0:T(1,128)} %get-tuple-element.21.gain0, f32[1,5120]{1,0:T(1,128)} %bitcast.96, f32[128,128]{1,0:T(8,128)} %fusion.9.mask_ref, bf16[5120,512]{1,0:T(8,128)(2,1)} %bitcast.71, ...), custom_call_target="tpu_custom_call" | custom-call | flops 1677721600 | bytes 13107200 | tf_op jit(solution)/shard_map/decoder_layer/pallas_call | solution.py:231
  141.6 19.4 %all_to_all.57 = bf16[4,128,1280]{2,1,0:T(8,128)(2,1)S(1)} all-to-all(bf16[4,128,1280]{2,1,0:T(8,128)(2,1)} %decoder_layer.4), channel_id=1, replica_groups={{0,2,4,6},{1,3,5,7},{8,10,12,14},{9,11,13,15},{16,18,20,22},{17,19,21,2..., dimensions={0} | all-to-all | bytes 2621440 | tf_op jit(solution)/shard_map/all_to_all | solution.py:297
  161.4 7.1 %collective-permute-done.13 = bf16[128,1280]{1,0:T(8,128)(2,1)S(1)} collective-permute-done((bf16[128,1280]{1,0:T(8,128)(2,1)S(1)}, bf16[128,1280]{1,0:T(8,128)(2,1)S(1)}, u32[]{:S(2)}, u32[]{:S(2)}) %collective-permute-start.13) | collective-permute-done | bytes 327712 | tf_op jit(solution)/shard_map/ppermute | solution.py:294
  173.2 13.7 %all-to-all-done.5.x_ref = bf16[4,128,1280]{2,1,0:T(8,128)(2,1)S(1)} async-done(((bf16[4,128,1280]{2,1,0:T(8,128)(2,1)}), bf16[4,128,1280]{2,1,0:T(8,128)(2,1)S(1)}, u32[]{:S(2)}, u32[]{:S(2)}) %all-to-all-start.5) | async-done | bytes 1310752 | tf_op jit(solution)/shard_map/all_to_all | solution.py:297
  188.0 8.9 %decoder_layer.5 = bf16[4,128,1280]{2,1,0:T(8,128)(2,1)} custom-call(s32[1]{0:T(128)} %bitcast.7.which, bf16[4,128,1280]{2,1,0:T(8,128)(2,1)} %copy-done.5, f32[1,5120]{1,0:T(1,128)} %get-tuple-element.21.gain0, f32[1,5120]{1,0:T(1,128)} %bitcast.97, f32[128,128]{1,0:T(8,128)} %fusion.9.mask_ref, bf16[5120,512]{1,0:T(8,128)(2,1)} %bitcast.72, ...), custom_call_target="tpu_custom_call" | custom-call | flops 1677721600 | bytes 13107200 | tf_op jit(solution)/shard_map/decoder_layer/pallas_call | solution.py:231
  197.0 15.8 %all_to_all.58 = bf16[4,128,1280]{2,1,0:T(8,128)(2,1)S(1)} all-to-all(bf16[4,128,1280]{2,1,0:T(8,128)(2,1)} %decoder_layer.5), channel_id=1, replica_groups={{0,2,4,6},{1,3,5,7},{8,10,12,14},{9,11,13,15},{16,18,20,22},{17,19,21,2..., dimensions={0} | all-to-all | bytes 2621440 | tf_op jit(solution)/shard_map/all_to_all | solution.py:297
  215.7 8.0 %collective-permute-done.14 = bf16[128,1280]{1,0:T(8,128)(2,1)S(1)} collective-permute-done((bf16[128,1280]{1,0:T(8,128)(2,1)S(1)}, bf16[128,1280]{1,0:T(8,128)(2,1)S(1)}, u32[]{:S(2)}, u32[]{:S(2)}) %collective-permute-start.14) | collective-permute-done | bytes 327712 | tf_op jit(solution)/shard_map/ppermute | solution.py:294
  227.3 15.5 %all_to_all.59.x_ref = bf16[4,128,1280]{2,1,0:T(8,128)(2,1)} all-to-all(bf16[4,128,1280]{2,1,0:T(8,128)(2,1)S(1)} %broadcast_in_dim.41), channel_id=1, replica_groups={{0,2,4,6},{1,3,5,7},{8,10,12,14},{9,11,13,15},{16,18,20,22},{17,19,21,2..., dimensions={0} | all-to-all | bytes 2621440 | tf_op jit(solution)/shard_map/all_to_all | solution.py:297
  242.8 8.7 %decoder_layer.6 = bf16[4,128,1280]{2,1,0:T(8,128)(2,1)} custom-call(s32[1]{0:T(128)} %bitcast.8.which, bf16[4,128,1280]{2,1,0:T(8,128)(2,1)} %all_to_all.59.x_ref, f32[1,5120]{1,0:T(1,128)} %get-tuple-element.21.gain0, f32[1,5120]{1,0:T(1,128)} %bitcast.98, f32[128,128]{1,0:T(8,128)} %fusion.9.mask_ref, bf16[5120,512]{1,0:T(8,128)(2,1)} %bitcast.73, ...), custom_call_target="tpu_custom_call" | custom-call | flops 1677721600 | bytes 13107200 | tf_op jit(solution)/shard_map/decoder_layer/pallas_call | solution.py:231
  251.5 15.8 %all_to_all.60 = bf16[4,128,1280]{2,1,0:T(8,128)(2,1)S(1)} all-to-all(bf16[4,128,1280]{2,1,0:T(8,128)(2,1)} %decoder_layer.6), channel_id=1, replica_groups={{0,2,4,6},{1,3,5,7},{8,10,12,14},{9,11,13,15},{16,18,20,22},{17,19,21,2..., dimensions={0} | all-to-all | bytes 2621440 | tf_op jit(solution)/shard_map/all_to_all | solution.py:297
  268.9 5.8 %collective-permute-done.16 = bf16[128,1280]{1,0:T(8,128)(2,1)S(1)} collective-permute-done((bf16[128,1280]{1,0:T(8,128)(2,1)S(1)}, bf16[128,1280]{1,0:T(8,128)(2,1)S(1)}, u32[]{:S(2)}, u32[]{:S(2)}) %collective-permute-start.16) | collective-permute-done | bytes 327712 | tf_op jit(solution)/shard_map/ppermute | solution.py:294
  276.0 3.7 %all-to-all-start.9 = ((bf16[4,128,1280]{2,1,0:T(8,128)(2,1)}), bf16[4,128,1280]{2,1,0:T(8,128)(2,1)S(1)}, u32[]{:S(2)}, u32[]{:S(2)}) async-start(bf16[4,128,1280]{2,1,0:T(8,128)(2,1)} %broadcast_in_dim.42), calls=%async_computation.9 | async-start | bytes 2621440 | tf_op jit(solution)/shard_map/all_to_all | solution.py:297
  281.4 10.5 %all-to-all-done.9.x_ref = bf16[4,128,1280]{2,1,0:T(8,128)(2,1)S(1)} async-done(((bf16[4,128,1280]{2,1,0:T(8,128)(2,1)}), bf16[4,128,1280]{2,1,0:T(8,128)(2,1)S(1)}, u32[]{:S(2)}, u32[]{:S(2)}) %all-to-all-start.9) | async-done | bytes 1310752 | tf_op jit(solution)/shard_map/all_to_all | solution.py:297
  293.0 8.9 %decoder_layer.7 = bf16[4,128,1280]{2,1,0:T(8,128)(2,1)} custom-call(s32[1]{0:T(128)} %bitcast.7.which, bf16[4,128,1280]{2,1,0:T(8,128)(2,1)} %copy-done.4, f32[1,5120]{1,0:T(1,128)} %get-tuple-element.21.gain0, f32[1,5120]{1,0:T(1,128)} %bitcast.99, f32[128,128]{1,0:T(8,128)} %fusion.9.mask_ref, bf16[5120,512]{1,0:T(8,128)(2,1)} %bitcast.74, ...), custom_call_target="tpu_custom_call" | custom-call | flops 1677721600 | bytes 13107200 | tf_op jit(solution)/shard_map/decoder_layer/pallas_call | solution.py:231
  301.9 3.6 %all-to-all-start.10 = ((bf16[4,128,1280]{2,1,0:T(8,128)(2,1)}), bf16[4,128,1280]{2,1,0:T(8,128)(2,1)S(1)}, u32[]{:S(2)}, u32[]{:S(2)}) async-start(bf16[4,128,1280]{2,1,0:T(8,128)(2,1)} %decoder_layer.7), calls=%async_computation.10 | async-start | bytes 2621440 | tf_op jit(solution)/shard_map/all_to_all | solution.py:297
  305.8 12.0 %all-to-all-done.10 = bf16[4,128,1280]{2,1,0:T(8,128)(2,1)S(1)} async-done(((bf16[4,128,1280]{2,1,0:T(8,128)(2,1)}), bf16[4,128,1280]{2,1,0:T(8,128)(2,1)S(1)}, u32[]{:S(2)}, u32[]{:S(2)}) %all-to-all-start.10) | async-done | bytes 1310752 | tf_op jit(solution)/shard_map/all_to_all | solution.py:297
  325.8 4.3 %collective-permute-done.19 = bf16[4,16,1280]{2,1,0:T(8,128)(2,1)S(1)} collective-permute-done((bf16[4,16,1280]{2,1,0:T(8,128)(2,1)S(1)}, bf16[4,16,1280]{2,1,0:T(8,128)(2,1)S(1)}, u32[]{:S(2)}, u32[]{:S(2)}) %collective-permute-start.19) | collective-permute-done | bytes 163872 | tf_op jit(solution)/shard_map/ppermute | solution.py:294
  330.2 3.9 %collective-permute-start.20 = (bf16[16,1280]{1,0:T(8,128)(2,1)S(1)}, bf16[16,1280]{1,0:T(8,128)(2,1)S(1)}, u32[]{:S(2)}, u32[]{:S(2)}) collective-permute-start(bf16[16,1280]{1,0:T(8,128)(2,1)S(1)} %get-tuple-element.36), channel_id=1, source_target_pairs={{0,0},{1,1},{2,32},{3,33},{4,64},{5,65},{6,96},{7,97},{32,2},{33,3... | collective-permute-start | bytes 122888 | tf_op jit(solution)/shard_map/ppermute | solution.py:411
  334.1 3.7 %collective-permute-start.21 = (bf16[16,1280]{1,0:T(8,128)(2,1)S(1)}, bf16[16,1280]{1,0:T(8,128)(2,1)S(1)}, u32[]{:S(2)}, u32[]{:S(2)}) collective-permute-start(bf16[16,1280]{1,0:T(8,128)(2,1)S(1)} %get-tuple-element.39), channel_id=1, source_target_pairs={{0,32},{1,33},{2,64},{3,65},{4,96},{5,97},{6,0},{7,1},{32,34},{33,... | collective-permute-start | bytes 122888 | tf_op jit(solution)/shard_map/ppermute | solution.py:411
  (120 shorter events, 58.6 us)
Async XLA Ops:
  0.0 42.6 %collective-permute-start.3 = (bf16[5120,512]{1,0:T(8,128)(2,1)}, bf16[5120,512]{1,0:T(8,128)(2,1)}, u32[]{:S(2)}, u32[]{:S(2)}) collective-permute-start(bf16[5120,512]{1,0:T(8,128)(2,1)} %bitcast.70), channel_id=1, source_target_pairs={{0,8},{8,0},{16,24},{24,16},{1,9},{9,1},{17,25},{25,17},{2,10},{10... | collective-permute-start | bytes 15728648 | tf_op jit(solution)/shard_map/ppermute | solution.py:281
  0.0 42.6 %collective-permute-start.6 = (bf16[512,5120]{1,0:T(8,128)(2,1)}, bf16[512,5120]{1,0:T(8,128)(2,1)}, u32[]{:S(2)}, u32[]{:S(2)}) collective-permute-start(bf16[512,5120]{1,0:T(8,128)(2,1)} %bitcast.75), channel_id=1, source_target_pairs={{0,8},{8,0},{16,24},{24,16},{1,9},{9,1},{17,25},{25,17},{2,10},{10... | collective-permute-start | bytes 15728648 | tf_op jit(solution)/shard_map/ppermute | solution.py:281
  5.7 16.5 %all-to-all-start = ((bf16[4,64,1280]{2,1,0:T(8,128)(2,1)}), bf16[4,64,1280]{2,1,0:T(8,128)(2,1)S(1)}, u32[]{:S(2)}, u32[]{:S(2)}) async-start(bf16[4,64,1280]{2,1,0:T(8,128)(2,1)} %encoder_units.1), calls=%async_computation | async-start | bytes 1310720 | tf_op jit(solution)/shard_map/all_to_all | solution.py:297
  11.1 26.1 %collective-permute-start.4 = (bf16[5120,128]{1,0:T(8,128)(2,1)S(1)}, bf16[5120,128]{1,0:T(8,128)(2,1)}, u32[]{:S(2)}, u32[]{:S(2)}) collective-permute-start(bf16[5120,128]{1,0:T(8,128)(2,1)S(1)} %bitcast.84), channel_id=1, source_target_pairs={{0,8},{8,0},{16,24},{24,16},{1,9},{9,1},{17,25},{25,17},{2,10},{10... | collective-permute-start | bytes 3932168 | tf_op jit(solution)/shard_map/ppermute | solution.py:281
  12.1 12.0 %copy-start.9 = (bf16[1,5120]{1,0:T(2,128)(2,1)S(1)}, bf16[1,5120]{1,0:T(2,128)(2,1)}, u32[]{:S(2)}) copy-start(bf16[1,5120]{1,0:T(2,128)(2,1)} %param.27) | copy-start | bytes 30724
  12.1 25.1 %copy-start.1 = (bf16[1,5120,128]{2,1,0:T(8,128)(2,1)S(1)}, bf16[1,5120,128]{2,1,0:T(8,128)(2,1)}, u32[]{:S(2)}) copy-start(bf16[1,5120,128]{2,1,0:T(8,128)(2,1)} %param.30) | copy-start | bytes 3932164
  23.3 5.4 %collective-permute-start = (bf16[64,1280]{1,0:T(8,128)(2,1)S(1)}, bf16[64,1280]{1,0:T(8,128)(2,1)S(1)}, u32[]{:S(2)}, u32[]{:S(2)}) collective-permute-start(bf16[64,1280]{1,0:T(8,128)(2,1)S(1)} %fusion.3), channel_id=1, source_target_pairs={{0,1},{1,0},{2,3},{3,2},{4,5},{5,4},{6,7},{7,6},{8,9},{9,8},{10,11... | collective-permute-start | bytes 491528 | tf_op jit(solution)/shard_map/ppermute | solution.py:294
  24.8 1.2 collective-permute-start.7
  25.9 7.9 %collective-permute-start.8 = (bf16[64,1280]{1,0:T(8,128)(2,1)S(1)}, bf16[64,1280]{1,0:T(8,128)(2,1)S(1)}, u32[]{:S(2)}, u32[]{:S(2)}) collective-permute-start(bf16[64,1280]{1,0:T(8,128)(2,1)S(1)} %fusion.3), channel_id=1, source_target_pairs={{0,16},{1,17},{2,18},{3,19},{4,20},{5,21},{6,22},{7,23},{8,24},{9,... | collective-permute-start | bytes 491528 | tf_op jit(solution)/shard_map/ppermute | solution.py:294
  28.7 8.5 %collective-permute-start.9 = (bf16[64,1280]{1,0:T(8,128)(2,1)S(1)}, bf16[64,1280]{1,0:T(8,128)(2,1)S(1)}, u32[]{:S(2)}, u32[]{:S(2)}) collective-permute-start(bf16[64,1280]{1,0:T(8,128)(2,1)S(1)} %fusion.3), channel_id=1, source_target_pairs={{0,17},{1,16},{2,19},{3,18},{4,21},{5,20},{6,23},{7,22},{8,25},{9,... | collective-permute-start | bytes 491528 | tf_op jit(solution)/shard_map/ppermute | solution.py:294
  33.8 8.8 %collective-permute-start.1 = (bf16[160,5120]{1,0:T(8,128)(2,1)}, bf16[160,5120]{1,0:T(8,128)(2,1)}, u32[]{:S(2)}, u32[]{:S(2)}) collective-permute-start(bf16[160,5120]{1,0:T(8,128)(2,1)} %bitcast.92), channel_id=1, source_target_pairs={{0,8},{8,0},{16,24},{24,16},{1,9},{9,1},{17,25},{25,17},{2,10},{10... | collective-permute-start | bytes 4915208 | tf_op jit(solution)/shard_map/ppermute | solution.py:281
  37.2 5.4 %collective-permute-start.2 = (bf16[160,5120]{1,0:T(8,128)(2,1)}, bf16[160,5120]{1,0:T(8,128)(2,1)}, u32[]{:S(2)}, u32[]{:S(2)}) collective-permute-start(bf16[160,5120]{1,0:T(8,128)(2,1)} %out0), channel_id=1, source_target_pairs={{0,8},{8,0},{16,24},{24,16},{1,9},{9,1},{17,25},{25,17},{2,10},{10... | collective-permute-start | bytes 4915208 | tf_op jit(solution)/shard_map/ppermute | solution.py:281
  37.2 5.4 %collective-permute-start.5 = (bf16[5120,128]{1,0:T(8,128)(2,1)S(1)}, bf16[5120,128]{1,0:T(8,128)(2,1)S(1)}, u32[]{:S(2)}, u32[]{:S(2)}) collective-permute-start(bf16[5120,128]{1,0:T(8,128)(2,1)S(1)} %bitcast.89), channel_id=1, source_target_pairs={{0,8},{8,0},{16,24},{24,16},{1,9},{9,1},{17,25},{25,17},{2,10},{10... | collective-permute-start | bytes 3932168 | tf_op jit(solution)/shard_map/ppermute | solution.py:281
  42.6 21.8 %copy-start.2 = (bf16[5120,128]{1,0:T(8,128)(2,1)}, bf16[5120,128]{1,0:T(8,128)(2,1)S(1)}, u32[]{:S(2)}) copy-start(bf16[5120,128]{1,0:T(8,128)(2,1)S(1)} %collective-permute-done.5.v1) | copy-start | bytes 3932164
  92.5 10.7 %collective-permute-start.10 = (bf16[128,1280]{1,0:T(8,128)(2,1)S(1)}, bf16[128,1280]{1,0:T(8,128)(2,1)S(1)}, u32[]{:S(2)}, u32[]{:S(2)}) collective-permute-start(bf16[128,1280]{1,0:T(8,128)(2,1)S(1)} %reduce_sum.99), channel_id=1, source_target_pairs={{0,1},{1,0},{2,3},{3,2},{4,5},{5,4},{6,7},{7,6},{8,9},{9,8},{10,11... | collective-permute-start | bytes 983048 | tf_op jit(solution)/shard_map/ppermute | solution.py:294
  92.8 12.6 %collective-permute-start.11 = (bf16[128,1280]{1,0:T(8,128)(2,1)S(1)}, bf16[128,1280]{1,0:T(8,128)(2,1)S(1)}, u32[]{:S(2)}, u32[]{:S(2)}) collective-permute-start(bf16[128,1280]{1,0:T(8,128)(2,1)S(1)} %reduce_sum.99), channel_id=1, source_target_pairs={{16,0},{17,1},{18,2},{19,3},{20,4},{21,5},{22,6},{23,7},{24,8},{25... | collective-permute-start | bytes 983048 | tf_op jit(solution)/shard_map/ppermute | solution.py:294
  97.1 13.2 %collective-permute-start.12 = (bf16[128,1280]{1,0:T(8,128)(2,1)S(1)}, bf16[128,1280]{1,0:T(8,128)(2,1)S(1)}, u32[]{:S(2)}, u32[]{:S(2)}) collective-permute-start(bf16[128,1280]{1,0:T(8,128)(2,1)S(1)} %reduce_sum.99), channel_id=1, source_target_pairs={{16,1},{17,0},{18,3},{19,2},{20,5},{21,4},{22,7},{23,6},{24,9},{25... | collective-permute-start | bytes 983048 | tf_op jit(solution)/shard_map/ppermute | solution.py:294
  111.7 20.2 %all-to-all-start.3 = ((bf16[4,128,1280]{2,1,0:T(8,128)(2,1)}), bf16[4,128,1280]{2,1,0:T(8,128)(2,1)S(1)}, u32[]{:S(2)}, u32[]{:S(2)}) async-start(bf16[4,128,1280]{2,1,0:T(8,128)(2,1)} %broadcast_in_dim.39), calls=%async_computation.3 | async-start | bytes 2621440 | tf_op jit(solution)/shard_map/all_to_all | solution.py:297
  161.3 7.2 %collective-permute-start.13 = (bf16[128,1280]{1,0:T(8,128)(2,1)S(1)}, bf16[128,1280]{1,0:T(8,128)(2,1)S(1)}, u32[]{:S(2)}, u32[]{:S(2)}) collective-permute-start(bf16[128,1280]{1,0:T(8,128)(2,1)S(1)} %add_convert_fusion.6), channel_id=1, source_target_pairs={{0,1},{1,0},{2,3},{3,2},{4,5},{5,4},{6,7},{7,6},{8,9},{9,8},{10,11... | collective-permute-start | bytes 983048 | tf_op jit(solution)/shard_map/ppermute | solution.py:294
  169.7 17.3 %all-to-all-start.5 = ((bf16[4,128,1280]{2,1,0:T(8,128)(2,1)}), bf16[4,128,1280]{2,1,0:T(8,128)(2,1)S(1)}, u32[]{:S(2)}, u32[]{:S(2)}) async-start(bf16[4,128,1280]{2,1,0:T(8,128)(2,1)} %broadcast_in_dim.40), calls=%async_computation.5 | async-start | bytes 2621440 | tf_op jit(solution)/shard_map/all_to_all | solution.py:297
  213.1 10.6 %collective-permute-start.14 = (bf16[128,1280]{1,0:T(8,128)(2,1)S(1)}, bf16[128,1280]{1,0:T(8,128)(2,1)S(1)}, u32[]{:S(2)}, u32[]{:S(2)}) collective-permute-start(bf16[128,1280]{1,0:T(8,128)(2,1)S(1)} %add_convert_fusion.4), channel_id=1, source_target_pairs={{0,16},{1,17},{2,18},{3,19},{4,20},{5,21},{6,22},{7,23},{8,24},{9,... | collective-permute-start | bytes 983048 | tf_op jit(solution)/shard_map/ppermute | solution.py:294
  214.4 12.7 %collective-permute-start.15 = (bf16[128,1280]{1,0:T(8,128)(2,1)S(1)}, bf16[128,1280]{1,0:T(8,128)(2,1)S(1)}, u32[]{:S(2)}, u32[]{:S(2)}) collective-permute-start(bf16[128,1280]{1,0:T(8,128)(2,1)S(1)} %add_convert_fusion.4), channel_id=1, source_target_pairs={{0,17},{1,16},{2,19},{3,18},{4,21},{5,20},{6,23},{7,22},{8,25},{9,... | collective-permute-start | bytes 983048 | tf_op jit(solution)/shard_map/ppermute | solution.py:294
  267.6 7.2 %collective-permute-start.16 = (bf16[128,1280]{1,0:T(8,128)(2,1)S(1)}, bf16[128,1280]{1,0:T(8,128)(2,1)S(1)}, u32[]{:S(2)}, u32[]{:S(2)}) collective-permute-start(bf16[128,1280]{1,0:T(8,128)(2,1)S(1)} %add_convert_fusion.2), channel_id=1, source_target_pairs={{0,1},{1,0},{2,3},{3,2},{4,5},{5,4},{6,7},{7,6},{8,9},{9,8},{10,11... | collective-permute-start | bytes 983048 | tf_op jit(solution)/shard_map/ppermute | solution.py:294
  276.0 15.9 %all-to-all-start.9 = ((bf16[4,128,1280]{2,1,0:T(8,128)(2,1)}), bf16[4,128,1280]{2,1,0:T(8,128)(2,1)S(1)}, u32[]{:S(2)}, u32[]{:S(2)}) async-start(bf16[4,128,1280]{2,1,0:T(8,128)(2,1)} %broadcast_in_dim.42), calls=%async_computation.9 | async-start | bytes 2621440 | tf_op jit(solution)/shard_map/all_to_all | solution.py:297
  301.9 15.8 %all-to-all-start.10 = ((bf16[4,128,1280]{2,1,0:T(8,128)(2,1)}), bf16[4,128,1280]{2,1,0:T(8,128)(2,1)S(1)}, u32[]{:S(2)}, u32[]{:S(2)}) async-start(bf16[4,128,1280]{2,1,0:T(8,128)(2,1)} %decoder_layer.7), calls=%async_computation.10 | async-start | bytes 2621440 | tf_op jit(solution)/shard_map/all_to_all | solution.py:297
  319.5 5.6 %collective-permute-start.17 = (bf16[4,16,1280]{2,1,0:T(8,128)(2,1)S(1)}, bf16[4,16,1280]{2,1,0:T(8,128)(2,1)S(1)}, u32[]{:S(2)}, u32[]{:S(2)}) collective-permute-start(bf16[4,16,1280]{2,1,0:T(8,128)(2,1)S(1)} %get-tuple-element.29), channel_id=1, source_target_pairs={{16,0},{17,1},{18,2},{19,3},{20,4},{21,5},{22,6},{23,7},{24,8},{25... | collective-permute-start | bytes 491528 | tf_op jit(solution)/shard_map/ppermute | solution.py:294
  321.6 4.3 %collective-permute-start.18 = (bf16[4,16,1280]{2,1,0:T(8,128)(2,1)S(1)}, bf16[4,16,1280]{2,1,0:T(8,128)(2,1)S(1)}, u32[]{:S(2)}, u32[]{:S(2)}) collective-permute-start(bf16[4,16,1280]{2,1,0:T(8,128)(2,1)S(1)} %get-tuple-element.30), channel_id=1, source_target_pairs={{16,1},{17,0},{18,3},{19,2},{20,5},{21,4},{22,7},{23,6},{24,9},{25... | collective-permute-start | bytes 491528 | tf_op jit(solution)/shard_map/ppermute | solution.py:294
  322.9 7.2 %collective-permute-start.19 = (bf16[4,16,1280]{2,1,0:T(8,128)(2,1)S(1)}, bf16[4,16,1280]{2,1,0:T(8,128)(2,1)S(1)}, u32[]{:S(2)}, u32[]{:S(2)}) collective-permute-start(bf16[4,16,1280]{2,1,0:T(8,128)(2,1)S(1)} %get-tuple-element.31), channel_id=1, source_target_pairs={{16,17},{17,16},{18,19},{19,18},{20,21},{21,20},{22,23},{23,22},{2... | collective-permute-start | bytes 491528 | tf_op jit(solution)/shard_map/ppermute | solution.py:294
  330.2 10.0 %collective-permute-start.20 = (bf16[16,1280]{1,0:T(8,128)(2,1)S(1)}, bf16[16,1280]{1,0:T(8,128)(2,1)S(1)}, u32[]{:S(2)}, u32[]{:S(2)}) collective-permute-start(bf16[16,1280]{1,0:T(8,128)(2,1)S(1)} %get-tuple-element.36), channel_id=1, source_target_pairs={{0,0},{1,1},{2,32},{3,33},{4,64},{5,65},{6,96},{7,97},{32,2},{33,3... | collective-permute-start | bytes 122888 | tf_op jit(solution)/shard_map/ppermute | solution.py:411
  334.1 7.7 %collective-permute-start.21 = (bf16[16,1280]{1,0:T(8,128)(2,1)S(1)}, bf16[16,1280]{1,0:T(8,128)(2,1)S(1)}, u32[]{:S(2)}, u32[]{:S(2)}) collective-permute-start(bf16[16,1280]{1,0:T(8,128)(2,1)S(1)} %get-tuple-element.39), channel_id=1, source_target_pairs={{0,32},{1,33},{2,64},{3,65},{4,96},{5,97},{6,0},{7,1},{32,34},{33,... | collective-permute-start | bytes 122888 | tf_op jit(solution)/shard_map/ppermute | solution.py:411
  337.8 6.1 %collective-permute-start.22 = (bf16[16,1280]{1,0:T(8,128)(2,1)S(1)}, bf16[16,1280]{1,0:T(8,128)(2,1)S(1)}, u32[]{:S(2)}, u32[]{:S(2)}) collective-permute-start(bf16[16,1280]{1,0:T(8,128)(2,1)S(1)} %get-tuple-element.38), channel_id=1, source_target_pairs={{0,64},{1,65},{2,96},{3,97},{4,0},{5,1},{6,32},{7,33},{32,66},{33,... | collective-permute-start | bytes 122888 | tf_op jit(solution)/shard_map/ppermute | solution.py:411
  339.9 5.2 %collective-permute-start.23 = (bf16[16,1280]{1,0:T(8,128)(2,1)S(1)}, bf16[16,1280]{1,0:T(8,128)(2,1)S(1)}, u32[]{:S(2)}, u32[]{:S(2)}) collective-permute-start(bf16[16,1280]{1,0:T(8,128)(2,1)S(1)} %get-tuple-element.37), channel_id=1, source_target_pairs={{0,96},{1,97},{2,0},{3,1},{4,32},{5,33},{6,64},{7,65},{32,98},{33,... | collective-permute-start | bytes 122888 | tf_op jit(solution)/shard_map/ppermute | solution.py:411
  (8 other events, 33.4 us)

commit v2 on v1

--- a/solution.py
+++ b/solution.py
@@ -58,9 +58,12 @@
     return pl.BlockSpec(memory_space=pltpu.SMEM)
 
 
-def encoder_kernel(
-    frames_ref, gain_ref, bias_ref, up_ref, up_bias_ref, down_ref, out_ref, up_v, down_v, rows, sems
-):
+def block_at(index, depth):
+    return pl.ds(pl.multiple_of(index * depth, depth), depth)
+
+
+def encoder_kernel(place, frames_ref, gain_ref, bias_ref, up_ref, up_bias_ref, down_ref, *rest):
+    outs, (up_v, down_v, rows, sems) = rest[:STACK], rest[STACK:]
     copies = [
         pltpu.make_async_copy(up_ref, up_v, sems.at[0]),
         pltpu.make_async_copy(down_ref, down_v, sems.at[1]),
@@ -79,22 +82,23 @@
     active = exact_gelu(raised).astype(BF)
     copies[1].wait()
     lowered = dot(active, down_v[...])
-    group, count = out_ref.shape[0], out_ref.shape[1]
+    count = outs[0].shape[0]
     for c in range(rows.shape[0]):
         cols = slice(c * LANES, (c + 1) * LANES)
         rows[c] = lowered[:, cols]
-        for j in range(group):
-            out_ref[j, :, cols] = rows[c, pl.ds(j, count, stride=group), :].astype(BF)
-
-
-def encoder(frames, gain, bias, up, up_bias, down):
+        for step in range(STACK):
+            j = lax.rem(place[0] + step, STACK)
+            outs[step][:, cols] = rows[c, pl.ds(j, count, stride=STACK), :].astype(BF)
+
+
+def encoder(place, frames, gain, bias, up, up_bias, down):
     count, width = frames.shape
     hidden = up.shape[1]
     return pl.pallas_call(
         encoder_kernel,
-        out_shape=jax.ShapeDtypeStruct((STACK, count // STACK, width), BF),
-        in_specs=[vmem(), vmem(), vmem(), anywhere(), vmem(), anywhere()],
-        out_specs=vmem(),
+        out_shape=[jax.ShapeDtypeStruct((count // STACK, width), BF)] * STACK,
+        in_specs=[smem(), vmem(), vmem(), vmem(), anywhere(), vmem(), anywhere()],
+        out_specs=[vmem()] * STACK,
         scratch_shapes=[
             pltpu.VMEM((width, hidden), BF),
             pltpu.VMEM((hidden, width), BF),
@@ -108,46 +112,49 @@
             transcendentals=count * hidden,
         ),
         name="encoder_units",
-    )(frames, gain, bias, up, up_bias, down)
-
-
-def adapter_kernel(x_ref, in0, in1, out0, out1, part_ref, win, wout, sems):
-    in_copies = [
-        pltpu.make_async_copy(ref, win.at[i], sems.at[i]) for i, ref in enumerate((in0, in1))
-    ]
-    out_copies = [
-        pltpu.make_async_copy(ref, wout.at[i], sems.at[2 + i])
-        for i, ref in enumerate((out0, out1))
-    ]
-    for copy in in_copies + out_copies:
+    )(place, frames, gain, bias, up, up_bias, down)
+
+
+def adapter_kernel(place, x0, x1, x2, x3, in0, in1, out0, out1, *rest):
+    xs, outs, (win, wout, sems) = (x0, x1, x2, x3), rest[:4], rest[4:]
+    blocks, depth = len(xs), x0.shape[1]
+    units = in0.shape[0]
+    made = [[], []]
+    for k in range(blocks):
+        sources = lax.rem(place[0] + blocks - k, blocks), lax.rem(place[0] + k, blocks)
+        for kind, pair in enumerate(((in0, in1), (out0, out1))):
+            part = block_at(sources[kind], depth)
+            for i in range(2):
+                target = (win, wout)[kind].at[k, pl.ds(i * units, units), :]
+                made[kind].append(
+                    pltpu.make_async_copy(pair[i].at[:, part], target, sems.at[kind, i, k])
+                )
+    for copy in made[0] + made[1]:
         copy.start()
-    blocks, _, depth = x_ref.shape
-    lifted = []
-    for i in range(2):
-        in_copies[i].wait()
-        total = sum(
-            dot_t(x_ref[b], win[i, :, b * depth : (b + 1) * depth]) for b in range(blocks)
-        )
-        lifted.append(exact_gelu(total).astype(BF))
-    for copy in out_copies:
-        copy.wait()
-    for b in range(blocks):
-        cols = slice(b * depth, (b + 1) * depth)
-        part_ref[b] = sum(dot(lifted[i], wout[i, :, cols]) for i in range(2)).astype(BF)
-
-
-def adapter(blocks, in_pair, out_pair):
+    total = 0.0
+    for k in range(blocks):
+        for copy in made[0][2 * k : 2 * k + 2]:
+            copy.wait()
+        total += dot_t(xs[k][...], win[k])
+    lifted = exact_gelu(total).astype(BF)
+    for k in range(blocks):
+        for copy in made[1][2 * k : 2 * k + 2]:
+            copy.wait()
+        outs[k][...] = dot(lifted, wout[k]).astype(BF)
+
+
+def adapter(place, blocks, in_pair, out_pair):
     units, width = in_pair[0].shape
-    rows = blocks.shape[1]
+    count, (rows, depth) = len(blocks), blocks[0].shape
     return pl.pallas_call(
         adapter_kernel,
-        out_shape=jax.ShapeDtypeStruct(blocks.shape, BF),
-        in_specs=[vmem()] + [anywhere()] * 4,
-        out_specs=vmem(),
+        out_shape=[jax.ShapeDtypeStruct((rows, depth), BF)] * count,
+        in_specs=[smem()] + [vmem()] * count + [anywhere()] * 4,
+        out_specs=[vmem()] * count,
         scratch_shapes=[
-            pltpu.VMEM((2, units, width), BF),
-            pltpu.VMEM((2, units, width), BF),
-            pltpu.SemaphoreType.DMA((4,)),
+            pltpu.VMEM((count, 2 * units, depth), BF),
+            pltpu.VMEM((count, 2 * units, depth), BF),
+            pltpu.SemaphoreType.DMA((2, 2, count)),
         ],
         compiler_params=pltpu.CompilerParams(vmem_limit_bytes=56 << 20),
         cost_estimate=pl.CostEstimate(
@@ -156,13 +163,18 @@
             transcendentals=2 * rows * units,
         ),
         name="adapter_units",
-    )(blocks, *in_pair, *out_pair)
+    )(place, *blocks, *in_pair, *out_pair)
 
 
 def layer_kernel(
-    which, x_ref, gain0, gain1, mask_ref, q0, k0, v0, o0, q1, k1, v1, o1, out_ref, wq, wk, wv, wo, sems
+    which, x_hbm, gain0, gain1, mask_ref, q0, k0, v0, o0, q1, k1, v1, o1, out_ref, x_ref, wq, wk, wv, wo, sems
 ):
     blocks, rows, depth = x_ref.shape
+    x_copies = [
+        pltpu.make_async_copy(x_hbm.at[b], x_ref.at[b], sems.at[4, b]) for b in range(blocks)
+    ]
+    for copy in x_copies:
+        copy.start()
 
     def copies(q_ref, k_ref, v_ref, o_ref):
         made = []
@@ -195,6 +207,8 @@
         begin((q1, k1, v1, o1))
 
     waits = copies(q0, k0, v0, o0)
+    for copy in x_copies:
+        copy.wait()
     squares = sum(
         jnp.sum(jnp.square(x_ref[b].astype(F32)), axis=-1, keepdims=True) for b in range(blocks)
     )
@@ -231,14 +245,15 @@
     return pl.pallas_call(
         layer_kernel,
         out_shape=jax.ShapeDtypeStruct(blocks.shape, BF),
-        in_specs=[smem(), vmem(), vmem(), vmem(), vmem()] + [anywhere()] * 8,
+        in_specs=[smem(), anywhere(), vmem(), vmem(), vmem()] + [anywhere()] * 8,
         out_specs=vmem(),
         scratch_shapes=[
+            pltpu.VMEM(blocks.shape, BF),
             pltpu.VMEM((count, depth, q_cols), BF),
             pltpu.VMEM((count, depth, kv_cols), BF),
             pltpu.VMEM((count, depth, kv_cols), BF),
             pltpu.VMEM((count, q_cols, depth), BF),
-            pltpu.SemaphoreType.DMA((4, count)),
+            pltpu.SemaphoreType.DMA((5, count)),
         ],
         compiler_params=pltpu.CompilerParams(vmem_limit_bytes=56 << 20),
         cost_estimate=pl.CostEstimate(
@@ -301,6 +316,19 @@
     def z_sum(partial):
         return jnp.sum(z_all_to_all(partial).astype(F32), axis=0)
 
+    def z_move(value, step):
+        pairs = [
+            (2 * z + y, 2 * ((z + step) % z_count) + y) for z in range(z_count) for y in range(2)
+        ]
+        return lax.ppermute(value, "tp", pairs)
+
+    def z_scatter(parts):
+        moved = [z_move(parts[step], step) for step in range(1, z_count)]
+        return sum(part.astype(F32) for part in [parts[0]] + moved)
+
+    def z_spread(shard):
+        return [shard] + [z_move(shard, step) for step in range(1, z_count)]
+
     def z_gather(shard):
         return z_all_to_all(jnp.broadcast_to(shard[None], (z_count,) + shard.shape))
 
@@ -310,36 +338,33 @@
     both = ((0, 0, 1), (1, 1, 1))
 
     own_layer = (q_weight[0], k_weight[0], v_weight[0], o_weight[0])
-    other_layer = tuple(chip_swap(weight) for weight in own_layer)
-    gains = [g.astype(F32).reshape(1, -1) for g in (attn_gain[0], chip_swap(attn_gain[0]))]
+    early = [chip_swap(own_layer[0]), chip_swap(own_layer[3])]
     in_pair = (adapt_in.T, chip_swap(adapt_in.T))
     out_pair = (adapt_out, chip_swap(adapt_out))
 
     width = frames.shape[3]
     tokens = frames.shape[2] // STACK
-    partial_down = encoder(frames[0, 0], ln_gain, ln_bias, enc_up, up_bias, enc_down)
+    place = z_index.astype(jnp.int32).reshape(1)
+    partial_down = encoder(place, frames[0, 0], ln_gain, ln_bias, enc_up, up_bias, enc_down)
     own_frames = lax.dynamic_index_in_dim(
         frames[0, 0].reshape(tokens, STACK, width), z_index, 1, keepdims=False
     )
     extra = at_first(own_frames.astype(F32) + down_bias.astype(F32)[None])
-    share = (z_sum(partial_down) + extra).astype(BF)
-    here = share.astype(F32) + y_move(share, both).astype(F32)
-    there = y_move(share, ((0, 1, 0), (1, 0, 0))).astype(F32) + y_move(
-        share, ((0, 1, 1), (1, 0, 1))
-    ).astype(F32)
-    here, in_pair, out_pair, other_layer, gains = lax.optimization_barrier(
-        (here, in_pair, out_pair, other_layer, gains)
-    )
+    share = (z_scatter(partial_down) + extra).astype(BF)
+    here = (share.astype(F32) + y_move(share, both).astype(F32)).astype(BF)
+    here, in_pair, out_pair, early, own_layer = lax.optimization_barrier(
+        (here, in_pair, out_pair, early, own_layer)
+    )
+    gains = [g.astype(F32).reshape(1, -1) for g in (attn_gain[0], chip_swap(attn_gain[0]))]
+    other_layer = (early[0], chip_swap(own_layer[1]), chip_swap(own_layer[2]), early[1])
+    there = y_move(here, ((0, 1, 1), (1, 0, 1)))
     encoded = jnp.where(high == 0, jnp.stack([here, there]), jnp.stack([there, here]))
-    encoded = encoded.astype(BF).reshape(2 * tokens, width)
-
-    share = z_sum(adapter(z_gather(encoded), in_pair, out_pair)).astype(BF)
-    moved = (
-        y_move(share, both),
-        y_move(share, ((1, 0, 0),)),
-        y_move(share, ((1, 0, 1),)),
-    )
-    hidden = (share.astype(F32) + sum(part.astype(F32) for part in moved)).astype(BF)
+    encoded = encoded.reshape(2 * tokens, width)
+
+    share = z_scatter(adapter(place, z_spread(encoded), in_pair, out_pair)).astype(BF)
+    summed = share.astype(F32) + y_move(share, both).astype(F32)
+    from_high = y_move(summed.astype(BF), ((1, 0, 1),))
+    hidden = (summed + from_high.astype(F32)).astype(BF)
 
     ends = jnp.cumsum(lengths[pool_index], axis=1, dtype=jnp.int32)
     token_ids = jnp.arange(tokens, dtype=jnp.int32)

time: 347 us -> 324 us (0.934)
  blocking collectives: 109 us -> 64.6 us
  waiting for transfers between devices: 120 us -> 141 us
    all_to_all x6 -> x4, blocking collectives: 109 us -> 64.6 us  [z_all_to_all(): lax.all_to_all(value, 'tp', split_axis=0, concat_axis=0, tiled=True, axis...]
    ppermute x0 -> x9, waiting for transfers between devices: none -> 37.2 us  [z_move(): return lax.ppermute(value, 'tp', pairs)]
    ppermute x0 -> x9, starting transfers between devices: none -> 12.7 us  [z_move(): return lax.ppermute(value, 'tp', pairs)]
    all_to_all x5 -> x4, waiting for transfers between devices: 59 us -> 47.6 us  [z_all_to_all(): lax.all_to_all(value, 'tp', split_axis=0, concat_axis=0, tiled=True, axis...]
    ppermute x13 -> x11, starting transfers between devices: 17.7 us -> 12.2 us  [y_move(): return lax.ppermute(value, ('section', 'tp'), pairs)]
    ppermute x7, waiting for transfers between devices: 5.35 us -> 0.02 us  [chip_swap(): lax.ppermute(value, 'section', [(i, i ^ 1) for i in range(section_count)])]
    all_to_all x5 -> x4, starting transfers between devices: 20.1 us -> 16.4 us  [z_all_to_all(): lax.all_to_all(value, 'tp', split_axis=0, concat_axis=0, tiled=True, axis...]
    ppermute x13 -> x11, waiting for transfers between devices: 50.2 us -> 51.1 us  [y_move(): return lax.ppermute(value, ('section', 'tp'), pairs)]
  transfers between devices with their start and end apart: 29 -> 35, of which waited for: 22 -> 26; matrix products, arithmetic and copies ran while one was open for 3% -> 2% of each run, Pallas kernels for 1% -> 2%
where the time goes in v2:
time: 324 us; the launch traced here: 323 us
  waiting for transfers between devices  141 us (44%)
  blocking collectives  64.6 us (20%)
  starting transfers between devices  51.7 us (16%)
  Pallas kernels  46.8 us (14%)
  other arithmetic  8.93 us (3%)
  local copies, waits for them, and re-layouts  8.82 us (3%)
    all_to_all x4, blocking collectives, z_all_to_all(): lax.all_to_all(value, 'tp', split_axis=0, concat_axis=0, tiled=True, axis...  64.6 us
    ppermute x11, waiting for transfers between devices, y_move(): return lax.ppermute(value, ('section', 'tp'), pairs)  51.1 us
    all_to_all x4, waiting for transfers between devices, z_all_to_all(): lax.all_to_all(value, 'tp', split_axis=0, concat_axis=0, tiled=True, axis...  47.6 us
    ppermute x9, waiting for transfers between devices, z_move(): return lax.ppermute(value, 'tp', pairs)  37.2 us
    pallas_call x4, Pallas kernels, decoder_layer(): pl.pallas_call(layer_kernel, out_shape=jax.ShapeDtypeStruct(blocks.shape,...  34.5 us
    all_to_all x4, starting transfers between devices, z_all_to_all(): lax.all_to_all(value, 'tp', split_axis=0, concat_axis=0, tiled=True, axis...  16.4 us
    ppermute x9, starting transfers between devices, z_move(): return lax.ppermute(value, 'tp', pairs)  12.7 us
    ppermute x11, starting transfers between devices, y_move(): return lax.ppermute(value, ('section', 'tp'), pairs)  12.2 us
  transfers between devices with their start and end apart: 35, of which 26 were waited for; matrix products, arithmetic and copies ran while one was open for 2% of the time, Pallas kernels for 2%

profile of v2, /device:TPU:30, one launch (start us, length us, event | category | flops | bytes accessed | tf_op | source)
XLA Modules:
  0.0 322.7 jit_solution(8794383818993725289)
XLA Ops:
  0.5 5.4 %encoder_units.1 = (bf16[64,1280]{1,0:T(8,128)(2,1)}, bf16[64,1280]{1,0:T(8,128)(2,1)}, bf16[64,1280]{1,0:T(8,128)(2,1)}, bf16[64,1280]{1,0:T(8,128)(2,1)}) custom-call(s32[1]{0:T(128)} %bitcast.9.place, bf16[256,1280]{1,0:T(8,128)(2,1)} %bitcast.88, bf16[1280]{0:T(1024)(128)(2,1)} %gain_ref.1, bf16[1280]{0:T(1024)(128)(2,1)} %bias_ref.1, ...), custom_call_target="tpu_custom_call" | custom-call | flops 838860800 | bytes 3276800 | tf_op jit(solution)/shard_map/encoder_units/pallas_call | solution.py:97
  8.4 6.2 %collective-permute-done = bf16[64,1280]{1,0:T(8,128)(2,1)S(1)} collective-permute-done((bf16[64,1280]{1,0:T(8,128)(2,1)}, bf16[64,1280]{1,0:T(8,128)(2,1)S(1)}, u32[]{:S(2)}, u32[]{:S(2)}) %collective-permute-start) | collective-permute-done | bytes 163872 | tf_op jit(solution)/shard_map/ppermute | solution.py:323
  16.4 5.5 %collective-permute-done.1 = bf16[64,1280]{1,0:T(8,128)(2,1)S(1)} collective-permute-done((bf16[64,1280]{1,0:T(8,128)(2,1)}, bf16[64,1280]{1,0:T(8,128)(2,1)S(1)}, u32[]{:S(2)}, u32[]{:S(2)}) %collective-permute-start.1) | collective-permute-done | bytes 163872 | tf_op jit(solution)/shard_map/ppermute | solution.py:323
  23.7 3.7 %collective-permute-done.2 = bf16[64,1280]{1,0:T(8,128)(2,1)S(1)} collective-permute-done((bf16[64,1280]{1,0:T(8,128)(2,1)}, bf16[64,1280]{1,0:T(8,128)(2,1)S(1)}, u32[]{:S(2)}, u32[]{:S(2)}) %collective-permute-start.2) | collective-permute-done | bytes 163872 | tf_op jit(solution)/shard_map/ppermute | solution.py:323
  28.4 4.6 %collective-permute-done.3 = bf16[64,1280]{1,0:T(8,128)(2,1)S(1)} collective-permute-done((bf16[64,1280]{1,0:T(8,128)(2,1)S(1)}, bf16[64,1280]{1,0:T(8,128)(2,1)S(1)}, u32[]{:S(2)}, u32[]{:S(2)}) %collective-permute-start.3) | collective-permute-done | bytes 163872 | tf_op jit(solution)/shard_map/ppermute | solution.py:309
  33.3 6.3 %collective-permute-done.8 = bf16[64,1280]{1,0:T(8,128)(2,1)S(1)} collective-permute-done((bf16[64,1280]{1,0:T(8,128)(2,1)S(1)}, bf16[64,1280]{1,0:T(8,128)(2,1)S(1)}, u32[]{:S(2)}, u32[]{:S(2)}) %collective-permute-start.8) | collective-permute-done | bytes 163872 | tf_op jit(solution)/shard_map/ppermute | solution.py:309
  43.3 6.3 %collective-permute-done.10.x2 = bf16[128,1280]{1,0:T(8,128)(2,1)S(1)} collective-permute-done((bf16[128,1280]{1,0:T(8,128)(2,1)S(1)}, bf16[128,1280]{1,0:T(8,128)(2,1)S(1)}, u32[]{:S(2)}, u32[]{:S(2)}) %collective-permute-start.10) | collective-permute-done | bytes 327712 | tf_op jit(solution)/shard_map/ppermute | solution.py:323
  54.0 6.9 %adapter_units.1 = (bf16[128,1280]{1,0:T(8,128)(2,1)}, bf16[128,1280]{1,0:T(8,128)(2,1)}, bf16[128,1280]{1,0:T(8,128)(2,1)}, bf16[128,1280]{1,0:T(8,128)(2,1)}) custom-call(s32[1]{0:T(128)} %bitcast.9.place, bf16[128,1280]{1,0:T(8,128)(2,1)} %bitcast.94, bf16[128,1280]{1,0:T(8,128)(2,1)} %copy-done.9, bf16[128,1280]{1,0:T(8,128)(2,1)} %copy-done.7, ...), custom_call_target="tpu_custom_call" | custom-call | flops 838860800 | bytes 6553600 | tf_op jit(solution)/shard_map/adapter_units/pallas_call | solution.py:149
  61.4 3.6 %collective-permute-start.13 = (bf16[128,1280]{1,0:T(8,128)(2,1)}, bf16[128,1280]{1,0:T(8,128)(2,1)S(1)}, u32[]{:S(2)}, u32[]{:S(2)}) collective-permute-start(bf16[128,1280]{1,0:T(8,128)(2,1)} %get-tuple-element.35), channel_id=1, source_target_pairs={{0,4},{1,5},{2,6},{3,7},{4,0},{5,1},{6,2},{7,3},{8,12},{9,13},{10,... | collective-permute-start | bytes 983048 | tf_op jit(solution)/shard_map/ppermute | solution.py:323
  65.0 7.8 %collective-permute-done.12 = bf16[128,1280]{1,0:T(8,128)(2,1)S(1)} collective-permute-done((bf16[128,1280]{1,0:T(8,128)(2,1)}, bf16[128,1280]{1,0:T(8,128)(2,1)S(1)}, u32[]{:S(2)}, u32[]{:S(2)}) %collective-permute-start.12) | collective-permute-done | bytes 327712 | tf_op jit(solution)/shard_map/ppermute | solution.py:323
  72.7 4.3 %collective-permute-done.13 = bf16[128,1280]{1,0:T(8,128)(2,1)S(1)} collective-permute-done((bf16[128,1280]{1,0:T(8,128)(2,1)}, bf16[128,1280]{1,0:T(8,128)(2,1)S(1)}, u32[]{:S(2)}, u32[]{:S(2)}) %collective-permute-start.13) | collective-permute-done | bytes 327712 | tf_op jit(solution)/shard_map/ppermute | solution.py:323
  78.4 7.1 %collective-permute-done.15 = bf16[128,1280]{1,0:T(8,128)(2,1)S(1)} collective-permute-done((bf16[128,1280]{1,0:T(8,128)(2,1)S(1)}, bf16[128,1280]{1,0:T(8,128)(2,1)S(1)}, u32[]{:S(2)}, u32[]{:S(2)}) %collective-permute-start.15) | collective-permute-done | bytes 327712 | tf_op jit(solution)/shard_map/ppermute | solution.py:309
  88.6 4.0 %collective-permute-done.16 = bf16[128,1280]{1,0:T(8,128)(2,1)S(1)} collective-permute-done((bf16[128,1280]{1,0:T(8,128)(2,1)S(1)}, bf16[128,1280]{1,0:T(8,128)(2,1)S(1)}, u32[]{:S(2)}, u32[]{:S(2)}) %collective-permute-start.16) | collective-permute-done | bytes 327712 | tf_op jit(solution)/shard_map/ppermute | solution.py:309
  93.9 5.6 %all-to-all-start = ((bf16[4,128,1280]{2,1,0:T(8,128)(2,1)}), bf16[4,128,1280]{2,1,0:T(8,128)(2,1)}, u32[]{:S(2)}, u32[]{:S(2)}) async-start(bf16[4,128,1280]{2,1,0:T(8,128)(2,1)} %broadcast_in_dim.36), calls=%async_computation | async-start | bytes 2621440 | tf_op jit(solution)/shard_map/all_to_all | solution.py:312
  102.0 12.9 %all-to-all-done.x_hbm = bf16[4,128,1280]{2,1,0:T(8,128)(2,1)} async-done(((bf16[4,128,1280]{2,1,0:T(8,128)(2,1)}), bf16[4,128,1280]{2,1,0:T(8,128)(2,1)}, u32[]{:S(2)}, u32[]{:S(2)}) %all-to-all-start) | async-done | bytes 1310752 | tf_op jit(solution)/shard_map/all_to_all | solution.py:312
  114.9 8.6 %decoder_layer.4 = bf16[4,128,1280]{2,1,0:T(8,128)(2,1)} custom-call(s32[1]{0:T(128)} %bitcast.8.which, bf16[4,128,1280]{2,1,0:T(8,128)(2,1)} %all-to-all-done.x_hbm, f32[1,5120]{1,0:T(1,128)} %get-tuple-element.57.gain0, f32[1,5120]{1,0:T(1,128)} %bitcast.96, f32[128,128]{1,0:T(8,128)} %fusion.9.mask_ref, bf16[5120,512]{1,0:T(8,128)(2,1)} %bitcast.68, ...), custom_call_target="tpu_custom_call" | custom-call | flops 1677721600 | bytes 13107200 | tf_op jit(solution)/shard_map/decoder_layer/pallas_call | solution.py:245
  123.5 17.5 %all_to_all.40 = bf16[4,128,1280]{2,1,0:T(8,128)(2,1)S(1)} all-to-all(bf16[4,128,1280]{2,1,0:T(8,128)(2,1)} %decoder_layer.4), channel_id=1, replica_groups={{0,2,4,6},{1,3,5,7},{8,10,12,14},{9,11,13,15},{16,18,20,22},{17,19,21,2..., dimensions={0} | all-to-all | bytes 2621440 | tf_op jit(solution)/shard_map/all_to_all | solution.py:312
  141.4 7.0 %collective-permute-done.20 = bf16[128,1280]{1,0:T(8,128)(2,1)S(1)} collective-permute-done((bf16[128,1280]{1,0:T(8,128)(2,1)S(1)}, bf16[128,1280]{1,0:T(8,128)(2,1)S(1)}, u32[]{:S(2)}, u32[]{:S(2)}) %collective-permute-start.20) | collective-permute-done | bytes 327712 | tf_op jit(solution)/shard_map/ppermute | solution.py:309
  153.3 12.3 %all-to-all-done.2.x_hbm = bf16[4,128,1280]{2,1,0:T(8,128)(2,1)S(1)} async-done(((bf16[4,128,1280]{2,1,0:T(8,128)(2,1)}), bf16[4,128,1280]{2,1,0:T(8,128)(2,1)S(1)}, u32[]{:S(2)}, u32[]{:S(2)}) %all-to-all-start.2) | async-done | bytes 1310752 | tf_op jit(solution)/shard_map/all_to_all | solution.py:312
  166.6 8.6 %decoder_layer.5 = bf16[4,128,1280]{2,1,0:T(8,128)(2,1)} custom-call(s32[1]{0:T(128)} %bitcast.7.which, bf16[4,128,1280]{2,1,0:T(8,128)(2,1)} %copy-done.3, f32[1,5120]{1,0:T(1,128)} %get-tuple-element.57.gain0, f32[1,5120]{1,0:T(1,128)} %bitcast.97, f32[128,128]{1,0:T(8,128)} %fusion.9.mask_ref, bf16[5120,512]{1,0:T(8,128)(2,1)} %bitcast.69, ...), custom_call_target="tpu_custom_call" | custom-call | flops 1677721600 | bytes 13107200 | tf_op jit(solution)/shard_map/decoder_layer/pallas_call | solution.py:245
  175.2 15.8 %all_to_all.41 = bf16[4,128,1280]{2,1,0:T(8,128)(2,1)S(1)} all-to-all(bf16[4,128,1280]{2,1,0:T(8,128)(2,1)} %decoder_layer.5), channel_id=1, replica_groups={{0,2,4,6},{1,3,5,7},{8,10,12,14},{9,11,13,15},{16,18,20,22},{17,19,21,2..., dimensions={0} | all-to-all | bytes 2621440 | tf_op jit(solution)/shard_map/all_to_all | solution.py:312
  193.9 8.0 %collective-permute-done.21 = bf16[128,1280]{1,0:T(8,128)(2,1)S(1)} collective-permute-done((bf16[128,1280]{1,0:T(8,128)(2,1)S(1)}, bf16[128,1280]{1,0:T(8,128)(2,1)S(1)}, u32[]{:S(2)}, u32[]{:S(2)}) %collective-permute-start.21) | collective-permute-done | bytes 327712 | tf_op jit(solution)/shard_map/ppermute | solution.py:309
  205.5 15.5 %all_to_all.42.x_hbm = bf16[4,128,1280]{2,1,0:T(8,128)(2,1)} all-to-all(bf16[4,128,1280]{2,1,0:T(8,128)(2,1)S(1)} %broadcast_in_dim.38), channel_id=1, replica_groups={{0,2,4,6},{1,3,5,7},{8,10,12,14},{9,11,13,15},{16,18,20,22},{17,19,21,2..., dimensions={0} | all-to-all | bytes 2621440 | tf_op jit(solution)/shard_map/all_to_all | solution.py:312
  220.9 8.6 %decoder_layer.6 = bf16[4,128,1280]{2,1,0:T(8,128)(2,1)} custom-call(s32[1]{0:T(128)} %bitcast.8.which, bf16[4,128,1280]{2,1,0:T(8,128)(2,1)} %all_to_all.42.x_hbm, f32[1,5120]{1,0:T(1,128)} %get-tuple-element.57.gain0, f32[1,5120]{1,0:T(1,128)} %bitcast.98, f32[128,128]{1,0:T(8,128)} %fusion.9.mask_ref, bf16[5120,512]{1,0:T(8,128)(2,1)} %bitcast.70, ...), custom_call_target="tpu_custom_call" | custom-call | flops 1677721600 | bytes 13107200 | tf_op jit(solution)/shard_map/decoder_layer/pallas_call | solution.py:245
  229.6 15.8 %all_to_all.43 = bf16[4,128,1280]{2,1,0:T(8,128)(2,1)S(1)} all-to-all(bf16[4,128,1280]{2,1,0:T(8,128)(2,1)} %decoder_layer.6), channel_id=1, replica_groups={{0,2,4,6},{1,3,5,7},{8,10,12,14},{9,11,13,15},{16,18,20,22},{17,19,21,2..., dimensions={0} | all-to-all | bytes 2621440 | tf_op jit(solution)/shard_map/all_to_all | solution.py:312
  246.9 6.0 %collective-permute-done.23 = bf16[128,1280]{1,0:T(8,128)(2,1)S(1)} collective-permute-done((bf16[128,1280]{1,0:T(8,128)(2,1)S(1)}, bf16[128,1280]{1,0:T(8,128)(2,1)S(1)}, u32[]{:S(2)}, u32[]{:S(2)}) %collective-permute-start.23) | collective-permute-done | bytes 327712 | tf_op jit(solution)/shard_map/ppermute | solution.py:309
  254.1 3.7 %all-to-all-start.6 = ((bf16[4,128,1280]{2,1,0:T(8,128)(2,1)}), bf16[4,128,1280]{2,1,0:T(8,128)(2,1)S(1)}, u32[]{:S(2)}, u32[]{:S(2)}) async-start(bf16[4,128,1280]{2,1,0:T(8,128)(2,1)} %broadcast_in_dim.39), calls=%async_computation.6 | async-start | bytes 2621440 | tf_op jit(solution)/shard_map/all_to_all | solution.py:312
  259.5 10.5 %all-to-all-done.6.x_hbm = bf16[4,128,1280]{2,1,0:T(8,128)(2,1)S(1)} async-done(((bf16[4,128,1280]{2,1,0:T(8,128)(2,1)}), bf16[4,128,1280]{2,1,0:T(8,128)(2,1)S(1)}, u32[]{:S(2)}, u32[]{:S(2)}) %all-to-all-start.6) | async-done | bytes 1310752 | tf_op jit(solution)/shard_map/all_to_all | solution.py:312
  271.1 8.6 %decoder_layer.7 = bf16[4,128,1280]{2,1,0:T(8,128)(2,1)} custom-call(s32[1]{0:T(128)} %bitcast.7.which, bf16[4,128,1280]{2,1,0:T(8,128)(2,1)} %copy-done.2, f32[1,5120]{1,0:T(1,128)} %get-tuple-element.57.gain0, f32[1,5120]{1,0:T(1,128)} %bitcast.99, f32[128,128]{1,0:T(8,128)} %fusion.9.mask_ref, bf16[5120,512]{1,0:T(8,128)(2,1)} %bitcast.71, ...), custom_call_target="tpu_custom_call" | custom-call | flops 1677721600 | bytes 13107200 | tf_op jit(solution)/shard_map/decoder_layer/pallas_call | solution.py:245
  283.6 12.0 %all-to-all-done.7 = bf16[4,128,1280]{2,1,0:T(8,128)(2,1)S(1)} async-done(((bf16[4,128,1280]{2,1,0:T(8,128)(2,1)}), bf16[4,128,1280]{2,1,0:T(8,128)(2,1)S(1)}, u32[]{:S(2)}, u32[]{:S(2)}) %all-to-all-start.7) | async-done | bytes 1310752 | tf_op jit(solution)/shard_map/all_to_all | solution.py:312
  303.6 4.1 %collective-permute-done.26 = bf16[4,16,1280]{2,1,0:T(8,128)(2,1)S(1)} collective-permute-done((bf16[4,16,1280]{2,1,0:T(8,128)(2,1)S(1)}, bf16[4,16,1280]{2,1,0:T(8,128)(2,1)S(1)}, u32[]{:S(2)}, u32[]{:S(2)}) %collective-permute-start.26) | collective-permute-done | bytes 163872 | tf_op jit(solution)/shard_map/ppermute | solution.py:309
  310.5 5.0 %collective-permute-start.28 = (bf16[16,1280]{1,0:T(8,128)(2,1)S(1)}, bf16[16,1280]{1,0:T(8,128)(2,1)S(1)}, u32[]{:S(2)}, u32[]{:S(2)}) collective-permute-start(bf16[16,1280]{1,0:T(8,128)(2,1)S(1)} %get-tuple-element.55), channel_id=1, source_target_pairs={{0,32},{1,33},{2,64},{3,65},{4,96},{5,97},{6,0},{7,1},{32,34},{33,... | collective-permute-start | bytes 122888 | tf_op jit(solution)/shard_map/ppermute | solution.py:436
  (136 shorter events, 64.5 us)
Async XLA Ops:
  0.0 33.0 %collective-permute-start.6 = (bf16[5120,512]{1,0:T(8,128)(2,1)}, bf16[5120,512]{1,0:T(8,128)(2,1)}, u32[]{:S(2)}, u32[]{:S(2)}) collective-permute-start(bf16[5120,512]{1,0:T(8,128)(2,1)} %bitcast.67), channel_id=1, source_target_pairs={{0,8},{8,0},{16,24},{24,16},{1,9},{9,1},{17,25},{25,17},{2,10},{10... | collective-permute-start | bytes 15728648 | tf_op jit(solution)/shard_map/ppermute | solution.py:296
  0.0 33.0 %collective-permute-start.7 = (bf16[512,5120]{1,0:T(8,128)(2,1)}, bf16[512,5120]{1,0:T(8,128)(2,1)}, u32[]{:S(2)}, u32[]{:S(2)}) collective-permute-start(bf16[512,5120]{1,0:T(8,128)(2,1)} %bitcast.72), channel_id=1, source_target_pairs={{0,8},{8,0},{16,24},{24,16},{1,9},{9,1},{17,25},{25,17},{2,10},{10... | collective-permute-start | bytes 15728648 | tf_op jit(solution)/shard_map/ppermute | solution.py:296
  5.9 8.7 %collective-permute-start = (bf16[64,1280]{1,0:T(8,128)(2,1)}, bf16[64,1280]{1,0:T(8,128)(2,1)S(1)}, u32[]{:S(2)}, u32[]{:S(2)}) collective-permute-start(bf16[64,1280]{1,0:T(8,128)(2,1)} %get-tuple-element.25), channel_id=1, source_target_pairs={{0,2},{1,3},{2,4},{3,5},{4,6},{5,7},{6,0},{7,1},{8,10},{9,11},{10,... | collective-permute-start | bytes 491528 | tf_op jit(solution)/shard_map/ppermute | solution.py:323
  7.9 25.1 %collective-permute-start.4 = (bf16[160,5120]{1,0:T(8,128)(2,1)S(1)}, bf16[160,5120]{1,0:T(8,128)(2,1)}, u32[]{:S(2)}, u32[]{:S(2)}) collective-permute-start(bf16[160,5120]{1,0:T(8,128)(2,1)S(1)} %bitcast.90), channel_id=1, source_target_pairs={{0,8},{8,0},{16,24},{24,16},{1,9},{9,1},{17,25},{25,17},{2,10},{10... | collective-permute-start | bytes 4915208 | tf_op jit(solution)/shard_map/ppermute | solution.py:296
  7.9 25.1 %collective-permute-start.5 = (bf16[160,5120]{1,0:T(8,128)(2,1)}, bf16[160,5120]{1,0:T(8,128)(2,1)}, u32[]{:S(2)}, u32[]{:S(2)}) collective-permute-start(bf16[160,5120]{1,0:T(8,128)(2,1)} %out0), channel_id=1, source_target_pairs={{0,8},{8,0},{16,24},{24,16},{1,9},{9,1},{17,25},{25,17},{2,10},{10... | collective-permute-start | bytes 4915208 | tf_op jit(solution)/shard_map/ppermute | solution.py:296
  14.6 7.3 %collective-permute-start.1 = (bf16[64,1280]{1,0:T(8,128)(2,1)}, bf16[64,1280]{1,0:T(8,128)(2,1)S(1)}, u32[]{:S(2)}, u32[]{:S(2)}) collective-permute-start(bf16[64,1280]{1,0:T(8,128)(2,1)} %get-tuple-element.26), channel_id=1, source_target_pairs={{0,4},{1,5},{2,6},{3,7},{4,0},{5,1},{6,2},{7,3},{8,12},{9,13},{10,... | collective-permute-start | bytes 491528 | tf_op jit(solution)/shard_map/ppermute | solution.py:323
  21.9 5.5 %collective-permute-start.2 = (bf16[64,1280]{1,0:T(8,128)(2,1)}, bf16[64,1280]{1,0:T(8,128)(2,1)S(1)}, u32[]{:S(2)}, u32[]{:S(2)}) collective-permute-start(bf16[64,1280]{1,0:T(8,128)(2,1)} %get-tuple-element.27), channel_id=1, source_target_pairs={{0,6},{1,7},{2,0},{3,1},{4,2},{5,3},{6,4},{7,5},{8,14},{9,15},{10,... | collective-permute-start | bytes 491528 | tf_op jit(solution)/shard_map/ppermute | solution.py:323
  33.0 6.6 %collective-permute-start.8 = (bf16[64,1280]{1,0:T(8,128)(2,1)S(1)}, bf16[64,1280]{1,0:T(8,128)(2,1)S(1)}, u32[]{:S(2)}, u32[]{:S(2)}) collective-permute-start(bf16[64,1280]{1,0:T(8,128)(2,1)S(1)} %add_convert_fusion.9), channel_id=1, source_target_pairs={{0,17},{1,16},{2,19},{3,18},{4,21},{5,20},{6,23},{7,22},{8,25},{9,... | collective-permute-start | bytes 491528 | tf_op jit(solution)/shard_map/ppermute | solution.py:309
  39.7 9.9 %collective-permute-start.10 = (bf16[128,1280]{1,0:T(8,128)(2,1)S(1)}, bf16[128,1280]{1,0:T(8,128)(2,1)S(1)}, u32[]{:S(2)}, u32[]{:S(2)}) collective-permute-start(bf16[128,1280]{1,0:T(8,128)(2,1)S(1)} %bitcast.91), channel_id=1, source_target_pairs={{0,4},{1,5},{2,6},{3,7},{4,0},{5,1},{6,2},{7,3},{8,12},{9,13},{10,... | collective-permute-start | bytes 983048 | tf_op jit(solution)/shard_map/ppermute | solution.py:323
  41.1 11.5 %collective-permute-start.11 = (bf16[128,1280]{1,0:T(8,128)(2,1)S(1)}, bf16[128,1280]{1,0:T(8,128)(2,1)S(1)}, u32[]{:S(2)}, u32[]{:S(2)}) collective-permute-start(bf16[128,1280]{1,0:T(8,128)(2,1)S(1)} %bitcast.92), channel_id=1, source_target_pairs={{0,6},{1,7},{2,0},{3,1},{4,2},{5,3},{6,4},{7,5},{8,14},{9,15},{10,... | collective-permute-start | bytes 983048 | tf_op jit(solution)/shard_map/ppermute | solution.py:323
  42.6 10.5 %collective-permute-start.9 = (bf16[128,1280]{1,0:T(8,128)(2,1)S(1)}, bf16[128,1280]{1,0:T(8,128)(2,1)S(1)}, u32[]{:S(2)}, u32[]{:S(2)}) collective-permute-start(bf16[128,1280]{1,0:T(8,128)(2,1)S(1)} %bitcast.93), channel_id=1, source_target_pairs={{0,2},{1,3},{2,4},{3,5},{4,6},{5,7},{6,0},{7,1},{8,10},{9,11},{10,... | collective-permute-start | bytes 983048 | tf_op jit(solution)/shard_map/ppermute | solution.py:323
  60.9 11.8 %collective-permute-start.12 = (bf16[128,1280]{1,0:T(8,128)(2,1)}, bf16[128,1280]{1,0:T(8,128)(2,1)S(1)}, u32[]{:S(2)}, u32[]{:S(2)}) collective-permute-start(bf16[128,1280]{1,0:T(8,128)(2,1)} %get-tuple-element.34), channel_id=1, source_target_pairs={{0,2},{1,3},{2,4},{3,5},{4,6},{5,7},{6,0},{7,1},{8,10},{9,11},{10,... | collective-permute-start | bytes 983048 | tf_op jit(solution)/shard_map/ppermute | solution.py:323
  61.4 15.7 %collective-permute-start.13 = (bf16[128,1280]{1,0:T(8,128)(2,1)}, bf16[128,1280]{1,0:T(8,128)(2,1)S(1)}, u32[]{:S(2)}, u32[]{:S(2)}) collective-permute-start(bf16[128,1280]{1,0:T(8,128)(2,1)} %get-tuple-element.35), channel_id=1, source_target_pairs={{0,4},{1,5},{2,6},{3,7},{4,0},{5,1},{6,2},{7,3},{8,12},{9,13},{10,... | collective-permute-start | bytes 983048 | tf_op jit(solution)/shard_map/ppermute | solution.py:323
  65.0 12.1 %collective-permute-start.14 = (bf16[128,1280]{1,0:T(8,128)(2,1)}, bf16[128,1280]{1,0:T(8,128)(2,1)S(1)}, u32[]{:S(2)}, u32[]{:S(2)}) collective-permute-start(bf16[128,1280]{1,0:T(8,128)(2,1)} %get-tuple-element.36), channel_id=1, source_target_pairs={{0,6},{1,7},{2,0},{3,1},{4,2},{5,3},{6,4},{7,5},{8,14},{9,15},{10,... | collective-permute-start | bytes 983048 | tf_op jit(solution)/shard_map/ppermute | solution.py:323
  78.3 7.2 %collective-permute-start.15 = (bf16[128,1280]{1,0:T(8,128)(2,1)S(1)}, bf16[128,1280]{1,0:T(8,128)(2,1)S(1)}, u32[]{:S(2)}, u32[]{:S(2)}) collective-permute-start(bf16[128,1280]{1,0:T(8,128)(2,1)S(1)} %add_convert_fusion.8), channel_id=1, source_target_pairs={{0,1},{1,0},{2,3},{3,2},{4,5},{5,4},{6,7},{7,6},{8,9},{9,8},{10,11... | collective-permute-start | bytes 983048 | tf_op jit(solution)/shard_map/ppermute | solution.py:309
  85.6 6.9 %collective-permute-start.16 = (bf16[128,1280]{1,0:T(8,128)(2,1)S(1)}, bf16[128,1280]{1,0:T(8,128)(2,1)S(1)}, u32[]{:S(2)}, u32[]{:S(2)}) collective-permute-start(bf16[128,1280]{1,0:T(8,128)(2,1)S(1)} %fusion), channel_id=1, source_target_pairs={{16,1},{17,0},{18,3},{19,2},{20,5},{21,4},{22,7},{23,6},{24,9},{25... | collective-permute-start | bytes 983048 | tf_op jit(solution)/shard_map/ppermute | solution.py:309
  88.0 14.0 %collective-permute-start.18 = (bf16[5120,128]{1,0:T(8,128)(2,1)S(1)}, bf16[5120,128]{1,0:T(8,128)(2,1)}, u32[]{:S(2)}, u32[]{:S(2)}) collective-permute-start(bf16[5120,128]{1,0:T(8,128)(2,1)S(1)} %bitcast.81), channel_id=1, source_target_pairs={{0,8},{8,0},{16,24},{24,16},{1,9},{9,1},{17,25},{25,17},{2,10},{10... | collective-permute-start | bytes 3932168 | tf_op jit(solution)/shard_map/ppermute | solution.py:296
  88.1 13.9 %collective-permute-start.19 = (bf16[5120,128]{1,0:T(8,128)(2,1)S(1)}, bf16[5120,128]{1,0:T(8,128)(2,1)}, u32[]{:S(2)}, u32[]{:S(2)}) collective-permute-start(bf16[5120,128]{1,0:T(8,128)(2,1)S(1)} %bitcast.86), channel_id=1, source_target_pairs={{0,8},{8,0},{16,24},{24,16},{1,9},{9,1},{17,25},{25,17},{2,10},{10... | collective-permute-start | bytes 3932168 | tf_op jit(solution)/shard_map/ppermute | solution.py:296
  93.9 21.0 %all-to-all-start = ((bf16[4,128,1280]{2,1,0:T(8,128)(2,1)}), bf16[4,128,1280]{2,1,0:T(8,128)(2,1)}, u32[]{:S(2)}, u32[]{:S(2)}) async-start(bf16[4,128,1280]{2,1,0:T(8,128)(2,1)} %broadcast_in_dim.36), calls=%async_computation | async-start | bytes 2621440 | tf_op jit(solution)/shard_map/all_to_all | solution.py:312
  141.3 7.2 %collective-permute-start.20 = (bf16[128,1280]{1,0:T(8,128)(2,1)S(1)}, bf16[128,1280]{1,0:T(8,128)(2,1)S(1)}, u32[]{:S(2)}, u32[]{:S(2)}) collective-permute-start(bf16[128,1280]{1,0:T(8,128)(2,1)S(1)} %add_convert_fusion.6), channel_id=1, source_target_pairs={{0,1},{1,0},{2,3},{3,2},{4,5},{5,4},{6,7},{7,6},{8,9},{9,8},{10,11... | collective-permute-start | bytes 983048 | tf_op jit(solution)/shard_map/ppermute | solution.py:309
  149.7 15.8 %all-to-all-start.2 = ((bf16[4,128,1280]{2,1,0:T(8,128)(2,1)}), bf16[4,128,1280]{2,1,0:T(8,128)(2,1)S(1)}, u32[]{:S(2)}, u32[]{:S(2)}) async-start(bf16[4,128,1280]{2,1,0:T(8,128)(2,1)} %broadcast_in_dim.37), calls=%async_computation.2 | async-start | bytes 2621440 | tf_op jit(solution)/shard_map/all_to_all | solution.py:312
  191.3 10.6 %collective-permute-start.21 = (bf16[128,1280]{1,0:T(8,128)(2,1)S(1)}, bf16[128,1280]{1,0:T(8,128)(2,1)S(1)}, u32[]{:S(2)}, u32[]{:S(2)}) collective-permute-start(bf16[128,1280]{1,0:T(8,128)(2,1)S(1)} %add_convert_fusion.4), channel_id=1, source_target_pairs={{0,16},{1,17},{2,18},{3,19},{4,20},{5,21},{6,22},{7,23},{8,24},{9,... | collective-permute-start | bytes 983048 | tf_op jit(solution)/shard_map/ppermute | solution.py:309
  192.6 12.7 %collective-permute-start.22 = (bf16[128,1280]{1,0:T(8,128)(2,1)S(1)}, bf16[128,1280]{1,0:T(8,128)(2,1)S(1)}, u32[]{:S(2)}, u32[]{:S(2)}) collective-permute-start(bf16[128,1280]{1,0:T(8,128)(2,1)S(1)} %add_convert_fusion.4), channel_id=1, source_target_pairs={{0,17},{1,16},{2,19},{3,18},{4,21},{5,20},{6,23},{7,22},{8,25},{9,... | collective-permute-start | bytes 983048 | tf_op jit(solution)/shard_map/ppermute | solution.py:309
  245.7 7.2 %collective-permute-start.23 = (bf16[128,1280]{1,0:T(8,128)(2,1)S(1)}, bf16[128,1280]{1,0:T(8,128)(2,1)S(1)}, u32[]{:S(2)}, u32[]{:S(2)}) collective-permute-start(bf16[128,1280]{1,0:T(8,128)(2,1)S(1)} %add_convert_fusion.2), channel_id=1, source_target_pairs={{0,1},{1,0},{2,3},{3,2},{4,5},{5,4},{6,7},{7,6},{8,9},{9,8},{10,11... | collective-permute-start | bytes 983048 | tf_op jit(solution)/shard_map/ppermute | solution.py:309
  254.1 15.9 %all-to-all-start.6 = ((bf16[4,128,1280]{2,1,0:T(8,128)(2,1)}), bf16[4,128,1280]{2,1,0:T(8,128)(2,1)S(1)}, u32[]{:S(2)}, u32[]{:S(2)}) async-start(bf16[4,128,1280]{2,1,0:T(8,128)(2,1)} %broadcast_in_dim.39), calls=%async_computation.6 | async-start | bytes 2621440 | tf_op jit(solution)/shard_map/all_to_all | solution.py:312
  279.7 15.8 %all-to-all-start.7 = ((bf16[4,128,1280]{2,1,0:T(8,128)(2,1)}), bf16[4,128,1280]{2,1,0:T(8,128)(2,1)S(1)}, u32[]{:S(2)}, u32[]{:S(2)}) async-start(bf16[4,128,1280]{2,1,0:T(8,128)(2,1)} %decoder_layer.7), calls=%async_computation.7 | async-start | bytes 2621440 | tf_op jit(solution)/shard_map/all_to_all | solution.py:312
  297.3 5.6 %collective-permute-start.24 = (bf16[4,16,1280]{2,1,0:T(8,128)(2,1)S(1)}, bf16[4,16,1280]{2,1,0:T(8,128)(2,1)S(1)}, u32[]{:S(2)}, u32[]{:S(2)}) collective-permute-start(bf16[4,16,1280]{2,1,0:T(8,128)(2,1)S(1)} %get-tuple-element.45), channel_id=1, source_target_pairs={{16,0},{17,1},{18,2},{19,3},{20,4},{21,5},{22,6},{23,7},{24,8},{25... | collective-permute-start | bytes 491528 | tf_op jit(solution)/shard_map/ppermute | solution.py:309
  300.5 7.2 %collective-permute-start.26 = (bf16[4,16,1280]{2,1,0:T(8,128)(2,1)S(1)}, bf16[4,16,1280]{2,1,0:T(8,128)(2,1)S(1)}, u32[]{:S(2)}, u32[]{:S(2)}) collective-permute-start(bf16[4,16,1280]{2,1,0:T(8,128)(2,1)S(1)} %get-tuple-element.47), channel_id=1, source_target_pairs={{16,17},{17,16},{18,19},{19,18},{20,21},{21,20},{22,23},{23,22},{2... | collective-permute-start | bytes 491528 | tf_op jit(solution)/shard_map/ppermute | solution.py:309
  307.8 9.7 %collective-permute-start.27 = (bf16[16,1280]{1,0:T(8,128)(2,1)S(1)}, bf16[16,1280]{1,0:T(8,128)(2,1)S(1)}, u32[]{:S(2)}, u32[]{:S(2)}) collective-permute-start(bf16[16,1280]{1,0:T(8,128)(2,1)S(1)} %get-tuple-element.52), channel_id=1, source_target_pairs={{0,0},{1,1},{2,32},{3,33},{4,64},{5,65},{6,96},{7,97},{32,2},{33,3... | collective-permute-start | bytes 122888 | tf_op jit(solution)/shard_map/ppermute | solution.py:436
  310.5 7.7 %collective-permute-start.28 = (bf16[16,1280]{1,0:T(8,128)(2,1)S(1)}, bf16[16,1280]{1,0:T(8,128)(2,1)S(1)}, u32[]{:S(2)}, u32[]{:S(2)}) collective-permute-start(bf16[16,1280]{1,0:T(8,128)(2,1)S(1)} %get-tuple-element.55), channel_id=1, source_target_pairs={{0,32},{1,33},{2,64},{3,65},{4,96},{5,97},{6,0},{7,1},{32,34},{33,... | collective-permute-start | bytes 122888 | tf_op jit(solution)/shard_map/ppermute | solution.py:436
  315.4 6.1 %collective-permute-start.29 = (bf16[16,1280]{1,0:T(8,128)(2,1)S(1)}, bf16[16,1280]{1,0:T(8,128)(2,1)S(1)}, u32[]{:S(2)}, u32[]{:S(2)}) collective-permute-start(bf16[16,1280]{1,0:T(8,128)(2,1)S(1)} %get-tuple-element.54), channel_id=1, source_target_pairs={{0,64},{1,65},{2,96},{3,97},{4,0},{5,1},{6,32},{7,33},{32,66},{33,... | collective-permute-start | bytes 122888 | tf_op jit(solution)/shard_map/ppermute | solution.py:436
  316.5 5.5 %collective-permute-start.30 = (bf16[16,1280]{1,0:T(8,128)(2,1)S(1)}, bf16[16,1280]{1,0:T(8,128)(2,1)S(1)}, u32[]{:S(2)}, u32[]{:S(2)}) collective-permute-start(bf16[16,1280]{1,0:T(8,128)(2,1)S(1)} %get-tuple-element.53), channel_id=1, source_target_pairs={{0,96},{1,97},{2,0},{3,1},{4,32},{5,33},{6,64},{7,65},{32,98},{33,... | collective-permute-start | bytes 122888 | tf_op jit(solution)/shard_map/ppermute | solution.py:436
  (18 other events, 124.2 us)

commit v3 on v2

--- a/solution.py
+++ b/solution.py
@@ -87,7 +87,7 @@
         cols = slice(c * LANES, (c + 1) * LANES)
         rows[c] = lowered[:, cols]
         for step in range(STACK):
-            j = lax.rem(place[0] + step, STACK)
+            j = lax.rem(place[0] + place[1] * step, STACK)
             outs[step][:, cols] = rows[c, pl.ds(j, count, stride=STACK), :].astype(BF)
 
 
@@ -121,7 +121,11 @@
     units = in0.shape[0]
     made = [[], []]
     for k in range(blocks):
-        sources = lax.rem(place[0] + blocks - k, blocks), lax.rem(place[0] + k, blocks)
+        away = place[1] * k
+        sources = (
+            lax.rem(place[0] + blocks * blocks - away, blocks),
+            lax.rem(place[0] + away, blocks),
+        )
         for kind, pair in enumerate(((in0, in1), (out0, out1))):
             part = block_at(sources[kind], depth)
             for i in range(2):
@@ -156,7 +160,7 @@
             pltpu.VMEM((count, 2 * units, depth), BF),
             pltpu.SemaphoreType.DMA((2, 2, count)),
         ],
-        compiler_params=pltpu.CompilerParams(vmem_limit_bytes=56 << 20),
+        compiler_params=pltpu.CompilerParams(vmem_limit_bytes=32 << 20),
         cost_estimate=pl.CostEstimate(
             flops=8 * rows * width * units,
             bytes_accessed=8 * width * units,
@@ -255,7 +259,7 @@
             pltpu.VMEM((count, q_cols, depth), BF),
             pltpu.SemaphoreType.DMA((5, count)),
         ],
-        compiler_params=pltpu.CompilerParams(vmem_limit_bytes=56 << 20),
+        compiler_params=pltpu.CompilerParams(vmem_limit_bytes=60 << 20),
         cost_estimate=pl.CostEstimate(
             flops=2 * rows * weights, bytes_accessed=2 * weights, transcendentals=rows * rows * 4
         ),
@@ -317,10 +321,14 @@
         return jnp.sum(z_all_to_all(partial).astype(F32), axis=0)
 
     def z_move(value, step):
-        pairs = [
-            (2 * z + y, 2 * ((z + step) % z_count) + y) for z in range(z_count) for y in range(2)
-        ]
-        return lax.ppermute(value, "tp", pairs)
+        pairs = []
+        for section in range(section_count):
+            turn_by = step if section % 2 == 0 else z_count - step
+            for z in range(z_count):
+                for y in range(2):
+                    start = section * tp_count + y
+                    pairs.append((start + 2 * z, start + 2 * ((z + turn_by) % z_count)))
+        return lax.ppermute(value, ("section", "tp"), pairs)
 
     def z_scatter(parts):
         moved = [z_move(parts[step], step) for step in range(1, z_count)]
@@ -344,7 +352,8 @@
 
     width = frames.shape[3]
     tokens = frames.shape[2] // STACK
-    place = z_index.astype(jnp.int32).reshape(1)
+    way = jnp.where(core == 0, 1, z_count - 1)
+    place = jnp.stack([z_index, way]).astype(jnp.int32)
     partial_down = encoder(place, frames[0, 0], ln_gain, ln_bias, enc_up, up_bias, enc_down)
     own_frames = lax.dynamic_index_in_dim(
         frames[0, 0].reshape(tokens, STACK, width), z_index, 1, keepdims=False

time: 324 us -> 321 us (level)
  waiting for transfers between devices: 141 us -> 135 us
    ppermute x9, waiting for transfers between devices: 37.2 us -> 31.9 us  [z_move(): return lax.ppermute(value, ('section', 'tp'), pairs)]
  transfers between devices with their start and end apart: 35 -> 35, of which waited for: 26 -> 26; matrix products, arithmetic and copies ran while one was open for 2% -> 4% of each run, Pallas kernels for 2% -> 2%
where the time goes in v3:
time: 321 us; the launch traced here: 320 us
  waiting for transfers between devices  135 us (42%)
  blocking collectives  63.9 us (20%)
  starting transfers between devices  54.2 us (17%)
  Pallas kernels  45.1 us (14%)
  local copies, waits for them, and re-layouts  11.1 us (3%)
  other arithmetic  10.4 us (3%)
    all_to_all x4, blocking collectives, z_all_to_all(): lax.all_to_all(value, 'tp', split_axis=0, concat_axis=0, tiled=True, axis...  63.9 us
    ppermute x11, waiting for transfers between devices, y_move(): return lax.ppermute(value, ('section', 'tp'), pairs)  51.2 us
    all_to_all x4, waiting for transfers between devices, z_all_to_all(): lax.all_to_all(value, 'tp', split_axis=0, concat_axis=0, tiled=True, axis...  46.6 us
    pallas_call x4, Pallas kernels, decoder_layer(): pl.pallas_call(layer_kernel, out_shape=jax.ShapeDtypeStruct(blocks.shape,...  34.5 us
    ppermute x9, waiting for transfers between devices, z_move(): return lax.ppermute(value, ('section', 'tp'), pairs)  31.9 us
    all_to_all x4, starting transfers between devices, z_all_to_all(): lax.all_to_all(value, 'tp', split_axis=0, concat_axis=0, tiled=True, axis...  15.4 us
    ppermute x9, starting transfers between devices, z_move(): return lax.ppermute(value, ('section', 'tp'), pairs)  15.1 us
    ppermute x11, starting transfers between devices, y_move(): return lax.ppermute(value, ('section', 'tp'), pairs)  11.8 us
  transfers between devices with their start and end apart: 35, of which 26 were waited for; matrix products, arithmetic and copies ran while one was open for 4% of the time, Pallas kernels for 2%

profile of v3, /device:TPU:30, one launch (start us, length us, event | category | flops | bytes accessed | tf_op | source)
XLA Modules:
  0.0 320.0 jit_solution(138638075239035395)
XLA Ops:
  1.1 5.4 %encoder_units.1 = (bf16[64,1280]{1,0:T(8,128)(2,1)}, bf16[64,1280]{1,0:T(8,128)(2,1)}, bf16[64,1280]{1,0:T(8,128)(2,1)}, bf16[64,1280]{1,0:T(8,128)(2,1)}) custom-call(s32[2]{0:T(128)} %pad_add_fusion.place, bf16[256,1280]{1,0:T(8,128)(2,1)} %bitcast.95, bf16[1280]{0:T(1024)(128)(2,1)} %gain_ref.1, bf16[1280]{0:T(1024)(128)(2,1)} %bias_ref.1, ...), custom_call_target="tpu_custom_call" | custom-call | flops 838860800 | bytes 3276800 | tf_op jit(solution)/shard_map/encoder_units/pallas_call | solution.py:97
  10.5 3.8 %collective-permute-done = bf16[64,1280]{1,0:T(8,128)(2,1)} collective-permute-done((bf16[64,1280]{1,0:T(8,128)(2,1)}, bf16[64,1280]{1,0:T(8,128)(2,1)}, u32[]{:S(2)}, u32[]{:S(2)}) %collective-permute-start) | collective-permute-done | bytes 163872 | tf_op jit(solution)/shard_map/ppermute | solution.py:331
  29.4 4.6 %collective-permute-done.3 = bf16[64,1280]{1,0:T(8,128)(2,1)S(1)} collective-permute-done((bf16[64,1280]{1,0:T(8,128)(2,1)S(1)}, bf16[64,1280]{1,0:T(8,128)(2,1)S(1)}, u32[]{:S(2)}, u32[]{:S(2)}) %collective-permute-start.3) | collective-permute-done | bytes 163872 | tf_op jit(solution)/shard_map/ppermute | solution.py:313
  34.3 6.4 %collective-permute-done.8 = bf16[64,1280]{1,0:T(8,128)(2,1)} collective-permute-done((bf16[64,1280]{1,0:T(8,128)(2,1)S(1)}, bf16[64,1280]{1,0:T(8,128)(2,1)}, u32[]{:S(2)}, u32[]{:S(2)}) %collective-permute-start.8) | collective-permute-done | bytes 163872 | tf_op jit(solution)/shard_map/ppermute | solution.py:313
  46.3 6.7 %collective-permute-done.10.x2 = bf16[128,1280]{1,0:T(8,128)(2,1)S(1)} collective-permute-done((bf16[128,1280]{1,0:T(8,128)(2,1)S(1)}, bf16[128,1280]{1,0:T(8,128)(2,1)S(1)}, u32[]{:S(2)}, u32[]{:S(2)}) %collective-permute-start.10) | collective-permute-done | bytes 327712 | tf_op jit(solution)/shard_map/ppermute | solution.py:331
  56.4 5.2 %adapter_units.1 = (bf16[128,1280]{1,0:T(8,128)(2,1)S(1)}, bf16[128,1280]{1,0:T(8,128)(2,1)S(1)}, bf16[128,1280]{1,0:T(8,128)(2,1)S(1)}, bf16[128,1280]{1,0:T(8,128)(2,1)S(1)}) custom-call(s32[2]{0:T(128)S(1)} %copy-done.2, bf16[128,1280]{1,0:T(8,128)(2,1)S(1)} %bitcast.73, bf16[128,1280]{1,0:T(8,128)(2,1)S(1)} %collective-permute-done.9.x1, ...), custom_call_target="tpu_custom_call" | custom-call | flops 838860800 | bytes 6553600 | tf_op jit(solution)/shard_map/adapter_units/pallas_call | solution.py:153
  65.5 10.7 %collective-permute-done.12 = bf16[128,1280]{1,0:T(8,128)(2,1)S(1)} collective-permute-done((bf16[128,1280]{1,0:T(8,128)(2,1)S(1)}, bf16[128,1280]{1,0:T(8,128)(2,1)S(1)}, u32[]{:S(2)}, u32[]{:S(2)}) %collective-permute-start.12) | collective-permute-done | bytes 327712 | tf_op jit(solution)/shard_map/ppermute | solution.py:331
  79.0 7.1 %collective-permute-done.15 = bf16[128,1280]{1,0:T(8,128)(2,1)S(1)} collective-permute-done((bf16[128,1280]{1,0:T(8,128)(2,1)S(1)}, bf16[128,1280]{1,0:T(8,128)(2,1)S(1)}, u32[]{:S(2)}, u32[]{:S(2)}) %collective-permute-start.15) | collective-permute-done | bytes 327712 | tf_op jit(solution)/shard_map/ppermute | solution.py:313
  89.1 4.0 %collective-permute-done.16 = bf16[128,1280]{1,0:T(8,128)(2,1)S(1)} collective-permute-done((bf16[128,1280]{1,0:T(8,128)(2,1)S(1)}, bf16[128,1280]{1,0:T(8,128)(2,1)S(1)}, u32[]{:S(2)}, u32[]{:S(2)}) %collective-permute-start.16) | collective-permute-done | bytes 327712 | tf_op jit(solution)/shard_map/ppermute | solution.py:313
  94.3 4.6 %all-to-all-start = ((bf16[4,128,1280]{2,1,0:T(8,128)(2,1)}), bf16[4,128,1280]{2,1,0:T(8,128)(2,1)}, u32[]{:S(2)}, u32[]{:S(2)}) async-start(bf16[4,128,1280]{2,1,0:T(8,128)(2,1)} %broadcast_in_dim.36), calls=%async_computation | async-start | bytes 2621440 | tf_op jit(solution)/shard_map/all_to_all | solution.py:316
  101.5 11.8 %all-to-all-done.x_hbm = bf16[4,128,1280]{2,1,0:T(8,128)(2,1)} async-done(((bf16[4,128,1280]{2,1,0:T(8,128)(2,1)}), bf16[4,128,1280]{2,1,0:T(8,128)(2,1)}, u32[]{:S(2)}, u32[]{:S(2)}) %all-to-all-start) | async-done | bytes 1310752 | tf_op jit(solution)/shard_map/all_to_all | solution.py:316
  113.3 8.6 %decoder_layer.4 = bf16[4,128,1280]{2,1,0:T(8,128)(2,1)} custom-call(s32[1]{0:T(128)} %bitcast.8.which, bf16[4,128,1280]{2,1,0:T(8,128)(2,1)} %all-to-all-done.x_hbm, f32[1,5120]{1,0:T(1,128)} %get-tuple-element.57.gain0, f32[1,5120]{1,0:T(1,128)} %bitcast.97, f32[128,128]{1,0:T(8,128)} %fusion.9.mask_ref, bf16[5120,512]{1,0:T(8,128)(2,1)} %bitcast.75, ...), custom_call_target="tpu_custom_call" | custom-call | flops 1677721600 | bytes 13107200 | tf_op jit(solution)/shard_map/decoder_layer/pallas_call | solution.py:249
  121.9 16.8 %all_to_all.40 = bf16[4,128,1280]{2,1,0:T(8,128)(2,1)S(1)} all-to-all(bf16[4,128,1280]{2,1,0:T(8,128)(2,1)} %decoder_layer.4), channel_id=1, replica_groups={{0,2,4,6},{1,3,5,7},{8,10,12,14},{9,11,13,15},{16,18,20,22},{17,19,21,2..., dimensions={0} | all-to-all | bytes 2621440 | tf_op jit(solution)/shard_map/all_to_all | solution.py:316
  139.1 7.1 %collective-permute-done.20 = bf16[128,1280]{1,0:T(8,128)(2,1)S(1)} collective-permute-done((bf16[128,1280]{1,0:T(8,128)(2,1)S(1)}, bf16[128,1280]{1,0:T(8,128)(2,1)S(1)}, u32[]{:S(2)}, u32[]{:S(2)}) %collective-permute-start.20) | collective-permute-done | bytes 327712 | tf_op jit(solution)/shard_map/ppermute | solution.py:313
  147.4 3.5 %all-to-all-start.2 = ((bf16[4,128,1280]{2,1,0:T(8,128)(2,1)}), bf16[4,128,1280]{2,1,0:T(8,128)(2,1)S(1)}, u32[]{:S(2)}, u32[]{:S(2)}) async-start(bf16[4,128,1280]{2,1,0:T(8,128)(2,1)} %broadcast_in_dim.37), calls=%async_computation.2 | async-start | bytes 2621440 | tf_op jit(solution)/shard_map/all_to_all | solution.py:316
  150.9 12.3 %all-to-all-done.2.x_hbm = bf16[4,128,1280]{2,1,0:T(8,128)(2,1)S(1)} async-done(((bf16[4,128,1280]{2,1,0:T(8,128)(2,1)}), bf16[4,128,1280]{2,1,0:T(8,128)(2,1)S(1)}, u32[]{:S(2)}, u32[]{:S(2)}) %all-to-all-start.2) | async-done | bytes 1310752 | tf_op jit(solution)/shard_map/all_to_all | solution.py:316
  164.3 8.6 %decoder_layer.5 = bf16[4,128,1280]{2,1,0:T(8,128)(2,1)} custom-call(s32[1]{0:T(128)} %bitcast.7.which, bf16[4,128,1280]{2,1,0:T(8,128)(2,1)} %copy-done.6, f32[1,5120]{1,0:T(1,128)} %get-tuple-element.57.gain0, f32[1,5120]{1,0:T(1,128)} %bitcast.98, f32[128,128]{1,0:T(8,128)} %fusion.9.mask_ref, bf16[5120,512]{1,0:T(8,128)(2,1)} %bitcast.76, ...), custom_call_target="tpu_custom_call" | custom-call | flops 1677721600 | bytes 13107200 | tf_op jit(solution)/shard_map/decoder_layer/pallas_call | solution.py:249
  172.9 15.8 %all_to_all.41 = bf16[4,128,1280]{2,1,0:T(8,128)(2,1)S(1)} all-to-all(bf16[4,128,1280]{2,1,0:T(8,128)(2,1)} %decoder_layer.5), channel_id=1, replica_groups={{0,2,4,6},{1,3,5,7},{8,10,12,14},{9,11,13,15},{16,18,20,22},{17,19,21,2..., dimensions={0} | all-to-all | bytes 2621440 | tf_op jit(solution)/shard_map/all_to_all | solution.py:316
  191.6 8.0 %collective-permute-done.21 = bf16[128,1280]{1,0:T(8,128)(2,1)S(1)} collective-permute-done((bf16[128,1280]{1,0:T(8,128)(2,1)S(1)}, bf16[128,1280]{1,0:T(8,128)(2,1)S(1)}, u32[]{:S(2)}, u32[]{:S(2)}) %collective-permute-start.21) | collective-permute-done | bytes 327712 | tf_op jit(solution)/shard_map/ppermute | solution.py:313
  199.6 3.4 %collective-permute-done.22 = bf16[128,1280]{1,0:T(8,128)(2,1)S(1)} collective-permute-done((bf16[128,1280]{1,0:T(8,128)(2,1)S(1)}, bf16[128,1280]{1,0:T(8,128)(2,1)S(1)}, u32[]{:S(2)}, u32[]{:S(2)}) %collective-permute-start.22) | collective-permute-done | bytes 327712 | tf_op jit(solution)/shard_map/ppermute | solution.py:313
  203.1 15.5 %all_to_all.42.x_hbm = bf16[4,128,1280]{2,1,0:T(8,128)(2,1)} all-to-all(bf16[4,128,1280]{2,1,0:T(8,128)(2,1)S(1)} %broadcast_in_dim.38), channel_id=1, replica_groups={{0,2,4,6},{1,3,5,7},{8,10,12,14},{9,11,13,15},{16,18,20,22},{17,19,21,2..., dimensions={0} | all-to-all | bytes 2621440 | tf_op jit(solution)/shard_map/all_to_all | solution.py:316
  218.6 8.6 %decoder_layer.6 = bf16[4,128,1280]{2,1,0:T(8,128)(2,1)} custom-call(s32[1]{0:T(128)} %bitcast.8.which, bf16[4,128,1280]{2,1,0:T(8,128)(2,1)} %all_to_all.42.x_hbm, f32[1,5120]{1,0:T(1,128)} %get-tuple-element.57.gain0, f32[1,5120]{1,0:T(1,128)} %bitcast.99, f32[128,128]{1,0:T(8,128)} %fusion.9.mask_ref, bf16[5120,512]{1,0:T(8,128)(2,1)} %bitcast.77, ...), custom_call_target="tpu_custom_call" | custom-call | flops 1677721600 | bytes 13107200 | tf_op jit(solution)/shard_map/decoder_layer/pallas_call | solution.py:249
  227.2 15.8 %all_to_all.43 = bf16[4,128,1280]{2,1,0:T(8,128)(2,1)S(1)} all-to-all(bf16[4,128,1280]{2,1,0:T(8,128)(2,1)} %decoder_layer.6), channel_id=1, replica_groups={{0,2,4,6},{1,3,5,7},{8,10,12,14},{9,11,13,15},{16,18,20,22},{17,19,21,2..., dimensions={0} | all-to-all | bytes 2621440 | tf_op jit(solution)/shard_map/all_to_all | solution.py:316
  244.2 6.3 %collective-permute-done.23 = bf16[128,1280]{1,0:T(8,128)(2,1)S(1)} collective-permute-done((bf16[128,1280]{1,0:T(8,128)(2,1)S(1)}, bf16[128,1280]{1,0:T(8,128)(2,1)S(1)}, u32[]{:S(2)}, u32[]{:S(2)}) %collective-permute-start.23) | collective-permute-done | bytes 327712 | tf_op jit(solution)/shard_map/ppermute | solution.py:313
  251.7 3.7 %all-to-all-start.6 = ((bf16[4,128,1280]{2,1,0:T(8,128)(2,1)}), bf16[4,128,1280]{2,1,0:T(8,128)(2,1)S(1)}, u32[]{:S(2)}, u32[]{:S(2)}) async-start(bf16[4,128,1280]{2,1,0:T(8,128)(2,1)} %broadcast_in_dim.39), calls=%async_computation.6 | async-start | bytes 2621440 | tf_op jit(solution)/shard_map/all_to_all | solution.py:316
  257.1 10.5 %all-to-all-done.6.x_hbm = bf16[4,128,1280]{2,1,0:T(8,128)(2,1)S(1)} async-done(((bf16[4,128,1280]{2,1,0:T(8,128)(2,1)}), bf16[4,128,1280]{2,1,0:T(8,128)(2,1)S(1)}, u32[]{:S(2)}, u32[]{:S(2)}) %all-to-all-start.6) | async-done | bytes 1310752 | tf_op jit(solution)/shard_map/all_to_all | solution.py:316
  268.7 8.6 %decoder_layer.7 = bf16[4,128,1280]{2,1,0:T(8,128)(2,1)} custom-call(s32[1]{0:T(128)} %bitcast.7.which, bf16[4,128,1280]{2,1,0:T(8,128)(2,1)} %copy-done.5, f32[1,5120]{1,0:T(1,128)} %get-tuple-element.57.gain0, f32[1,5120]{1,0:T(1,128)} %bitcast.100, f32[128,128]{1,0:T(8,128)} %fusion.9.mask_ref, bf16[5120,512]{1,0:T(8,128)(2,1)} %bitcast.78, ...), custom_call_target="tpu_custom_call" | custom-call | flops 1677721600 | bytes 13107200 | tf_op jit(solution)/shard_map/decoder_layer/pallas_call | solution.py:249
  277.3 3.6 %all-to-all-start.7 = ((bf16[4,128,1280]{2,1,0:T(8,128)(2,1)}), bf16[4,128,1280]{2,1,0:T(8,128)(2,1)S(1)}, u32[]{:S(2)}, u32[]{:S(2)}) async-start(bf16[4,128,1280]{2,1,0:T(8,128)(2,1)} %decoder_layer.7), calls=%async_computation.7 | async-start | bytes 2621440 | tf_op jit(solution)/shard_map/all_to_all | solution.py:316
  281.2 12.0 %all-to-all-done.7 = bf16[4,128,1280]{2,1,0:T(8,128)(2,1)S(1)} async-done(((bf16[4,128,1280]{2,1,0:T(8,128)(2,1)}), bf16[4,128,1280]{2,1,0:T(8,128)(2,1)S(1)}, u32[]{:S(2)}, u32[]{:S(2)}) %all-to-all-start.7) | async-done | bytes 1310752 | tf_op jit(solution)/shard_map/all_to_all | solution.py:316
  301.2 3.7 %collective-permute-done.26 = bf16[4,16,1280]{2,1,0:T(8,128)(2,1)S(1)} collective-permute-done((bf16[4,16,1280]{2,1,0:T(8,128)(2,1)S(1)}, bf16[4,16,1280]{2,1,0:T(8,128)(2,1)S(1)}, u32[]{:S(2)}, u32[]{:S(2)}) %collective-permute-start.26) | collective-permute-done | bytes 163872 | tf_op jit(solution)/shard_map/ppermute | solution.py:313
  308.1 4.9 %collective-permute-start.28 = (bf16[16,1280]{1,0:T(8,128)(2,1)S(1)}, bf16[16,1280]{1,0:T(8,128)(2,1)S(1)}, u32[]{:S(2)}, u32[]{:S(2)}) collective-permute-start(bf16[16,1280]{1,0:T(8,128)(2,1)S(1)} %get-tuple-element.55), channel_id=1, source_target_pairs={{0,32},{1,33},{2,64},{3,65},{4,96},{5,97},{6,0},{7,1},{32,34},{33,... | collective-permute-start | bytes 122888 | tf_op jit(solution)/shard_map/ppermute | solution.py:445
  315.7 3.3 %collective-permute-done.29 = bf16[16,1280]{1,0:T(8,128)(2,1)S(1)} collective-permute-done((bf16[16,1280]{1,0:T(8,128)(2,1)S(1)}, bf16[16,1280]{1,0:T(8,128)(2,1)S(1)}, u32[]{:S(2)}, u32[]{:S(2)}) %collective-permute-start.29) | collective-permute-done | bytes 40992 | tf_op jit(solution)/shard_map/ppermute | solution.py:445
  (131 shorter events, 68.6 us)
Async XLA Ops:
  0.0 34.0 %collective-permute-start.6 = (bf16[5120,512]{1,0:T(8,128)(2,1)}, bf16[5120,512]{1,0:T(8,128)(2,1)}, u32[]{:S(2)}, u32[]{:S(2)}) collective-permute-start(bf16[5120,512]{1,0:T(8,128)(2,1)} %bitcast.74), channel_id=1, source_target_pairs={{0,8},{8,0},{16,24},{24,16},{1,9},{9,1},{17,25},{25,17},{2,10},{10... | collective-permute-start | bytes 15728648 | tf_op jit(solution)/shard_map/ppermute | solution.py:300
  0.0 34.0 %collective-permute-start.7 = (bf16[512,5120]{1,0:T(8,128)(2,1)}, bf16[512,5120]{1,0:T(8,128)(2,1)}, u32[]{:S(2)}, u32[]{:S(2)}) collective-permute-start(bf16[512,5120]{1,0:T(8,128)(2,1)} %bitcast.79), channel_id=1, source_target_pairs={{0,8},{8,0},{16,24},{24,16},{1,9},{9,1},{17,25},{25,17},{2,10},{10... | collective-permute-start | bytes 15728648 | tf_op jit(solution)/shard_map/ppermute | solution.py:300
  6.6 7.7 %collective-permute-start = (bf16[64,1280]{1,0:T(8,128)(2,1)}, bf16[64,1280]{1,0:T(8,128)(2,1)}, u32[]{:S(2)}, u32[]{:S(2)}) collective-permute-start(bf16[64,1280]{1,0:T(8,128)(2,1)} %get-tuple-element.25), channel_id=1, source_target_pairs={{0,2},{1,3},{2,4},{3,5},{4,6},{5,7},{6,0},{7,1},{8,14},{9,15},{10,... | collective-permute-start | bytes 491528 | tf_op jit(solution)/shard_map/ppermute | solution.py:331
  8.5 25.5 %collective-permute-start.4 = (bf16[160,5120]{1,0:T(8,128)(2,1)S(1)}, bf16[160,5120]{1,0:T(8,128)(2,1)}, u32[]{:S(2)}, u32[]{:S(2)}) collective-permute-start(bf16[160,5120]{1,0:T(8,128)(2,1)S(1)} %bitcast.68), channel_id=1, source_target_pairs={{0,8},{8,0},{16,24},{24,16},{1,9},{9,1},{17,25},{25,17},{2,10},{10... | collective-permute-start | bytes 4915208 | tf_op jit(solution)/shard_map/ppermute | solution.py:300
  10.4 23.6 %collective-permute-start.5 = (bf16[160,5120]{1,0:T(8,128)(2,1)S(1)}, bf16[160,5120]{1,0:T(8,128)(2,1)}, u32[]{:S(2)}, u32[]{:S(2)}) collective-permute-start(bf16[160,5120]{1,0:T(8,128)(2,1)S(1)} %copy-done.1), channel_id=1, source_target_pairs={{0,8},{8,0},{16,24},{24,16},{1,9},{9,1},{17,25},{25,17},{2,10},{10... | collective-permute-start | bytes 4915208 | tf_op jit(solution)/shard_map/ppermute | solution.py:300
  14.3 7.1 %collective-permute-start.1 = (bf16[64,1280]{1,0:T(8,128)(2,1)}, bf16[64,1280]{1,0:T(8,128)(2,1)}, u32[]{:S(2)}, u32[]{:S(2)}) collective-permute-start(bf16[64,1280]{1,0:T(8,128)(2,1)} %get-tuple-element.26), channel_id=1, source_target_pairs={{0,4},{1,5},{2,6},{3,7},{4,0},{5,1},{6,2},{7,3},{8,12},{9,13},{10,... | collective-permute-start | bytes 491528 | tf_op jit(solution)/shard_map/ppermute | solution.py:331
  21.4 6.0 %collective-permute-start.2 = (bf16[64,1280]{1,0:T(8,128)(2,1)}, bf16[64,1280]{1,0:T(8,128)(2,1)S(1)}, u32[]{:S(2)}, u32[]{:S(2)}) collective-permute-start(bf16[64,1280]{1,0:T(8,128)(2,1)} %get-tuple-element.27), channel_id=1, source_target_pairs={{0,6},{1,7},{2,0},{3,1},{4,2},{5,3},{6,4},{7,5},{8,10},{9,11},{10,... | collective-permute-start | bytes 491528 | tf_op jit(solution)/shard_map/ppermute | solution.py:331
  34.0 6.7 %collective-permute-start.8 = (bf16[64,1280]{1,0:T(8,128)(2,1)S(1)}, bf16[64,1280]{1,0:T(8,128)(2,1)}, u32[]{:S(2)}, u32[]{:S(2)}) collective-permute-start(bf16[64,1280]{1,0:T(8,128)(2,1)S(1)} %add_convert_fusion.9), channel_id=1, source_target_pairs={{0,17},{1,16},{2,19},{3,18},{4,21},{5,20},{6,23},{7,22},{8,25},{9,... | collective-permute-start | bytes 491528 | tf_op jit(solution)/shard_map/ppermute | solution.py:313
  41.8 11.2 %collective-permute-start.10 = (bf16[128,1280]{1,0:T(8,128)(2,1)S(1)}, bf16[128,1280]{1,0:T(8,128)(2,1)S(1)}, u32[]{:S(2)}, u32[]{:S(2)}) collective-permute-start(bf16[128,1280]{1,0:T(8,128)(2,1)S(1)} %bitcast.70), channel_id=1, source_target_pairs={{0,4},{1,5},{2,6},{3,7},{4,0},{5,1},{6,2},{7,3},{8,12},{9,13},{10,... | collective-permute-start | bytes 983048 | tf_op jit(solution)/shard_map/ppermute | solution.py:331
  43.7 11.9 %collective-permute-start.11 = (bf16[128,1280]{1,0:T(8,128)(2,1)S(1)}, bf16[128,1280]{1,0:T(8,128)(2,1)S(1)}, u32[]{:S(2)}, u32[]{:S(2)}) collective-permute-start(bf16[128,1280]{1,0:T(8,128)(2,1)S(1)} %bitcast.71), channel_id=1, source_target_pairs={{0,6},{1,7},{2,0},{3,1},{4,2},{5,3},{6,4},{7,5},{8,10},{9,11},{10,... | collective-permute-start | bytes 983048 | tf_op jit(solution)/shard_map/ppermute | solution.py:331
  45.6 10.9 %collective-permute-start.9 = (bf16[128,1280]{1,0:T(8,128)(2,1)S(1)}, bf16[128,1280]{1,0:T(8,128)(2,1)S(1)}, u32[]{:S(2)}, u32[]{:S(2)}) collective-permute-start(bf16[128,1280]{1,0:T(8,128)(2,1)S(1)} %bitcast.72), channel_id=1, source_target_pairs={{0,2},{1,3},{2,4},{3,5},{4,6},{5,7},{6,0},{7,1},{8,14},{9,15},{10,... | collective-permute-start | bytes 983048 | tf_op jit(solution)/shard_map/ppermute | solution.py:331
  61.7 14.6 %collective-permute-start.12 = (bf16[128,1280]{1,0:T(8,128)(2,1)S(1)}, bf16[128,1280]{1,0:T(8,128)(2,1)S(1)}, u32[]{:S(2)}, u32[]{:S(2)}) collective-permute-start(bf16[128,1280]{1,0:T(8,128)(2,1)S(1)} %get-tuple-element.34), channel_id=1, source_target_pairs={{0,2},{1,3},{2,4},{3,5},{4,6},{5,7},{6,0},{7,1},{8,14},{9,15},{10,... | collective-permute-start | bytes 983048 | tf_op jit(solution)/shard_map/ppermute | solution.py:331
  61.8 17.0 %collective-permute-start.13 = (bf16[128,1280]{1,0:T(8,128)(2,1)S(1)}, bf16[128,1280]{1,0:T(8,128)(2,1)S(1)}, u32[]{:S(2)}, u32[]{:S(2)}) collective-permute-start(bf16[128,1280]{1,0:T(8,128)(2,1)S(1)} %get-tuple-element.35), channel_id=1, source_target_pairs={{0,4},{1,5},{2,6},{3,7},{4,0},{5,1},{6,2},{7,3},{8,12},{9,13},{10,... | collective-permute-start | bytes 983048 | tf_op jit(solution)/shard_map/ppermute | solution.py:331
  64.9 13.8 %collective-permute-start.14 = (bf16[128,1280]{1,0:T(8,128)(2,1)S(1)}, bf16[128,1280]{1,0:T(8,128)(2,1)S(1)}, u32[]{:S(2)}, u32[]{:S(2)}) collective-permute-start(bf16[128,1280]{1,0:T(8,128)(2,1)S(1)} %get-tuple-element.36), channel_id=1, source_target_pairs={{0,6},{1,7},{2,0},{3,1},{4,2},{5,3},{6,4},{7,5},{8,10},{9,11},{10,... | collective-permute-start | bytes 983048 | tf_op jit(solution)/shard_map/ppermute | solution.py:331
  78.9 7.2 %collective-permute-start.15 = (bf16[128,1280]{1,0:T(8,128)(2,1)S(1)}, bf16[128,1280]{1,0:T(8,128)(2,1)S(1)}, u32[]{:S(2)}, u32[]{:S(2)}) collective-permute-start(bf16[128,1280]{1,0:T(8,128)(2,1)S(1)} %add_convert_fusion.8), channel_id=1, source_target_pairs={{0,1},{1,0},{2,3},{3,2},{4,5},{5,4},{6,7},{7,6},{8,9},{9,8},{10,11... | collective-permute-start | bytes 983048 | tf_op jit(solution)/shard_map/ppermute | solution.py:313
  86.2 6.8 %collective-permute-start.16 = (bf16[128,1280]{1,0:T(8,128)(2,1)S(1)}, bf16[128,1280]{1,0:T(8,128)(2,1)S(1)}, u32[]{:S(2)}, u32[]{:S(2)}) collective-permute-start(bf16[128,1280]{1,0:T(8,128)(2,1)S(1)} %fusion), channel_id=1, source_target_pairs={{16,1},{17,0},{18,3},{19,2},{20,5},{21,4},{22,7},{23,6},{24,9},{25... | collective-permute-start | bytes 983048 | tf_op jit(solution)/shard_map/ppermute | solution.py:313
  88.5 13.0 %collective-permute-start.18 = (bf16[5120,128]{1,0:T(8,128)(2,1)S(1)}, bf16[5120,128]{1,0:T(8,128)(2,1)}, u32[]{:S(2)}, u32[]{:S(2)}) collective-permute-start(bf16[5120,128]{1,0:T(8,128)(2,1)S(1)} %bitcast.88), channel_id=1, source_target_pairs={{0,8},{8,0},{16,24},{24,16},{1,9},{9,1},{17,25},{25,17},{2,10},{10... | collective-permute-start | bytes 3932168 | tf_op jit(solution)/shard_map/ppermute | solution.py:300
  88.6 12.9 %collective-permute-start.19 = (bf16[5120,128]{1,0:T(8,128)(2,1)S(1)}, bf16[5120,128]{1,0:T(8,128)(2,1)}, u32[]{:S(2)}, u32[]{:S(2)}) collective-permute-start(bf16[5120,128]{1,0:T(8,128)(2,1)S(1)} %bitcast.93), channel_id=1, source_target_pairs={{0,8},{8,0},{16,24},{24,16},{1,9},{9,1},{17,25},{25,17},{2,10},{10... | collective-permute-start | bytes 3932168 | tf_op jit(solution)/shard_map/ppermute | solution.py:300
  94.3 19.0 %all-to-all-start = ((bf16[4,128,1280]{2,1,0:T(8,128)(2,1)}), bf16[4,128,1280]{2,1,0:T(8,128)(2,1)}, u32[]{:S(2)}, u32[]{:S(2)}) async-start(bf16[4,128,1280]{2,1,0:T(8,128)(2,1)} %broadcast_in_dim.36), calls=%async_computation | async-start | bytes 2621440 | tf_op jit(solution)/shard_map/all_to_all | solution.py:316
  139.0 7.2 %collective-permute-start.20 = (bf16[128,1280]{1,0:T(8,128)(2,1)S(1)}, bf16[128,1280]{1,0:T(8,128)(2,1)S(1)}, u32[]{:S(2)}, u32[]{:S(2)}) collective-permute-start(bf16[128,1280]{1,0:T(8,128)(2,1)S(1)} %add_convert_fusion.6), channel_id=1, source_target_pairs={{0,1},{1,0},{2,3},{3,2},{4,5},{5,4},{6,7},{7,6},{8,9},{9,8},{10,11... | collective-permute-start | bytes 983048 | tf_op jit(solution)/shard_map/ppermute | solution.py:313
  147.4 15.8 %all-to-all-start.2 = ((bf16[4,128,1280]{2,1,0:T(8,128)(2,1)}), bf16[4,128,1280]{2,1,0:T(8,128)(2,1)S(1)}, u32[]{:S(2)}, u32[]{:S(2)}) async-start(bf16[4,128,1280]{2,1,0:T(8,128)(2,1)} %broadcast_in_dim.37), calls=%async_computation.2 | async-start | bytes 2621440 | tf_op jit(solution)/shard_map/all_to_all | solution.py:316
  189.0 10.6 %collective-permute-start.21 = (bf16[128,1280]{1,0:T(8,128)(2,1)S(1)}, bf16[128,1280]{1,0:T(8,128)(2,1)S(1)}, u32[]{:S(2)}, u32[]{:S(2)}) collective-permute-start(bf16[128,1280]{1,0:T(8,128)(2,1)S(1)} %add_convert_fusion.4), channel_id=1, source_target_pairs={{0,16},{1,17},{2,18},{3,19},{4,20},{5,21},{6,22},{7,23},{8,24},{9,... | collective-permute-start | bytes 983048 | tf_op jit(solution)/shard_map/ppermute | solution.py:313
  190.3 12.7 %collective-permute-start.22 = (bf16[128,1280]{1,0:T(8,128)(2,1)S(1)}, bf16[128,1280]{1,0:T(8,128)(2,1)S(1)}, u32[]{:S(2)}, u32[]{:S(2)}) collective-permute-start(bf16[128,1280]{1,0:T(8,128)(2,1)S(1)} %add_convert_fusion.4), channel_id=1, source_target_pairs={{0,17},{1,16},{2,19},{3,18},{4,21},{5,20},{6,23},{7,22},{8,25},{9,... | collective-permute-start | bytes 983048 | tf_op jit(solution)/shard_map/ppermute | solution.py:313
  243.3 7.2 %collective-permute-start.23 = (bf16[128,1280]{1,0:T(8,128)(2,1)S(1)}, bf16[128,1280]{1,0:T(8,128)(2,1)S(1)}, u32[]{:S(2)}, u32[]{:S(2)}) collective-permute-start(bf16[128,1280]{1,0:T(8,128)(2,1)S(1)} %add_convert_fusion.2), channel_id=1, source_target_pairs={{0,1},{1,0},{2,3},{3,2},{4,5},{5,4},{6,7},{7,6},{8,9},{9,8},{10,11... | collective-permute-start | bytes 983048 | tf_op jit(solution)/shard_map/ppermute | solution.py:313
  251.7 15.9 %all-to-all-start.6 = ((bf16[4,128,1280]{2,1,0:T(8,128)(2,1)}), bf16[4,128,1280]{2,1,0:T(8,128)(2,1)S(1)}, u32[]{:S(2)}, u32[]{:S(2)}) async-start(bf16[4,128,1280]{2,1,0:T(8,128)(2,1)} %broadcast_in_dim.39), calls=%async_computation.6 | async-start | bytes 2621440 | tf_op jit(solution)/shard_map/all_to_all | solution.py:316
  277.3 15.8 %all-to-all-start.7 = ((bf16[4,128,1280]{2,1,0:T(8,128)(2,1)}), bf16[4,128,1280]{2,1,0:T(8,128)(2,1)S(1)}, u32[]{:S(2)}, u32[]{:S(2)}) async-start(bf16[4,128,1280]{2,1,0:T(8,128)(2,1)} %decoder_layer.7), calls=%async_computation.7 | async-start | bytes 2621440 | tf_op jit(solution)/shard_map/all_to_all | solution.py:316
  294.9 5.6 %collective-permute-start.24 = (bf16[4,16,1280]{2,1,0:T(8,128)(2,1)S(1)}, bf16[4,16,1280]{2,1,0:T(8,128)(2,1)S(1)}, u32[]{:S(2)}, u32[]{:S(2)}) collective-permute-start(bf16[4,16,1280]{2,1,0:T(8,128)(2,1)S(1)} %get-tuple-element.45), channel_id=1, source_target_pairs={{16,0},{17,1},{18,2},{19,3},{20,4},{21,5},{22,6},{23,7},{24,8},{25... | collective-permute-start | bytes 491528 | tf_op jit(solution)/shard_map/ppermute | solution.py:313
  297.7 7.2 %collective-permute-start.26 = (bf16[4,16,1280]{2,1,0:T(8,128)(2,1)S(1)}, bf16[4,16,1280]{2,1,0:T(8,128)(2,1)S(1)}, u32[]{:S(2)}, u32[]{:S(2)}) collective-permute-start(bf16[4,16,1280]{2,1,0:T(8,128)(2,1)S(1)} %get-tuple-element.47), channel_id=1, source_target_pairs={{16,17},{17,16},{18,19},{19,18},{20,21},{21,20},{22,23},{23,22},{2... | collective-permute-start | bytes 491528 | tf_op jit(solution)/shard_map/ppermute | solution.py:313
  305.1 9.2 %collective-permute-start.27 = (bf16[16,1280]{1,0:T(8,128)(2,1)S(1)}, bf16[16,1280]{1,0:T(8,128)(2,1)S(1)}, u32[]{:S(2)}, u32[]{:S(2)}) collective-permute-start(bf16[16,1280]{1,0:T(8,128)(2,1)S(1)} %get-tuple-element.52), channel_id=1, source_target_pairs={{0,0},{1,1},{2,32},{3,33},{4,64},{5,65},{6,96},{7,97},{32,2},{33,3... | collective-permute-start | bytes 122888 | tf_op jit(solution)/shard_map/ppermute | solution.py:445
  308.1 7.7 %collective-permute-start.28 = (bf16[16,1280]{1,0:T(8,128)(2,1)S(1)}, bf16[16,1280]{1,0:T(8,128)(2,1)S(1)}, u32[]{:S(2)}, u32[]{:S(2)}) collective-permute-start(bf16[16,1280]{1,0:T(8,128)(2,1)S(1)} %get-tuple-element.55), channel_id=1, source_target_pairs={{0,32},{1,33},{2,64},{3,65},{4,96},{5,97},{6,0},{7,1},{32,34},{33,... | collective-permute-start | bytes 122888 | tf_op jit(solution)/shard_map/ppermute | solution.py:445
  312.9 6.1 %collective-permute-start.29 = (bf16[16,1280]{1,0:T(8,128)(2,1)S(1)}, bf16[16,1280]{1,0:T(8,128)(2,1)S(1)}, u32[]{:S(2)}, u32[]{:S(2)}) collective-permute-start(bf16[16,1280]{1,0:T(8,128)(2,1)S(1)} %get-tuple-element.54), channel_id=1, source_target_pairs={{0,64},{1,65},{2,96},{3,97},{4,0},{5,1},{6,32},{7,33},{32,66},{33,... | collective-permute-start | bytes 122888 | tf_op jit(solution)/shard_map/ppermute | solution.py:445
  313.8 5.4 %collective-permute-start.30 = (bf16[16,1280]{1,0:T(8,128)(2,1)S(1)}, bf16[16,1280]{1,0:T(8,128)(2,1)S(1)}, u32[]{:S(2)}, u32[]{:S(2)}) collective-permute-start(bf16[16,1280]{1,0:T(8,128)(2,1)S(1)} %get-tuple-element.53), channel_id=1, source_target_pairs={{0,96},{1,97},{2,0},{3,1},{4,32},{5,33},{6,64},{7,65},{32,98},{33,... | collective-permute-start | bytes 122888 | tf_op jit(solution)/shard_map/ppermute | solution.py:445
  (15 other events, 127.0 us)

commit v4 on v3

--- a/solution.py
+++ b/solution.py
@@ -259,7 +259,7 @@
             pltpu.VMEM((count, q_cols, depth), BF),
             pltpu.SemaphoreType.DMA((5, count)),
         ],
-        compiler_params=pltpu.CompilerParams(vmem_limit_bytes=60 << 20),
+        compiler_params=pltpu.CompilerParams(vmem_limit_bytes=50 << 20),
         cost_estimate=pl.CostEstimate(
             flops=2 * rows * weights, bytes_accessed=2 * weights, transcendentals=rows * rows * 4
         ),

time: 321 us -> 308 us (0.960)
  Pallas kernels: 45.1 us -> 38 us
  blocking collectives: 63.9 us -> 60.5 us
    pallas_call x4, Pallas kernels: 34.5 us -> 27.4 us  [decoder_layer(): pl.pallas_call(layer_kernel, out_shape=jax.ShapeDtypeStruct(blocks.shape,...]
    all_to_all x4, blocking collectives: 63.9 us -> 60.5 us  [z_all_to_all(): lax.all_to_all(value, 'tp', split_axis=0, concat_axis=0, tiled=True, axis...]
  transfers between devices with their start and end apart: 35 -> 35, of which waited for: 26 -> 27; matrix products, arithmetic and copies ran while one was open for 4% -> 3% of each run, Pallas kernels for 2% -> 2%
where the time goes in v4:
time: 308 us; the launch traced here: 307 us
  waiting for transfers between devices  137 us (44%)
  blocking collectives  60.5 us (20%)
  starting transfers between devices  54 us (18%)
  Pallas kernels  38 us (12%)
  local copies, waits for them, and re-layouts  8.9 us (3%)
  other arithmetic  8.57 us (3%)
    all_to_all x4, blocking collectives, z_all_to_all(): lax.all_to_all(value, 'tp', split_axis=0, concat_axis=0, tiled=True, axis...  60.5 us
    ppermute x11, waiting for transfers between devices, y_move(): return lax.ppermute(value, ('section', 'tp'), pairs)  51.2 us
    all_to_all x4, waiting for transfers between devices, z_all_to_all(): lax.all_to_all(value, 'tp', split_axis=0, concat_axis=0, tiled=True, axis...  48.1 us
    ppermute x9, waiting for transfers between devices, z_move(): return lax.ppermute(value, ('section', 'tp'), pairs)  31.9 us
    pallas_call x4, Pallas kernels, decoder_layer(): pl.pallas_call(layer_kernel, out_shape=jax.ShapeDtypeStruct(blocks.shape,...  27.4 us
    ppermute x9, starting transfers between devices, z_move(): return lax.ppermute(value, ('section', 'tp'), pairs)  15.1 us
    all_to_all x4, starting transfers between devices, z_all_to_all(): lax.all_to_all(value, 'tp', split_axis=0, concat_axis=0, tiled=True, axis...  14.6 us
    ppermute x11, starting transfers between devices, y_move(): return lax.ppermute(value, ('section', 'tp'), pairs)  12.2 us
  transfers between devices with their start and end apart: 35, of which 27 were waited for; matrix products, arithmetic and copies ran while one was open for 3% of the time, Pallas kernels for 2%

profile of v4, /device:TPU:30, one launch (start us, length us, event | category | flops | bytes accessed | tf_op | source)
XLA Modules:
  0.0 307.4 jit_solution(17848987269047933423)
XLA Ops:
  1.1 5.4 %encoder_units.1 = (bf16[64,1280]{1,0:T(8,128)(2,1)}, bf16[64,1280]{1,0:T(8,128)(2,1)}, bf16[64,1280]{1,0:T(8,128)(2,1)}, bf16[64,1280]{1,0:T(8,128)(2,1)}) custom-call(s32[2]{0:T(128)} %pad_add_fusion.place, bf16[256,1280]{1,0:T(8,128)(2,1)} %bitcast.94, bf16[1280]{0:T(1024)(128)(2,1)} %gain_ref.1, bf16[1280]{0:T(1024)(128)(2,1)} %bias_ref.1, ...), custom_call_target="tpu_custom_call" | custom-call | flops 838860800 | bytes 3276800 | tf_op jit(solution)/shard_map/encoder_units/pallas_call | solution.py:97
  10.5 3.8 %collective-permute-done = bf16[64,1280]{1,0:T(8,128)(2,1)} collective-permute-done((bf16[64,1280]{1,0:T(8,128)(2,1)}, bf16[64,1280]{1,0:T(8,128)(2,1)}, u32[]{:S(2)}, u32[]{:S(2)}) %collective-permute-start) | collective-permute-done | bytes 163872 | tf_op jit(solution)/shard_map/ppermute | solution.py:331
  29.4 4.6 %collective-permute-done.3 = bf16[64,1280]{1,0:T(8,128)(2,1)S(1)} collective-permute-done((bf16[64,1280]{1,0:T(8,128)(2,1)S(1)}, bf16[64,1280]{1,0:T(8,128)(2,1)S(1)}, u32[]{:S(2)}, u32[]{:S(2)}) %collective-permute-start.3) | collective-permute-done | bytes 163872 | tf_op jit(solution)/shard_map/ppermute | solution.py:313
  34.4 6.4 %collective-permute-done.8 = bf16[64,1280]{1,0:T(8,128)(2,1)} collective-permute-done((bf16[64,1280]{1,0:T(8,128)(2,1)S(1)}, bf16[64,1280]{1,0:T(8,128)(2,1)}, u32[]{:S(2)}, u32[]{:S(2)}) %collective-permute-start.8) | collective-permute-done | bytes 163872 | tf_op jit(solution)/shard_map/ppermute | solution.py:313
  46.3 6.7 %collective-permute-done.10.x2 = bf16[128,1280]{1,0:T(8,128)(2,1)S(1)} collective-permute-done((bf16[128,1280]{1,0:T(8,128)(2,1)S(1)}, bf16[128,1280]{1,0:T(8,128)(2,1)S(1)}, u32[]{:S(2)}, u32[]{:S(2)}) %collective-permute-start.10) | collective-permute-done | bytes 327712 | tf_op jit(solution)/shard_map/ppermute | solution.py:331
  56.4 5.2 %adapter_units.1 = (bf16[128,1280]{1,0:T(8,128)(2,1)S(1)}, bf16[128,1280]{1,0:T(8,128)(2,1)S(1)}, bf16[128,1280]{1,0:T(8,128)(2,1)S(1)}, bf16[128,1280]{1,0:T(8,128)(2,1)S(1)}) custom-call(s32[2]{0:T(128)S(1)} %copy-done.3, bf16[128,1280]{1,0:T(8,128)(2,1)S(1)} %bitcast.78, bf16[128,1280]{1,0:T(8,128)(2,1)S(1)} %collective-permute-done.9.x1, ...), custom_call_target="tpu_custom_call" | custom-call | flops 838860800 | bytes 6553600 | tf_op jit(solution)/shard_map/adapter_units/pallas_call | solution.py:153
  61.7 3.2 %collective-permute-start.13 = (bf16[128,1280]{1,0:T(8,128)(2,1)S(1)}, bf16[128,1280]{1,0:T(8,128)(2,1)S(1)}, u32[]{:S(2)}, u32[]{:S(2)}) collective-permute-start(bf16[128,1280]{1,0:T(8,128)(2,1)S(1)} %get-tuple-element.35), channel_id=1, source_target_pairs={{0,4},{1,5},{2,6},{3,7},{4,0},{5,1},{6,2},{7,3},{8,12},{9,13},{10,... | collective-permute-start | bytes 983048 | tf_op jit(solution)/shard_map/ppermute | solution.py:331
  65.5 10.7 %collective-permute-done.12 = bf16[128,1280]{1,0:T(8,128)(2,1)S(1)} collective-permute-done((bf16[128,1280]{1,0:T(8,128)(2,1)S(1)}, bf16[128,1280]{1,0:T(8,128)(2,1)S(1)}, u32[]{:S(2)}, u32[]{:S(2)}) %collective-permute-start.12) | collective-permute-done | bytes 327712 | tf_op jit(solution)/shard_map/ppermute | solution.py:331
  79.0 7.1 %collective-permute-done.15 = bf16[128,1280]{1,0:T(8,128)(2,1)S(1)} collective-permute-done((bf16[128,1280]{1,0:T(8,128)(2,1)S(1)}, bf16[128,1280]{1,0:T(8,128)(2,1)S(1)}, u32[]{:S(2)}, u32[]{:S(2)}) %collective-permute-start.15) | collective-permute-done | bytes 327712 | tf_op jit(solution)/shard_map/ppermute | solution.py:313
  89.0 4.0 %collective-permute-done.16 = bf16[128,1280]{1,0:T(8,128)(2,1)S(1)} collective-permute-done((bf16[128,1280]{1,0:T(8,128)(2,1)S(1)}, bf16[128,1280]{1,0:T(8,128)(2,1)S(1)}, u32[]{:S(2)}, u32[]{:S(2)}) %collective-permute-start.16) | collective-permute-done | bytes 327712 | tf_op jit(solution)/shard_map/ppermute | solution.py:313
  94.3 3.9 %all-to-all-start = ((bf16[4,128,1280]{2,1,0:T(8,128)(2,1)}), bf16[4,128,1280]{2,1,0:T(8,128)(2,1)S(1)}, u32[]{:S(2)}, u32[]{:S(2)}) async-start(bf16[4,128,1280]{2,1,0:T(8,128)(2,1)} %broadcast_in_dim.36), calls=%async_computation | async-start | bytes 2621440 | tf_op jit(solution)/shard_map/all_to_all | solution.py:316
  99.5 13.4 %all-to-all-done.x_hbm = bf16[4,128,1280]{2,1,0:T(8,128)(2,1)S(1)} async-done(((bf16[4,128,1280]{2,1,0:T(8,128)(2,1)}), bf16[4,128,1280]{2,1,0:T(8,128)(2,1)S(1)}, u32[]{:S(2)}, u32[]{:S(2)}) %all-to-all-start) | async-done | bytes 1310752 | tf_op jit(solution)/shard_map/all_to_all | solution.py:316
  112.9 6.5 %decoder_layer.4 = bf16[4,128,1280]{2,1,0:T(8,128)(2,1)S(1)} custom-call(s32[1]{0:T(128)} %bitcast.8.which, bf16[4,128,1280]{2,1,0:T(8,128)(2,1)S(1)} %all-to-all-done.x_hbm, f32[1,5120]{1,0:T(1,128)S(1)} %get-tuple-element.57.gain0, f32[1,5120]{1,0:T(1,128)S(1)} %bitcast.79, f32[128,128]{1,0:T(8,128)S(1)} %fusion.9.mask_ref, bf16[5120,512]{1,0:T(8,128)(2,1)} %bitcast.84, ...), custom_call_target="tpu_custom_call" | custom-call | flops 1677721600 | bytes 13107200 | tf_op jit(solution)/shard_map/decoder_layer/pallas_call | solution.py:249
  119.4 16.3 %all_to_all.40 = bf16[4,128,1280]{2,1,0:T(8,128)(2,1)S(1)} all-to-all(bf16[4,128,1280]{2,1,0:T(8,128)(2,1)S(1)} %decoder_layer.4), channel_id=1, replica_groups={{0,2,4,6},{1,3,5,7},{8,10,12,14},{9,11,13,15},{16,18,20,22},{17,19,21,2..., dimensions={0} | all-to-all | bytes 2621440 | tf_op jit(solution)/shard_map/all_to_all | solution.py:316
  136.1 7.1 %collective-permute-done.20 = bf16[128,1280]{1,0:T(8,128)(2,1)S(1)} collective-permute-done((bf16[128,1280]{1,0:T(8,128)(2,1)S(1)}, bf16[128,1280]{1,0:T(8,128)(2,1)S(1)}, u32[]{:S(2)}, u32[]{:S(2)}) %collective-permute-start.20) | collective-permute-done | bytes 327712 | tf_op jit(solution)/shard_map/ppermute | solution.py:313
  144.3 3.5 %all-to-all-start.2 = ((bf16[4,128,1280]{2,1,0:T(8,128)(2,1)}), bf16[4,128,1280]{2,1,0:T(8,128)(2,1)S(1)}, u32[]{:S(2)}, u32[]{:S(2)}) async-start(bf16[4,128,1280]{2,1,0:T(8,128)(2,1)} %broadcast_in_dim.37), calls=%async_computation.2 | async-start | bytes 2621440 | tf_op jit(solution)/shard_map/all_to_all | solution.py:316
  147.9 12.3 %all-to-all-done.2.x_hbm = bf16[4,128,1280]{2,1,0:T(8,128)(2,1)S(1)} async-done(((bf16[4,128,1280]{2,1,0:T(8,128)(2,1)}), bf16[4,128,1280]{2,1,0:T(8,128)(2,1)S(1)}, u32[]{:S(2)}, u32[]{:S(2)}) %all-to-all-start.2) | async-done | bytes 1310752 | tf_op jit(solution)/shard_map/all_to_all | solution.py:316
  160.2 6.7 %decoder_layer.5 = bf16[4,128,1280]{2,1,0:T(8,128)(2,1)S(1)} custom-call(s32[1]{0:T(128)} %bitcast.7.which, bf16[4,128,1280]{2,1,0:T(8,128)(2,1)S(1)} %all-to-all-done.2.x_hbm, f32[1,5120]{1,0:T(1,128)S(1)} %get-tuple-element.57.gain0, f32[1,5120]{1,0:T(1,128)S(1)} %bitcast.80, f32[128,128]{1,0:T(8,128)S(1)} %fusion.9.mask_ref, bf16[5120,512]{1,0:T(8,128)(2,1)} %bitcast.85, ...), custom_call_target="tpu_custom_call" | custom-call | flops 1677721600 | bytes 13107200 | tf_op jit(solution)/shard_map/decoder_layer/pallas_call | solution.py:249
  166.8 14.7 %all_to_all.41 = bf16[4,128,1280]{2,1,0:T(8,128)(2,1)S(1)} all-to-all(bf16[4,128,1280]{2,1,0:T(8,128)(2,1)S(1)} %decoder_layer.5), channel_id=1, replica_groups={{0,2,4,6},{1,3,5,7},{8,10,12,14},{9,11,13,15},{16,18,20,22},{17,19,21,2..., dimensions={0} | all-to-all | bytes 2621440 | tf_op jit(solution)/shard_map/all_to_all | solution.py:316
  184.4 8.0 %collective-permute-done.21 = bf16[128,1280]{1,0:T(8,128)(2,1)S(1)} collective-permute-done((bf16[128,1280]{1,0:T(8,128)(2,1)S(1)}, bf16[128,1280]{1,0:T(8,128)(2,1)S(1)}, u32[]{:S(2)}, u32[]{:S(2)}) %collective-permute-start.21) | collective-permute-done | bytes 327712 | tf_op jit(solution)/shard_map/ppermute | solution.py:313
  192.4 3.4 %collective-permute-done.22 = bf16[128,1280]{1,0:T(8,128)(2,1)S(1)} collective-permute-done((bf16[128,1280]{1,0:T(8,128)(2,1)S(1)}, bf16[128,1280]{1,0:T(8,128)(2,1)S(1)}, u32[]{:S(2)}, u32[]{:S(2)}) %collective-permute-start.22) | collective-permute-done | bytes 327712 | tf_op jit(solution)/shard_map/ppermute | solution.py:313
  196.0 14.7 %all_to_all.42.x_hbm = bf16[4,128,1280]{2,1,0:T(8,128)(2,1)S(1)} all-to-all(bf16[4,128,1280]{2,1,0:T(8,128)(2,1)S(1)} %broadcast_in_dim.38), channel_id=1, replica_groups={{0,2,4,6},{1,3,5,7},{8,10,12,14},{9,11,13,15},{16,18,20,22},{17,19,21,2..., dimensions={0} | all-to-all | bytes 2621440 | tf_op jit(solution)/shard_map/all_to_all | solution.py:316
  210.7 6.5 %decoder_layer.6 = bf16[4,128,1280]{2,1,0:T(8,128)(2,1)S(1)} custom-call(s32[1]{0:T(128)} %bitcast.8.which, bf16[4,128,1280]{2,1,0:T(8,128)(2,1)S(1)} %all_to_all.42.x_hbm, f32[1,5120]{1,0:T(1,128)S(1)} %get-tuple-element.57.gain0, f32[1,5120]{1,0:T(1,128)S(1)} %bitcast.81, f32[128,128]{1,0:T(8,128)S(1)} %fusion.9.mask_ref, bf16[5120,512]{1,0:T(8,128)(2,1)} %bitcast.86, ...), custom_call_target="tpu_custom_call" | custom-call | flops 1677721600 | bytes 13107200 | tf_op jit(solution)/shard_map/decoder_layer/pallas_call | solution.py:249
  217.2 14.7 %all_to_all.43 = bf16[4,128,1280]{2,1,0:T(8,128)(2,1)S(1)} all-to-all(bf16[4,128,1280]{2,1,0:T(8,128)(2,1)S(1)} %decoder_layer.6), channel_id=1, replica_groups={{0,2,4,6},{1,3,5,7},{8,10,12,14},{9,11,13,15},{16,18,20,22},{17,19,21,2..., dimensions={0} | all-to-all | bytes 2621440 | tf_op jit(solution)/shard_map/all_to_all | solution.py:316
  233.5 5.9 %collective-permute-done.23 = bf16[128,1280]{1,0:T(8,128)(2,1)S(1)} collective-permute-done((bf16[128,1280]{1,0:T(8,128)(2,1)S(1)}, bf16[128,1280]{1,0:T(8,128)(2,1)S(1)}, u32[]{:S(2)}, u32[]{:S(2)}) %collective-permute-start.23) | collective-permute-done | bytes 327712 | tf_op jit(solution)/shard_map/ppermute | solution.py:313
  240.6 3.7 %all-to-all-start.6 = ((bf16[4,128,1280]{2,1,0:T(8,128)(2,1)}), bf16[4,128,1280]{2,1,0:T(8,128)(2,1)S(1)}, u32[]{:S(2)}, u32[]{:S(2)}) async-start(bf16[4,128,1280]{2,1,0:T(8,128)(2,1)} %broadcast_in_dim.39), calls=%async_computation.6 | async-start | bytes 2621440 | tf_op jit(solution)/shard_map/all_to_all | solution.py:316
  246.1 10.5 %all-to-all-done.6.x_hbm = bf16[4,128,1280]{2,1,0:T(8,128)(2,1)S(1)} async-done(((bf16[4,128,1280]{2,1,0:T(8,128)(2,1)}), bf16[4,128,1280]{2,1,0:T(8,128)(2,1)S(1)}, u32[]{:S(2)}, u32[]{:S(2)}) %all-to-all-start.6) | async-done | bytes 1310752 | tf_op jit(solution)/shard_map/all_to_all | solution.py:316
  256.6 7.7 %decoder_layer.7 = bf16[4,128,1280]{2,1,0:T(8,128)(2,1)} custom-call(s32[1]{0:T(128)} %bitcast.7.which, bf16[4,128,1280]{2,1,0:T(8,128)(2,1)S(1)} %all-to-all-done.6.x_hbm, f32[1,5120]{1,0:T(1,128)S(1)} %get-tuple-element.57.gain0, f32[1,5120]{1,0:T(1,128)S(1)} %bitcast.82, f32[128,128]{1,0:T(8,128)S(1)} %fusion.9.mask_ref, bf16[5120,512]{1,0:T(8,128)(2,1)} %bitcast.87, ...), custom_call_target="tpu_custom_call" | custom-call | flops 1677721600 | bytes 13107200 | tf_op jit(solution)/shard_map/decoder_layer/pallas_call | solution.py:249
  264.3 3.6 %all-to-all-start.7 = ((bf16[4,128,1280]{2,1,0:T(8,128)(2,1)}), bf16[4,128,1280]{2,1,0:T(8,128)(2,1)S(1)}, u32[]{:S(2)}, u32[]{:S(2)}) async-start(bf16[4,128,1280]{2,1,0:T(8,128)(2,1)} %decoder_layer.7), calls=%async_computation.7 | async-start | bytes 2621440 | tf_op jit(solution)/shard_map/all_to_all | solution.py:316
  268.2 12.0 %all-to-all-done.7 = bf16[4,128,1280]{2,1,0:T(8,128)(2,1)S(1)} async-done(((bf16[4,128,1280]{2,1,0:T(8,128)(2,1)}), bf16[4,128,1280]{2,1,0:T(8,128)(2,1)S(1)}, u32[]{:S(2)}, u32[]{:S(2)}) %all-to-all-start.7) | async-done | bytes 1310752 | tf_op jit(solution)/shard_map/all_to_all | solution.py:316
  288.2 4.1 %collective-permute-done.26 = bf16[4,16,1280]{2,1,0:T(8,128)(2,1)S(1)} collective-permute-done((bf16[4,16,1280]{2,1,0:T(8,128)(2,1)S(1)}, bf16[4,16,1280]{2,1,0:T(8,128)(2,1)S(1)}, u32[]{:S(2)}, u32[]{:S(2)}) %collective-permute-start.26) | collective-permute-done | bytes 163872 | tf_op jit(solution)/shard_map/ppermute | solution.py:313
  295.4 4.6 %collective-permute-start.28 = (bf16[16,1280]{1,0:T(8,128)(2,1)S(1)}, bf16[16,1280]{1,0:T(8,128)(2,1)S(1)}, u32[]{:S(2)}, u32[]{:S(2)}) collective-permute-start(bf16[16,1280]{1,0:T(8,128)(2,1)S(1)} %get-tuple-element.55), channel_id=1, source_target_pairs={{0,32},{1,33},{2,64},{3,65},{4,96},{5,97},{6,0},{7,1},{32,34},{33,... | collective-permute-start | bytes 122888 | tf_op jit(solution)/shard_map/ppermute | solution.py:445
  (125 shorter events, 65.9 us)
Async XLA Ops:
  0.0 34.0 %collective-permute-start.6 = (bf16[5120,512]{1,0:T(8,128)(2,1)}, bf16[5120,512]{1,0:T(8,128)(2,1)}, u32[]{:S(2)}, u32[]{:S(2)}) collective-permute-start(bf16[5120,512]{1,0:T(8,128)(2,1)} %bitcast.83), channel_id=1, source_target_pairs={{0,8},{8,0},{16,24},{24,16},{1,9},{9,1},{17,25},{25,17},{2,10},{10... | collective-permute-start | bytes 15728648 | tf_op jit(solution)/shard_map/ppermute | solution.py:300
  0.0 34.0 %collective-permute-start.7 = (bf16[512,5120]{1,0:T(8,128)(2,1)}, bf16[512,5120]{1,0:T(8,128)(2,1)}, u32[]{:S(2)}, u32[]{:S(2)}) collective-permute-start(bf16[512,5120]{1,0:T(8,128)(2,1)} %bitcast.88), channel_id=1, source_target_pairs={{0,8},{8,0},{16,24},{24,16},{1,9},{9,1},{17,25},{25,17},{2,10},{10... | collective-permute-start | bytes 15728648 | tf_op jit(solution)/shard_map/ppermute | solution.py:300
  6.6 7.7 %collective-permute-start = (bf16[64,1280]{1,0:T(8,128)(2,1)}, bf16[64,1280]{1,0:T(8,128)(2,1)}, u32[]{:S(2)}, u32[]{:S(2)}) collective-permute-start(bf16[64,1280]{1,0:T(8,128)(2,1)} %get-tuple-element.25), channel_id=1, source_target_pairs={{0,2},{1,3},{2,4},{3,5},{4,6},{5,7},{6,0},{7,1},{8,14},{9,15},{10,... | collective-permute-start | bytes 491528 | tf_op jit(solution)/shard_map/ppermute | solution.py:331
  8.6 25.5 %collective-permute-start.4 = (bf16[160,5120]{1,0:T(8,128)(2,1)S(1)}, bf16[160,5120]{1,0:T(8,128)(2,1)}, u32[]{:S(2)}, u32[]{:S(2)}) collective-permute-start(bf16[160,5120]{1,0:T(8,128)(2,1)S(1)} %bitcast.73), channel_id=1, source_target_pairs={{0,8},{8,0},{16,24},{24,16},{1,9},{9,1},{17,25},{25,17},{2,10},{10... | collective-permute-start | bytes 4915208 | tf_op jit(solution)/shard_map/ppermute | solution.py:300
  10.4 23.6 %collective-permute-start.5 = (bf16[160,5120]{1,0:T(8,128)(2,1)S(1)}, bf16[160,5120]{1,0:T(8,128)(2,1)}, u32[]{:S(2)}, u32[]{:S(2)}) collective-permute-start(bf16[160,5120]{1,0:T(8,128)(2,1)S(1)} %copy-done.2), channel_id=1, source_target_pairs={{0,8},{8,0},{16,24},{24,16},{1,9},{9,1},{17,25},{25,17},{2,10},{10... | collective-permute-start | bytes 4915208 | tf_op jit(solution)/shard_map/ppermute | solution.py:300
  14.3 7.1 %collective-permute-start.1 = (bf16[64,1280]{1,0:T(8,128)(2,1)}, bf16[64,1280]{1,0:T(8,128)(2,1)}, u32[]{:S(2)}, u32[]{:S(2)}) collective-permute-start(bf16[64,1280]{1,0:T(8,128)(2,1)} %get-tuple-element.26), channel_id=1, source_target_pairs={{0,4},{1,5},{2,6},{3,7},{4,0},{5,1},{6,2},{7,3},{8,12},{9,13},{10,... | collective-permute-start | bytes 491528 | tf_op jit(solution)/shard_map/ppermute | solution.py:331
  21.4 6.0 %collective-permute-start.2 = (bf16[64,1280]{1,0:T(8,128)(2,1)}, bf16[64,1280]{1,0:T(8,128)(2,1)S(1)}, u32[]{:S(2)}, u32[]{:S(2)}) collective-permute-start(bf16[64,1280]{1,0:T(8,128)(2,1)} %get-tuple-element.27), channel_id=1, source_target_pairs={{0,6},{1,7},{2,0},{3,1},{4,2},{5,3},{6,4},{7,5},{8,10},{9,11},{10,... | collective-permute-start | bytes 491528 | tf_op jit(solution)/shard_map/ppermute | solution.py:331
  28.6 5.4 %collective-permute-start.3 = (bf16[64,1280]{1,0:T(8,128)(2,1)S(1)}, bf16[64,1280]{1,0:T(8,128)(2,1)S(1)}, u32[]{:S(2)}, u32[]{:S(2)}) collective-permute-start(bf16[64,1280]{1,0:T(8,128)(2,1)S(1)} %fusion.4), channel_id=1, source_target_pairs={{0,1},{1,0},{2,3},{3,2},{4,5},{5,4},{6,7},{7,6},{8,9},{9,8},{10,11... | collective-permute-start | bytes 491528 | tf_op jit(solution)/shard_map/ppermute | solution.py:313
  34.1 6.7 %collective-permute-start.8 = (bf16[64,1280]{1,0:T(8,128)(2,1)S(1)}, bf16[64,1280]{1,0:T(8,128)(2,1)}, u32[]{:S(2)}, u32[]{:S(2)}) collective-permute-start(bf16[64,1280]{1,0:T(8,128)(2,1)S(1)} %add_convert_fusion.9), channel_id=1, source_target_pairs={{0,17},{1,16},{2,19},{3,18},{4,21},{5,20},{6,23},{7,22},{8,25},{9,... | collective-permute-start | bytes 491528 | tf_op jit(solution)/shard_map/ppermute | solution.py:313
  41.8 11.2 %collective-permute-start.10 = (bf16[128,1280]{1,0:T(8,128)(2,1)S(1)}, bf16[128,1280]{1,0:T(8,128)(2,1)S(1)}, u32[]{:S(2)}, u32[]{:S(2)}) collective-permute-start(bf16[128,1280]{1,0:T(8,128)(2,1)S(1)} %bitcast.75), channel_id=1, source_target_pairs={{0,4},{1,5},{2,6},{3,7},{4,0},{5,1},{6,2},{7,3},{8,12},{9,13},{10,... | collective-permute-start | bytes 983048 | tf_op jit(solution)/shard_map/ppermute | solution.py:331
  43.7 11.9 %collective-permute-start.11 = (bf16[128,1280]{1,0:T(8,128)(2,1)S(1)}, bf16[128,1280]{1,0:T(8,128)(2,1)S(1)}, u32[]{:S(2)}, u32[]{:S(2)}) collective-permute-start(bf16[128,1280]{1,0:T(8,128)(2,1)S(1)} %bitcast.76), channel_id=1, source_target_pairs={{0,6},{1,7},{2,0},{3,1},{4,2},{5,3},{6,4},{7,5},{8,10},{9,11},{10,... | collective-permute-start | bytes 983048 | tf_op jit(solution)/shard_map/ppermute | solution.py:331
  45.6 10.9 %collective-permute-start.9 = (bf16[128,1280]{1,0:T(8,128)(2,1)S(1)}, bf16[128,1280]{1,0:T(8,128)(2,1)S(1)}, u32[]{:S(2)}, u32[]{:S(2)}) collective-permute-start(bf16[128,1280]{1,0:T(8,128)(2,1)S(1)} %bitcast.77), channel_id=1, source_target_pairs={{0,2},{1,3},{2,4},{3,5},{4,6},{5,7},{6,0},{7,1},{8,14},{9,15},{10,... | collective-permute-start | bytes 983048 | tf_op jit(solution)/shard_map/ppermute | solution.py:331
  61.7 14.6 %collective-permute-start.12 = (bf16[128,1280]{1,0:T(8,128)(2,1)S(1)}, bf16[128,1280]{1,0:T(8,128)(2,1)S(1)}, u32[]{:S(2)}, u32[]{:S(2)}) collective-permute-start(bf16[128,1280]{1,0:T(8,128)(2,1)S(1)} %get-tuple-element.34), channel_id=1, source_target_pairs={{0,2},{1,3},{2,4},{3,5},{4,6},{5,7},{6,0},{7,1},{8,14},{9,15},{10,... | collective-permute-start | bytes 983048 | tf_op jit(solution)/shard_map/ppermute | solution.py:331
  61.7 17.0 %collective-permute-start.13 = (bf16[128,1280]{1,0:T(8,128)(2,1)S(1)}, bf16[128,1280]{1,0:T(8,128)(2,1)S(1)}, u32[]{:S(2)}, u32[]{:S(2)}) collective-permute-start(bf16[128,1280]{1,0:T(8,128)(2,1)S(1)} %get-tuple-element.35), channel_id=1, source_target_pairs={{0,4},{1,5},{2,6},{3,7},{4,0},{5,1},{6,2},{7,3},{8,12},{9,13},{10,... | collective-permute-start | bytes 983048 | tf_op jit(solution)/shard_map/ppermute | solution.py:331
  64.9 13.8 %collective-permute-start.14 = (bf16[128,1280]{1,0:T(8,128)(2,1)S(1)}, bf16[128,1280]{1,0:T(8,128)(2,1)S(1)}, u32[]{:S(2)}, u32[]{:S(2)}) collective-permute-start(bf16[128,1280]{1,0:T(8,128)(2,1)S(1)} %get-tuple-element.36), channel_id=1, source_target_pairs={{0,6},{1,7},{2,0},{3,1},{4,2},{5,3},{6,4},{7,5},{8,10},{9,11},{10,... | collective-permute-start | bytes 983048 | tf_op jit(solution)/shard_map/ppermute | solution.py:331
  78.9 7.2 %collective-permute-start.15 = (bf16[128,1280]{1,0:T(8,128)(2,1)S(1)}, bf16[128,1280]{1,0:T(8,128)(2,1)S(1)}, u32[]{:S(2)}, u32[]{:S(2)}) collective-permute-start(bf16[128,1280]{1,0:T(8,128)(2,1)S(1)} %add_convert_fusion.8), channel_id=1, source_target_pairs={{0,1},{1,0},{2,3},{3,2},{4,5},{5,4},{6,7},{7,6},{8,9},{9,8},{10,11... | collective-permute-start | bytes 983048 | tf_op jit(solution)/shard_map/ppermute | solution.py:313
  86.2 6.8 %collective-permute-start.16 = (bf16[128,1280]{1,0:T(8,128)(2,1)S(1)}, bf16[128,1280]{1,0:T(8,128)(2,1)S(1)}, u32[]{:S(2)}, u32[]{:S(2)}) collective-permute-start(bf16[128,1280]{1,0:T(8,128)(2,1)S(1)} %fusion), channel_id=1, source_target_pairs={{16,1},{17,0},{18,3},{19,2},{20,5},{21,4},{22,7},{23,6},{24,9},{25... | collective-permute-start | bytes 983048 | tf_op jit(solution)/shard_map/ppermute | solution.py:313
  88.4 11.0 %collective-permute-start.18 = (bf16[5120,128]{1,0:T(8,128)(2,1)S(1)}, bf16[5120,128]{1,0:T(8,128)(2,1)}, u32[]{:S(2)}, u32[]{:S(2)}) collective-permute-start(bf16[5120,128]{1,0:T(8,128)(2,1)S(1)} %bitcast.68), channel_id=1, source_target_pairs={{0,8},{8,0},{16,24},{24,16},{1,9},{9,1},{17,25},{25,17},{2,10},{10... | collective-permute-start | bytes 3932168 | tf_op jit(solution)/shard_map/ppermute | solution.py:300
  88.5 10.9 %collective-permute-start.19 = (bf16[5120,128]{1,0:T(8,128)(2,1)}, bf16[5120,128]{1,0:T(8,128)(2,1)}, u32[]{:S(2)}, u32[]{:S(2)}) collective-permute-start(bf16[5120,128]{1,0:T(8,128)(2,1)} %bitcast.17.v0), channel_id=1, source_target_pairs={{0,8},{8,0},{16,24},{24,16},{1,9},{9,1},{17,25},{25,17},{2,10},{10... | collective-permute-start | bytes 3932168 | tf_op jit(solution)/shard_map/ppermute | solution.py:300
  94.3 18.6 %all-to-all-start = ((bf16[4,128,1280]{2,1,0:T(8,128)(2,1)}), bf16[4,128,1280]{2,1,0:T(8,128)(2,1)S(1)}, u32[]{:S(2)}, u32[]{:S(2)}) async-start(bf16[4,128,1280]{2,1,0:T(8,128)(2,1)} %broadcast_in_dim.36), calls=%async_computation | async-start | bytes 2621440 | tf_op jit(solution)/shard_map/all_to_all | solution.py:316
  136.0 7.2 %collective-permute-start.20 = (bf16[128,1280]{1,0:T(8,128)(2,1)S(1)}, bf16[128,1280]{1,0:T(8,128)(2,1)S(1)}, u32[]{:S(2)}, u32[]{:S(2)}) collective-permute-start(bf16[128,1280]{1,0:T(8,128)(2,1)S(1)} %add_convert_fusion.6), channel_id=1, source_target_pairs={{0,1},{1,0},{2,3},{3,2},{4,5},{5,4},{6,7},{7,6},{8,9},{9,8},{10,11... | collective-permute-start | bytes 983048 | tf_op jit(solution)/shard_map/ppermute | solution.py:313
  144.3 15.8 %all-to-all-start.2 = ((bf16[4,128,1280]{2,1,0:T(8,128)(2,1)}), bf16[4,128,1280]{2,1,0:T(8,128)(2,1)S(1)}, u32[]{:S(2)}, u32[]{:S(2)}) async-start(bf16[4,128,1280]{2,1,0:T(8,128)(2,1)} %broadcast_in_dim.37), calls=%async_computation.2 | async-start | bytes 2621440 | tf_op jit(solution)/shard_map/all_to_all | solution.py:316
  181.8 10.6 %collective-permute-start.21 = (bf16[128,1280]{1,0:T(8,128)(2,1)S(1)}, bf16[128,1280]{1,0:T(8,128)(2,1)S(1)}, u32[]{:S(2)}, u32[]{:S(2)}) collective-permute-start(bf16[128,1280]{1,0:T(8,128)(2,1)S(1)} %add_convert_fusion.4), channel_id=1, source_target_pairs={{0,16},{1,17},{2,18},{3,19},{4,20},{5,21},{6,22},{7,23},{8,24},{9,... | collective-permute-start | bytes 983048 | tf_op jit(solution)/shard_map/ppermute | solution.py:313
  183.1 12.7 %collective-permute-start.22 = (bf16[128,1280]{1,0:T(8,128)(2,1)S(1)}, bf16[128,1280]{1,0:T(8,128)(2,1)S(1)}, u32[]{:S(2)}, u32[]{:S(2)}) collective-permute-start(bf16[128,1280]{1,0:T(8,128)(2,1)S(1)} %add_convert_fusion.4), channel_id=1, source_target_pairs={{0,17},{1,16},{2,19},{3,18},{4,21},{5,20},{6,23},{7,22},{8,25},{9,... | collective-permute-start | bytes 983048 | tf_op jit(solution)/shard_map/ppermute | solution.py:313
  232.2 7.2 %collective-permute-start.23 = (bf16[128,1280]{1,0:T(8,128)(2,1)S(1)}, bf16[128,1280]{1,0:T(8,128)(2,1)S(1)}, u32[]{:S(2)}, u32[]{:S(2)}) collective-permute-start(bf16[128,1280]{1,0:T(8,128)(2,1)S(1)} %add_convert_fusion.2), channel_id=1, source_target_pairs={{0,1},{1,0},{2,3},{3,2},{4,5},{5,4},{6,7},{7,6},{8,9},{9,8},{10,11... | collective-permute-start | bytes 983048 | tf_op jit(solution)/shard_map/ppermute | solution.py:313
  240.6 15.9 %all-to-all-start.6 = ((bf16[4,128,1280]{2,1,0:T(8,128)(2,1)}), bf16[4,128,1280]{2,1,0:T(8,128)(2,1)S(1)}, u32[]{:S(2)}, u32[]{:S(2)}) async-start(bf16[4,128,1280]{2,1,0:T(8,128)(2,1)} %broadcast_in_dim.39), calls=%async_computation.6 | async-start | bytes 2621440 | tf_op jit(solution)/shard_map/all_to_all | solution.py:316
  264.3 15.8 %all-to-all-start.7 = ((bf16[4,128,1280]{2,1,0:T(8,128)(2,1)}), bf16[4,128,1280]{2,1,0:T(8,128)(2,1)S(1)}, u32[]{:S(2)}, u32[]{:S(2)}) async-start(bf16[4,128,1280]{2,1,0:T(8,128)(2,1)} %decoder_layer.7), calls=%async_computation.7 | async-start | bytes 2621440 | tf_op jit(solution)/shard_map/all_to_all | solution.py:316
  281.9 5.6 %collective-permute-start.24 = (bf16[4,16,1280]{2,1,0:T(8,128)(2,1)S(1)}, bf16[4,16,1280]{2,1,0:T(8,128)(2,1)S(1)}, u32[]{:S(2)}, u32[]{:S(2)}) collective-permute-start(bf16[4,16,1280]{2,1,0:T(8,128)(2,1)S(1)} %get-tuple-element.45), channel_id=1, source_target_pairs={{16,0},{17,1},{18,2},{19,3},{20,4},{21,5},{22,6},{23,7},{24,8},{25... | collective-permute-start | bytes 491528 | tf_op jit(solution)/shard_map/ppermute | solution.py:313
  285.1 7.2 %collective-permute-start.26 = (bf16[4,16,1280]{2,1,0:T(8,128)(2,1)S(1)}, bf16[4,16,1280]{2,1,0:T(8,128)(2,1)S(1)}, u32[]{:S(2)}, u32[]{:S(2)}) collective-permute-start(bf16[4,16,1280]{2,1,0:T(8,128)(2,1)S(1)} %get-tuple-element.47), channel_id=1, source_target_pairs={{16,17},{17,16},{18,19},{19,18},{20,21},{21,20},{22,23},{23,22},{2... | collective-permute-start | bytes 491528 | tf_op jit(solution)/shard_map/ppermute | solution.py:313
  292.4 9.7 %collective-permute-start.27 = (bf16[16,1280]{1,0:T(8,128)(2,1)S(1)}, bf16[16,1280]{1,0:T(8,128)(2,1)S(1)}, u32[]{:S(2)}, u32[]{:S(2)}) collective-permute-start(bf16[16,1280]{1,0:T(8,128)(2,1)S(1)} %get-tuple-element.52), channel_id=1, source_target_pairs={{0,0},{1,1},{2,32},{3,33},{4,64},{5,65},{6,96},{7,97},{32,2},{33,3... | collective-permute-start | bytes 122888 | tf_op jit(solution)/shard_map/ppermute | solution.py:445
  295.4 7.7 %collective-permute-start.28 = (bf16[16,1280]{1,0:T(8,128)(2,1)S(1)}, bf16[16,1280]{1,0:T(8,128)(2,1)S(1)}, u32[]{:S(2)}, u32[]{:S(2)}) collective-permute-start(bf16[16,1280]{1,0:T(8,128)(2,1)S(1)} %get-tuple-element.55), channel_id=1, source_target_pairs={{0,32},{1,33},{2,64},{3,65},{4,96},{5,97},{6,0},{7,1},{32,34},{33,... | collective-permute-start | bytes 122888 | tf_op jit(solution)/shard_map/ppermute | solution.py:445
  300.1 6.1 %collective-permute-start.29 = (bf16[16,1280]{1,0:T(8,128)(2,1)S(1)}, bf16[16,1280]{1,0:T(8,128)(2,1)S(1)}, u32[]{:S(2)}, u32[]{:S(2)}) collective-permute-start(bf16[16,1280]{1,0:T(8,128)(2,1)S(1)} %get-tuple-element.54), channel_id=1, source_target_pairs={{0,64},{1,65},{2,96},{3,97},{4,0},{5,1},{6,32},{7,33},{32,66},{33,... | collective-permute-start | bytes 122888 | tf_op jit(solution)/shard_map/ppermute | solution.py:445
  (12 other events, 112.5 us)
